TPU v7x, 512 devices: a whole 4x8x8 slice. The times are simulated.
512 devices in a mesh: section: 32 (over x, z_lo, core), aux: 2 (over z_hi), dp: 8 (over y).
Axes of the slice: x: 4, y: 8, z: 8 (z_hi: 2, z_lo: 4; z = z_hi * 4 + z_lo), core: 2. Of those that a mesh axis runs over, the one named last changes fastest.
Arguments:
- aux_rows: bfloat16 [32, 8, 256, 2048], P(None, 'dp', 'section', 'aux'), may hold values from -30 to 30
- predictors: bfloat16 [2, 32, 32, 8, 8, 512], P('aux', None, 'section', 'dp'), may hold values from -0.125 to 0.125
- queries: bfloat16 [32, 2048, 4096], P('section', 'dp', 'aux'), may hold values from -600 to 600
- target: bfloat16 [32, 2048, 4096], P('section', 'dp', 'aux'), may hold values from -3 to 3
- lengths: int32 [8, 4], P('dp'), may hold values from 1 to 128, 256 in all within a row
Outputs:
- grad_rows: bfloat16 [32, 8, 256, 2048], P(None, 'dp', 'section', 'aux')
- grad_predictors: float32 [2, 32, 32, 8, 8, 512], P('aux', None, 'section', 'dp')
Inputs may be any that keep to these rules, and one draw needn't show every extreme that they name: Each row holds 4 prompt lengths summing to 256; the largest is exactly 128.
All inputs are finite; a program needn't handle non-finite values.
Results may differ from a plain program's by a relative error of at most 0.024.
The roundings to bfloat16 on the way count: a program that leaves them out, or rounds other values in their place, can miss the bound.
Values may be sent and summed in bfloat16 or wider, within the bound.
No kernel may reach another device: no remote copies, remote signals or barrier semaphores. Data moves between devices by JAX's collectives and lax.ppermute only.
A program may use at most 64 MiB of HBM per device.

v0:
```python
import math

import jax
import jax.numpy as jnp
from jax import lax
from jax.sharding import PartitionSpec as P

HEAD_DIM = 128


def doc_mask(lens, count):
    ends = jnp.cumsum(lens)
    pos = jnp.arange(count, dtype=jnp.int32)
    docs = jnp.sum((pos[:, None] >= ends[None, :]).astype(jnp.int32), axis=1)
    return (docs[:, None] == docs[None, :]) & (pos[None, :] <= pos[:, None])


def attend_grads(qrows, keys, values, goal, mask):
    tok, kvh, hdim = keys.shape
    group = qrows.shape[1] // (kvh * hdim)
    scale = 1.0 / math.sqrt(hdim)
    q_four = qrows.reshape(tok, kvh, group, hdim)
    scores = jnp.einsum("ihgd,jhd->hgij", q_four, keys, preferred_element_type=jnp.float32) * scale
    scores = jnp.where(mask[None, None], scores, -1e30)
    top = jnp.max(scores, axis=-1, keepdims=True)
    expo = jnp.exp(scores - top)
    probs = expo / jnp.sum(expo, axis=-1, keepdims=True)
    probs_b = probs.astype(jnp.bfloat16)
    attn_out = jnp.einsum(
        "hgij,jhd->ihgd", probs_b, values, preferred_element_type=jnp.float32
    ).reshape(tok, -1)
    dout = attn_out - goal.astype(jnp.float32)
    dout_b = dout.astype(jnp.bfloat16).reshape(tok, kvh, group, hdim)
    dprob = jnp.einsum("ihgd,jhd->hgij", dout_b, values, preferred_element_type=jnp.float32)
    delta = jnp.sum((dout * attn_out).reshape(tok, kvh, group, hdim), axis=-1)
    delta = jnp.transpose(delta, (1, 2, 0))[..., None]
    dscore = (probs * (dprob - delta) * scale).astype(jnp.bfloat16)
    dkeys = jnp.einsum("hgij,ihgd->jhd", dscore, q_four, preferred_element_type=jnp.float32)
    dvalues = jnp.einsum("hgij,ihgd->jhd", probs_b, dout_b, preferred_element_type=jnp.float32)
    return (dkeys.astype(jnp.bfloat16), dvalues.astype(jnp.bfloat16))


def per_device(aux_rows, predictors, queries, target, lengths):
    own = lax.all_to_all(aux_rows, "section", split_axis=0, concat_axis=2, tiled=True)
    tok = own.shape[2]
    half_width = own.shape[3]
    full_rows = lax.all_gather(own.reshape(tok, half_width), "aux", axis=1, tiled=True)
    wide = lax.all_gather(predictors, "dp", axis=3, tiled=True)
    mine = lax.all_to_all(wide, "section", split_axis=1, concat_axis=2, tiled=True)
    blocks = mine.shape
    width = blocks[5]
    weight = mine.reshape(-1, width)
    predicted = jnp.dot(full_rows, weight, preferred_element_type=jnp.float32).astype(jnp.bfloat16)
    split = predicted.reshape(1, tok, 2, width // 2)
    cache = lax.all_to_all(split, "aux", split_axis=2, concat_axis=0, tiled=True)
    heads_here = width // 2 // HEAD_DIM
    keys = cache[0].reshape(tok, heads_here, HEAD_DIM)
    values = cache[1].reshape(tok, heads_here, HEAD_DIM)
    mask = doc_mask(lengths[0], tok)
    dkeys, dvalues = attend_grads(queries[0], keys, values, target[0], mask)
    back = jnp.stack([dkeys.reshape(tok, 1, width // 2), dvalues.reshape(tok, 1, width // 2)])
    owned_grads = lax.all_to_all(back, "aux", split_axis=0, concat_axis=2, tiled=True)
    dpredicted = owned_grads.reshape(tok, width)
    weight_grad = lax.dot_general(
        full_rows, dpredicted, (((0,), (0,)), ((), ())), preferred_element_type=jnp.float32
    ).astype(jnp.bfloat16)
    row_term = lax.dot_general(
        dpredicted, weight, (((1,), (1,)), ((), ())), preferred_element_type=jnp.float32
    )
    row_sum = lax.psum_scatter(
        row_term.astype(jnp.bfloat16), "aux", scatter_dimension=1, tiled=True
    )
    row_out = row_sum.reshape(1, 1, tok, half_width)
    grad_rows = lax.all_to_all(row_out, "section", split_axis=2, concat_axis=0, tiled=True)
    term = weight_grad.reshape(blocks)
    owners = lax.all_to_all(term, "section", split_axis=2, concat_axis=1, tiled=True)
    grad_predictors = lax.psum_scatter(
        owners.astype(jnp.float32).astype(jnp.bfloat16), "dp", scatter_dimension=3, tiled=True
    ).astype(jnp.float32)
    return (grad_rows, grad_predictors)


def solution(mesh):
    return jax.shard_map(
        per_device,
        mesh=mesh,
        in_specs=(
            P(None, "dp", "section", "aux"),
            P("aux", None, "section", "dp", None, None),
            P("section", "dp", "aux"),
            P("section", "dp", "aux"),
            P("dp", None),
        ),
        out_specs=(P(None, "dp", "section", "aux"), P("aux", None, "section", "dp", None, None)),
        check_vma=False,
    )
```

profile of v0, /device:TPU:1, one launch (start us, length us, event | category | flops | bytes accessed | tf_op | source)
XLA Modules:
  0.0 358.1 jit_solution(4326151872085627347)
XLA Ops:
  8.0 0.0 all-gather.5.cloned.1.call-start
  8.0 0.7 all-gather.5.cloned.1.call-update
  8.7 28.3 %all_to_all.72 = bf16[32,1,8,1024]{3,2,1,0:T(8,128)(2,1)} all-to-all(bf16[32,1,8,1024]{3,2,1,0:T(8,128)(2,1)} %param.5), channel_id=1, replica_groups=mesh['section'=32,'aux'=2,'dp'=8] {'section'}, dimensions={0} | all-to-all | bytes 1048576 | tf_op jit(solution)/shard_map/all_to_all | solution.py:44
  37.0 0.0 copy-start.2
  37.0 19.3 %all-gather.5.cloned.1.call-done = bf16[1,32,1,8,8,512]{5,4,3,2,0,1:T(8,128)(2,1)} async-done(((bf16[1,32,1,1,8,512]{5,4,3,2,0,1:T(8,128)(2,1)}), bf16[1,32,1,8,8,512]{5,4,3,2,0,1:T(8,128)(2,1)}) %all-gather.5.cloned.1.call-update) | async-done | bytes 2097168 | tf_op jit(solution)/shard_map/all_gather | solution.py:48
  56.4 12.0 %all-to-all-start.1 = ((bf16[1,32,1,8,8,512]{5,4,3,2,0,1:T(8,128)(2,1)}), bf16[1,32,1,8,8,512]{5,4,3,2,0,1:T(8,128)(2,1)S(1)}, u32[]{:S(2)}, u32[]{:S(2)}) async-start(bf16[1,32,1,8,8,512]{5,4,3,2,0,1:T(8,128)(2,1)} %all-gather.5.cloned.1.call-done), calls=%async_computation.1 | async-start | bytes 4194304 | tf_op jit(solution)/shard_map/all_to_all | solution.py:49
  68.4 0.0 all-gather.3.cloned.1.call-start
  68.4 0.5 all-gather.3.cloned.1.call-update
  68.9 0.0 copy-done.2
  68.9 0.2 reduce-window.8
  69.1 54.6 %all-gather.3.cloned.1.call-done = bf16[256,2048]{1,0:T(8,128)(2,1)} async-done(((bf16[256,1024]{1,0:T(8,128)(2,1)}), bf16[256,2048]{1,0:T(8,128)(2,1)}) %all-gather.3.cloned.1.call-update) | async-done | bytes 1048592 | tf_op jit(solution)/shard_map/all_gather | solution.py:47
  123.8 16.8 %all-to-all-done.1 = bf16[1,32,1,8,8,512]{5,4,3,2,0,1:T(8,128)(2,1)S(1)} async-done(((bf16[1,32,1,8,8,512]{5,4,3,2,0,1:T(8,128)(2,1)}), bf16[1,32,1,8,8,512]{5,4,3,2,0,1:T(8,128)(2,1)S(1)}, u32[]{:S(2)}, u32[]{:S(2)}) %all-to-all-start.1) | async-done | bytes 2097184 | tf_op jit(solution)/shard_map/all_to_all | solution.py:49
  140.6 1.9 convolution_convert_fusion.2
  142.5 0.0 copy-start.1
  142.5 0.8 copy.84
  143.4 4.6 %all-to-all-start.2 = ((bf16[1,256,2,256]{1,3,0,2:T(8,128)(2,1)}), bf16[1,256,2,256]{1,3,0,2:T(8,128)(2,1)S(1)}, u32[]{:S(2)}, u32[]{:S(2)}) async-start(bf16[1,256,2,256]{1,3,0,2:T(8,128)(2,1)} %bitcast.133), calls=%async_computation.2 | async-start | bytes 524288 | tf_op jit(solution)/shard_map/all_to_all | solution.py:55
  148.0 0.1 convert_reduce_fusion
  148.1 2.3 copy.92
  150.4 0.0 copy-done.1
  150.4 1.6 copy.64
  152.0 0.1 fusion.18
  152.1 3.8 %all-to-all-done.2 = bf16[1,256,2,256]{1,3,0,2:T(8,128)(2,1)S(1)} async-done(((bf16[1,256,2,256]{1,3,0,2:T(8,128)(2,1)}), bf16[1,256,2,256]{1,3,0,2:T(8,128)(2,1)S(1)}, u32[]{:S(2)}, u32[]{:S(2)}) %all-to-all-start.2) | async-done | bytes 262176 | tf_op jit(solution)/shard_map/all_to_all | solution.py:55
  155.9 4.7 %fusion.23 = (f32[2,8,256]{2,1,0:T(8,128)S(1)}, f32[2,8,256,256]{2,3,1,0:T(8,128)}) fusion(pred[256,256]{0,1:T(8,128)(4,1)S(1)} %fusion.18, bf16[256,2,128,1]{0,2,3,1:T(8,128)(2,1)S(1)} %bitcast.141, bf16[256,2,8,128]{0,3,2,1:T(8,128)(2,1)} %bitcast.130), kind=kOutput, calls=%fused_computation.38 | convolution fusion | flops 272630016 | bytes 5455872 | tf_op jit(solution)/shard_map/sub | solution.py:26
  160.7 0.0 copy-start
  160.7 2.8 fusion.11
  163.4 0.1 copy-done
  163.5 1.1 fusion.6
  164.6 0.8 fusion.14
  165.4 4.0 %fusion.15 = bf16[2,256,128]{1,2,0:T(8,128)(2,1)S(1)} fusion(bf16[256,2,8,128]{0,3,2,1:T(8,128)(2,1)} %bitcast.131, bf16[256,2,128,1]{0,2,3,1:T(8,128)(2,1)S(1)} %bitcast.138, bf16[256,2,8,128]{0,3,2,1:T(8,128)(2,1)S(1)} %get-tuple-element.13, f32[2,8,256]{2,1,0:T(8,128)} %bitcast.142, f32[2,8,256,256]{2,3,1,0:T(8,128)} %get-tuple-element.17, ...), kind=kOutput, calls=%fused_computation.25 | convolution fusion | flops 542179328 | bytes 6586368 | tf_op jit(solution)/shard_map/hgij,ihgd->jhd/dot_general | solution.py:38
  169.5 10.7 %all_to_all.73 = bf16[2,256,1,256]{1,3,2,0:T(8,128)(2,1)S(1)} all-to-all(bf16[2,256,1,256]{1,3,2,0:T(8,128)(2,1)S(1)} %pad_maximum_fusion), channel_id=1, replica_groups=mesh['section'=32,'aux'=2,'dp'=8] {'aux'}, dimensions={0} | all-to-all | bytes 524288 | tf_op jit(solution)/shard_map/all_to_all | solution.py:62
  180.2 3.3 fusion.5
  183.4 3.9 %copy.71 = bf16[2048,512]{1,0:T(8,128)(2,1)} copy(bf16[2048,512]{0,1:T(8,128)(2,1)} %fusion.5) | data formatting | bytes 4194304 | tf_op jit(solution)/shard_map/convert_element_type | solution.py:66
  187.4 11.5 %all-to-all-start.5 = ((bf16[1,1,32,8,8,512]{5,4,3,1,0,2:T(8,128)(2,1)}), bf16[1,1,32,8,8,512]{5,4,3,1,0,2:T(8,128)(2,1)}, u32[]{:S(2)}, u32[]{:S(2)}) async-start(bf16[1,1,32,8,8,512]{5,4,3,1,0,2:T(8,128)(2,1)} %bitcast.123), calls=%async_computation.6 | async-start | bytes 4194304 | tf_op jit(solution)/shard_map/all_to_all | solution.py:76
  198.8 0.0 reduce-scatter.3.cloned.1.call-start
  198.9 1.7 convolution_convert_fusion.1
  200.6 0.0 reduce-scatter.3.cloned.1.call-update
  200.6 0.2 all-reduce.3.cloned.1.call-start
  200.9 70.2 %all-to-all-done.5 = bf16[1,1,32,8,8,512]{5,4,3,1,0,2:T(8,128)(2,1)} async-done(((bf16[1,1,32,8,8,512]{5,4,3,1,0,2:T(8,128)(2,1)}), bf16[1,1,32,8,8,512]{5,4,3,1,0,2:T(8,128)(2,1)}, u32[]{:S(2)}, u32[]{:S(2)}) %all-to-all-start.5) | async-done | bytes 2097184 | tf_op jit(solution)/shard_map/all_to_all | solution.py:76
  271.1 0.0 all-reduce.3.cloned.1.call-update
  271.1 0.0 reduce-scatter.3.cloned.1.call-done
  271.2 1.9 copy.96
  273.0 0.5 broadcast.50
  273.5 3.7 %reduce = bf16[256,1024]{1,0:T(8,128)(2,1)S(1)} reduce(bf16[256,1,1,1024]{3,2,1,0:T(2,128)(2,1)S(1)} %bitcast.126, bf16[]{:T(256)} %broadcast.50), dimensions={1,2}, to_apply=%bitcast.120.reduce_sub_computation | reduce | bytes 1048578
  277.2 1.1 reshape.132
  278.4 4.5 %all-to-all-start.4 = ((bf16[32,2,4096]{2,1,0:T(2,128)(2,1)}), bf16[32,2,4096]{2,1,0:T(2,128)(2,1)S(1)}, u32[]{:S(2)}, u32[]{:S(2)}) async-start(bf16[32,2,4096]{2,1,0:T(2,128)(2,1)} %reshape.132), calls=%async_computation.5 | async-start | bytes 1048576 | tf_op jit(solution)/shard_map/all_to_all | solution.py:74
  282.9 1.3 dynamic-slice
  284.1 15.6 %all-to-all-done.4 = bf16[32,2,4096]{2,1,0:T(2,128)(2,1)S(1)} async-done(((bf16[32,2,4096]{2,1,0:T(2,128)(2,1)}), bf16[32,2,4096]{2,1,0:T(2,128)(2,1)S(1)}, u32[]{:S(2)}, u32[]{:S(2)}) %all-to-all-start.4) | async-done | bytes 524320 | tf_op jit(solution)/shard_map/all_to_all | solution.py:74
  299.7 0.5 reshape.133
  300.3 1.0 copy.95
  301.2 47.1 %all-reduce.3.cloned.1.call-done = bf16[1,32,1,8,8,512]{5,4,3,1,2,0:T(8,128)(2,1)} async-done(((bf16[1,32,1,8,8,512]{5,4,3,1,2,0:T(8,128)(2,1)}), bf16[1,32,1,8,8,512]{5,4,3,1,2,0:T(8,128)(2,1)}) %all-reduce.3.cloned.1.call-update) | async-done | bytes 2097168
  348.3 2.4 bitcast_convert_fusion
  (2 shorter events, 0.0 us)
Async XLA Ops:
  8.0 48.4 %all-gather.5.cloned.1.call-start = ((), (), s32[]{:S(2)}) async-start(), calls=%async_computation.8 | async-start | bytes 2359296 | tf_op jit(solution)/shard_map/all_gather | solution.py:48
  37.0 31.9 %copy-start.2 = (s32[1,4]{1,0:T(1,128)S(1)}, s32[1,4]{1,0:T(1,128)}, u32[]{:S(2)}) copy-start(s32[1,4]{1,0:T(1,128)} %param.9) | copy-start | bytes 52
  56.4 84.2 %all-to-all-start.1 = ((bf16[1,32,1,8,8,512]{5,4,3,2,0,1:T(8,128)(2,1)}), bf16[1,32,1,8,8,512]{5,4,3,2,0,1:T(8,128)(2,1)S(1)}, u32[]{:S(2)}, u32[]{:S(2)}) async-start(bf16[1,32,1,8,8,512]{5,4,3,2,0,1:T(8,128)(2,1)} %all-gather.5.cloned.1.call-done), calls=%async_computation.1 | async-start | bytes 4194304 | tf_op jit(solution)/shard_map/all_to_all | solution.py:49
  68.4 55.4 %all-gather.3.cloned.1.call-start = ((), (), s32[]{:S(2)}) async-start(), calls=%async_computation.7 | async-start | bytes 1572864 | tf_op jit(solution)/shard_map/all_gather | solution.py:47
  142.5 7.9 %copy-start.1 = (bf16[1,256,2048]{2,1,0:T(8,128)(2,1)S(1)}, bf16[1,256,2048]{2,1,0:T(8,128)(2,1)}, u32[]{:S(2)}) copy-start(bf16[1,256,2048]{2,1,0:T(8,128)(2,1)} %param.8) | copy-start | bytes 3145732
  143.4 12.6 %all-to-all-start.2 = ((bf16[1,256,2,256]{1,3,0,2:T(8,128)(2,1)}), bf16[1,256,2,256]{1,3,0,2:T(8,128)(2,1)S(1)}, u32[]{:S(2)}, u32[]{:S(2)}) async-start(bf16[1,256,2,256]{1,3,0,2:T(8,128)(2,1)} %bitcast.133), calls=%async_computation.2 | async-start | bytes 524288 | tf_op jit(solution)/shard_map/all_to_all | solution.py:55
  160.7 2.9 copy-start
  187.4 83.7 %all-to-all-start.5 = ((bf16[1,1,32,8,8,512]{5,4,3,1,0,2:T(8,128)(2,1)}), bf16[1,1,32,8,8,512]{5,4,3,1,0,2:T(8,128)(2,1)}, u32[]{:S(2)}, u32[]{:S(2)}) async-start(bf16[1,1,32,8,8,512]{5,4,3,1,0,2:T(8,128)(2,1)} %bitcast.123), calls=%async_computation.6 | async-start | bytes 4194304 | tf_op jit(solution)/shard_map/all_to_all | solution.py:76
  198.8 72.3 %reduce-scatter.3.cloned.1.call-start = ((), (), s32[]{:S(2)}) async-start(), calls=%async_computation.9 | async-start | bytes 1572864 | tf_op jit(solution)/shard_map/reduce_scatter | solution.py:70
  200.6 147.7 %all-reduce.3.cloned.1.call-start = ((), (), s32[]{:S(2)}) async-start(), calls=%async_computation.10 | async-start | bytes 4194304
  278.4 21.4 %all-to-all-start.4 = ((bf16[32,2,4096]{2,1,0:T(2,128)(2,1)}), bf16[32,2,4096]{2,1,0:T(2,128)(2,1)S(1)}, u32[]{:S(2)}, u32[]{:S(2)}) async-start(bf16[32,2,4096]{2,1,0:T(2,128)(2,1)} %reshape.132), calls=%async_computation.5 | async-start | bytes 1048576 | tf_op jit(solution)/shard_map/all_to_all | solution.py:74
Sparse Core Ops, SparseCore 0:
  10.9 45.4 all-gather.4
  271.2 77.0 all-reduce.2
Sparse Core Ops, SparseCore 1:
  70.9 52.8 all-gather.2
  202.1 51.5 reduce-scatter.2
where the time goes:
time: 361 us; the launch traced here: 358 us
  waiting for transfers between devices  229 us (63%)
  blocking collectives  39 us (11%)
  starting transfers between devices  32.9 us (9%)
  matrix products  17.5 us (5%)
  between operations  15.6 us (4%)
  local copies, waits for them, and re-layouts  15 us (4%)
  other arithmetic  9.21 us (3%)
    all_to_all x1, waiting for transfers between devices, per_device(): lax.all_to_all(term, 'section', split_axis=2, concat_axis=1, tiled=True)  70.2 us
    all_gather x1, waiting for transfers between devices, per_device(): lax.all_gather(own.reshape(tok, half_width), 'aux', axis=1, tiled=True)  54.6 us
    unnamed x5, waiting for transfers between devices  48.3 us
    all_to_all x1, blocking collectives, per_device(): lax.all_to_all(aux_rows, 'section', split_axis=0, concat_axis=2, tiled=True)  28.3 us
    all_gather x1, waiting for transfers between devices, per_device(): wide = lax.all_gather(predictors, 'dp', axis=3, tiled=True)  19.3 us
    all_to_all x1, waiting for transfers between devices, per_device(): lax.all_to_all(wide, 'section', split_axis=1, concat_axis=2, tiled=True)  16.8 us
    all_to_all x1, waiting for transfers between devices, per_device(): lax.all_to_all(row_out, 'section', split_axis=2, concat_axis=0, tiled=True)  15.6 us
    all_to_all x1, starting transfers between devices, per_device(): lax.all_to_all(wide, 'section', split_axis=1, concat_axis=2, tiled=True)  12 us
  transfers between devices with their start and end apart: 8, of which 7 were waited for; matrix products, arithmetic and copies ran while one was open for 4% of the time, Pallas kernels for 0%

commit v1 on v0

--- a/solution.py
+++ b/solution.py
@@ -41,42 +41,57 @@
 
 
 def per_device(aux_rows, predictors, queries, target, lengths):
-    own = lax.all_to_all(aux_rows, "section", split_axis=0, concat_axis=2, tiled=True)
-    tok = own.shape[2]
-    half_width = own.shape[3]
-    full_rows = lax.all_gather(own.reshape(tok, half_width), "aux", axis=1, tiled=True)
-    wide = lax.all_gather(predictors, "dp", axis=3, tiled=True)
-    mine = lax.all_to_all(wide, "section", split_axis=1, concat_axis=2, tiled=True)
-    blocks = mine.shape
-    width = blocks[5]
-    weight = mine.reshape(-1, width)
-    predicted = jnp.dot(full_rows, weight, preferred_element_type=jnp.float32).astype(jnp.bfloat16)
-    split = predicted.reshape(1, tok, 2, width // 2)
-    cache = lax.all_to_all(split, "aux", split_axis=2, concat_axis=0, tiled=True)
-    heads_here = width // 2 // HEAD_DIM
-    keys = cache[0].reshape(tok, heads_here, HEAD_DIM)
-    values = cache[1].reshape(tok, heads_here, HEAD_DIM)
+    sections = lax.axis_size("section")
+    auxes = lax.axis_size("aux")
+    shards = lax.axis_size("dp")
+    both = ("section", "aux")
+    peers = sections * auxes
+    blk, width = predictors.shape[4:]
+    part = width // auxes
+    rows_each, feats = aux_rows.shape[2:]
+    tok = sections * rows_each
+
+    w_out = predictors.reshape(sections, blk, auxes, part).swapaxes(1, 2).reshape(peers, blk, part)
+    w_in = lax.all_to_all(w_out, both, split_axis=0, concat_axis=0, tiled=True)
+    w_all = lax.all_gather(w_in, "dp", axis=0)
+    weight = jnp.transpose(
+        w_all.reshape(shards, sections, auxes, blk, part), (1, 0, 3, 2, 4)
+    ).reshape(sections * shards * blk, auxes * part)
+
+    r_out = jnp.broadcast_to(
+        aux_rows.reshape(sections, 1, rows_each, feats), (sections, auxes, rows_each, feats)
+    ).reshape(peers, rows_each, feats)
+    r_in = lax.all_to_all(r_out, both, split_axis=0, concat_axis=0, tiled=True)
+    rows = jnp.swapaxes(r_in.reshape(sections, auxes, rows_each, feats), 1, 2).reshape(tok, -1)
+
+    cache = jnp.dot(rows, weight, preferred_element_type=jnp.float32).astype(jnp.bfloat16)
+    keys = cache[:, :part].reshape(tok, part // HEAD_DIM, HEAD_DIM)
+    values = cache[:, part:].reshape(tok, part // HEAD_DIM, HEAD_DIM)
     mask = doc_mask(lengths[0], tok)
     dkeys, dvalues = attend_grads(queries[0], keys, values, target[0], mask)
-    back = jnp.stack([dkeys.reshape(tok, 1, width // 2), dvalues.reshape(tok, 1, width // 2)])
-    owned_grads = lax.all_to_all(back, "aux", split_axis=0, concat_axis=2, tiled=True)
-    dpredicted = owned_grads.reshape(tok, width)
-    weight_grad = lax.dot_general(
-        full_rows, dpredicted, (((0,), (0,)), ((), ())), preferred_element_type=jnp.float32
+    dcache = jnp.concatenate([dkeys.reshape(tok, part), dvalues.reshape(tok, part)], axis=1)
+
+    w_grad = lax.dot_general(
+        rows, dcache, (((0,), (0,)), ((), ())), preferred_element_type=jnp.float32
     ).astype(jnp.bfloat16)
-    row_term = lax.dot_general(
-        dpredicted, weight, (((1,), (1,)), ((), ())), preferred_element_type=jnp.float32
-    )
-    row_sum = lax.psum_scatter(
-        row_term.astype(jnp.bfloat16), "aux", scatter_dimension=1, tiled=True
-    )
-    row_out = row_sum.reshape(1, 1, tok, half_width)
-    grad_rows = lax.all_to_all(row_out, "section", split_axis=2, concat_axis=0, tiled=True)
-    term = weight_grad.reshape(blocks)
-    owners = lax.all_to_all(term, "section", split_axis=2, concat_axis=1, tiled=True)
-    grad_predictors = lax.psum_scatter(
-        owners.astype(jnp.float32).astype(jnp.bfloat16), "dp", scatter_dimension=3, tiled=True
+    w_grad = jnp.transpose(
+        w_grad.reshape(sections, shards, blk, auxes, part), (1, 0, 3, 2, 4)
+    ).reshape(shards, peers, blk, part)
+    w_sum = lax.psum_scatter(w_grad, "dp", scatter_dimension=0, tiled=True)
+    w_back = lax.all_to_all(w_sum.reshape(peers, blk, part), both, split_axis=0, concat_axis=0, tiled=True)
+    grad_predictors = (
+        w_back.reshape(sections, auxes, blk, part).swapaxes(1, 2).reshape(predictors.shape)
     ).astype(jnp.float32)
+
+    r_term = lax.dot_general(
+        dcache, weight, (((1,), (1,)), ((), ())), preferred_element_type=jnp.float32
+    ).astype(jnp.bfloat16)
+    r_send = jnp.swapaxes(
+        r_term.reshape(sections, rows_each, auxes, feats), 1, 2
+    ).reshape(peers, rows_each, feats)
+    r_back = lax.all_to_all(r_send, both, split_axis=0, concat_axis=0, tiled=True)
+    r_sum = jnp.sum(r_back.reshape(sections, auxes, rows_each, feats).astype(jnp.float32), axis=1)
+    grad_rows = r_sum.astype(jnp.bfloat16).reshape(aux_rows.shape)
     return (grad_rows, grad_predictors)
 
 

time: 361 us -> 183 us (0.51)
  waiting for transfers between devices: 229 us -> 35.9 us
  blocking collectives: 39 us -> 71.6 us
  starting transfers between devices: 32.9 us -> 19.8 us
  local copies, waits for them, and re-layouts: 15 us -> 21.2 us
    all_to_all x4 -> x2, waiting for transfers between devices: 106 us -> 12.4 us  [the longest x1 12.4 us: per_device(): lax.all_to_all(w_sum.reshape(peers, blk, part), both, split_axis=0, conca...]
    all_gather x2 -> x1, waiting for transfers between devices: 74 us -> 23.5 us  [per_device(): w_all = lax.all_gather(w_in, 'dp', axis=0)]
    unnamed x5 -> x2, waiting for transfers between devices: 48.3 us -> 0.03 us
    all_to_all x2, blocking collectives: 39 us -> 71.6 us  [the longest x1 43.3 us: per_device(): lax.all_to_all(r_send, both, split_axis=0, concat_axis=0, tiled=True)]
    all_to_all x4 -> x2, starting transfers between devices: 32.6 us -> 19.8 us  [the longest x1 14.3 us: per_device(): lax.all_to_all(w_sum.reshape(peers, blk, part), both, split_axis=0, conca...]
    transpose x0 -> x2, local copies, waits for them, and re-layouts: none -> 7.16 us  [the longest x1 3.77 us: per_device(): jnp.transpose(w_all.reshape(shards, sections, auxes, blk, part), (1, 0, 3...]
    unnamed x2 -> x0, other arithmetic: 6.06 us -> none
    unnamed x11, local copies, waits for them, and re-layouts: 4.49 us -> 0.79 us
  transfers between devices with their start and end apart: 8 -> 4, of which waited for: 7 -> 2; matrix products, arithmetic and copies ran while one was open for 4% -> 7% of each run, Pallas kernels for 0% -> 0%
where the time goes in v1:
time: 183 us
  blocking collectives  71.6 us (39%)
  waiting for transfers between devices  35.9 us (20%)
  local copies, waits for them, and re-layouts  21.2 us (12%)
  starting transfers between devices  19.8 us (11%)
  matrix products  14.3 us (8%)
  between operations  14.1 us (8%)
  other arithmetic  5.67 us (3%)
    all_to_all x1, blocking collectives, per_device(): lax.all_to_all(r_send, both, split_axis=0, concat_axis=0, tiled=True)  43.3 us
    all_to_all x1, blocking collectives, per_device(): w_in = lax.all_to_all(w_out, both, split_axis=0, concat_axis=0, tiled=True)  28.4 us
    all_gather x1, waiting for transfers between devices, per_device(): w_all = lax.all_gather(w_in, 'dp', axis=0)  23.5 us
    all_to_all x1, starting transfers between devices, per_device(): lax.all_to_all(w_sum.reshape(peers, blk, part), both, split_axis=0, conca...  14.3 us
    all_to_all x1, waiting for transfers between devices, per_device(): lax.all_to_all(w_sum.reshape(peers, blk, part), both, split_axis=0, conca...  12.4 us
    all_to_all x1, starting transfers between devices, per_device(): r_in = lax.all_to_all(r_out, both, split_axis=0, concat_axis=0, tiled=True)  5.48 us
    sub x1, matrix products, attend_grads(): expo = jnp.exp(scores - top)  4.63 us
    dot_general x1, matrix products, attend_grads(): jnp.einsum('hgij,ihgd->jhd', dscore, q_four, preferred_element_type=jnp.f...  4.24 us
  transfers between devices with their start and end apart: 4, of which 2 were waited for; matrix products, arithmetic and copies ran while one was open for 7% of the time, Pallas kernels for 0%

profile of v1, /device:TPU:1, one launch (start us, length us, event | category | flops | bytes accessed | tf_op | source)
XLA Modules:
  0.0 182.6 jit_solution(15393364490433274464)
XLA Ops:
  7.2 0.0 all-gather.3.cloned.1.call-start
  7.2 28.4 %all_to_all.20 = bf16[64,8,256]{2,1,0:T(8,128)(2,1)} all-to-all(bf16[64,8,256]{2,1,0:T(8,128)(2,1)} %bitcast.127), channel_id=1, replica_groups=mesh['section'=32,'aux'=2,'dp'=8] {'section','aux'}, dimensions={0} | all-to-all | bytes 524288 | tf_op jit(solution)/shard_map/all_to_all | solution.py:55
  35.6 0.0 copy-start.3
  35.6 0.0 all-gather.3.cloned.1.call-update
  35.6 2.2 %broadcast_in_dim.18 = bf16[32,2,8,1024]{3,2,1,0:T(8,128)(2,1)} broadcast(bf16[32,8,1024]{2,1,0:T(8,128)(2,1)} %bitcast.120), dimensions={0,2,3} | broadcast | bytes 1572864 | tf_op jit(solution)/shard_map/broadcast_in_dim | solution.py:61
  37.8 0.0 copy-start.2
  37.8 5.5 %all-to-all-start = ((bf16[64,8,1024]{2,1,0:T(8,128)(2,1)}), bf16[64,8,1024]{2,1,0:T(8,128)(2,1)S(1)}, u32[]{:S(2)}, u32[]{:S(2)}) async-start(bf16[64,8,1024]{2,1,0:T(8,128)(2,1)} %bitcast.3), calls=%async_computation | async-start | bytes 2097152 | tf_op jit(solution)/shard_map/all_to_all | solution.py:64
  43.3 0.0 reduce-scatter.2.cloned.1.call-start
  43.4 0.0 copy-done.3
  43.4 1.3 copy.79
  44.7 0.0 copy-done.2
  44.7 0.0 copy-start.4
  44.7 1.6 copy.56
  46.4 0.0 copy-done.4
  46.4 0.2 reduce-window.8
  46.5 0.1 convert_reduce_fusion
  46.6 0.7 fusion.18
  47.4 23.5 %all-gather.3.cloned.1.call-done = bf16[512,8,256]{2,1,0:T(8,128)(2,1)} async-done(((bf16[64,8,256]{2,1,0:T(8,128)(2,1)}), bf16[512,8,256]{2,1,0:T(8,128)(2,1)}) %all-gather.3.cloned.1.call-update) | async-done | bytes 2097168 | tf_op jit(solution)/shard_map/all_gather | solution.py:56
  70.9 3.8 %copy.51 = bf16[32,8,8,2,256]{4,3,2,1,0:T(2,128)(2,1)S(1)} copy(bf16[32,8,8,2,256]{4,2,3,0,1:T(8,128)(2,1)} %bitcast.114) | data formatting | bytes 4194304 | tf_op jit(solution)/shard_map/transpose | solution.py:57
  74.6 0.5 copy.80
  75.2 0.0 all-to-all-done
  75.2 0.7 convolution_convert_fusion.2
  76.0 4.6 %fusion.36 = (f32[2,8,256]{2,1,0:T(8,128)S(1)}, f32[2,8,256,256]{2,3,1,0:T(8,128)}) fusion(pred[256,256]{0,1:T(8,128)(4,1)} %fusion.18, bf16[256,2,8,128]{0,3,2,1:T(8,128)(2,1)} %bitcast.118, bf16[256,2,128,1]{2,1,0,3:T(2,128)(2,1)S(1)} %bitcast.129), kind=kOutput, calls=%fused_computation.45 | convolution fusion | flops 272630016 | bytes 5455872 | tf_op jit(solution)/shard_map/sub | solution.py:26
  80.6 0.0 copy-start
  80.6 2.8 %fusion.11 = bf16[2,8,256,256]{2,3,1,0:T(8,128)(2,1)S(1)} fusion(f32[2,8,256,256]{2,3,1,0:T(8,128)} %get-tuple-element.7, f32[2,8,256]{2,1,0:T(8,128)S(1)} %get-tuple-element.6), kind=kLoop, calls=%fused_computation.19 | loop fusion | flops 2097152 | bytes 6307840 | tf_op jit(solution)/shard_map/convert_element_type | solution.py:28
  83.4 0.1 copy-done
  83.5 1.1 fusion.6
  84.6 0.0 copy-start.1
  84.6 0.8 fusion.14
  85.4 0.2 copy-done.1
  85.6 4.2 %fusion.15 = bf16[2,256,128]{1,2,0:T(8,128)(2,1)S(1)} fusion(bf16[256,2,8,128]{0,3,2,1:T(8,128)(2,1)} %bitcast.119, bf16[256,2,8,128]{0,3,2,1:T(8,128)(2,1)} %copy-done.1, f32[2,8,256]{2,1,0:T(8,128)} %bitcast.130, f32[2,8,256,256]{2,3,1,0:T(8,128)} %get-tuple-element.7, f32[2,8,256]{2,1,0:T(8,128)S(1)} %get-tuple-element.6, ...), kind=kOutput, calls=%fused_computation.25 | convolution fusion | flops 542179328 | bytes 6586368 | tf_op jit(solution)/shard_map/hgij,ihgd->jhd/dot_general | solution.py:38
  89.8 2.0 %fusion.5 = bf16[2048,512]{0,1:T(8,128)(2,1)} fusion(bf16[256,2048]{1,0:T(8,128)(2,1)S(1)} %bitcast.112, bf16[256,256]{0,1:T(8,128)(2,1)S(1)} %bitcast.115, bf16[256,256]{0,1:T(8,128)(2,1)S(1)} %bitcast.123), kind=kOutput, calls=%fused_computation.9 | convolution fusion | flops 538443776 | bytes 3407872 | tf_op jit(solution)/shard_map/dot_general | solution.py:74
  91.8 3.9 %copy.62 = bf16[2048,512]{1,0:T(8,128)(2,1)} copy(bf16[2048,512]{0,1:T(8,128)(2,1)} %fusion.5) | data formatting | bytes 4194304 | tf_op jit(solution)/shard_map/convert_element_type | solution.py:76
  95.8 4.0 %reshape.167 = bf16[32,8,8,2,256]{4,3,2,1,0:T(2,128)(2,1)} reshape(bf16[2048,512]{1,0:T(8,128)(2,1)} %copy.62) | data formatting | bytes 4194304 | tf_op jit(solution)/shard_map/reshape | solution.py:78
  99.7 3.4 %copy.63 = bf16[8,32,2,8,256]{4,3,2,1,0:T(8,128)(2,1)} copy(bf16[8,32,2,8,256]{4,2,3,0,1:T(2,128)(2,1)} %bitcast.109) | data formatting | bytes 4194304 | tf_op jit(solution)/shard_map/transpose | solution.py:77
  103.1 0.0 reduce-scatter.2.cloned.1.call-update
  103.2 0.8 convolution_convert_fusion.1
  103.9 43.3 %all_to_all.21 = bf16[64,8,1024]{2,1,0:T(8,128)(2,1)S(1)} all-to-all(bf16[64,8,1024]{2,1,0:T(8,128)(2,1)S(1)} %bitcast.113), channel_id=1, replica_groups=mesh['section'=32,'aux'=2,'dp'=8] {'section','aux'}, dimensions={0} | all-to-all | bytes 2097152 | tf_op jit(solution)/shard_map/all_to_all | solution.py:92
  147.2 0.0 reduce-scatter.2.cloned.1.call-done
  147.2 14.3 %all-to-all-start.3 = ((bf16[64,8,256]{2,1,0:T(8,128)(2,1)}), bf16[64,8,256]{2,1,0:T(8,128)(2,1)S(1)}, u32[]{:S(2)}, u32[]{:S(2)}) async-start(bf16[64,8,256]{2,1,0:T(8,128)(2,1)} %bitcast.128), calls=%async_computation.4 | async-start | bytes 524288 | tf_op jit(solution)/shard_map/all_to_all | solution.py:81
  161.5 1.1 bitcast_reduce_fusion
  162.6 12.4 %all-to-all-done.3 = bf16[64,8,256]{2,1,0:T(8,128)(2,1)S(1)} async-done(((bf16[64,8,256]{2,1,0:T(8,128)(2,1)}), bf16[64,8,256]{2,1,0:T(8,128)(2,1)S(1)}, u32[]{:S(2)}, u32[]{:S(2)}) %all-to-all-start.3) | async-done | bytes 262176 | tf_op jit(solution)/shard_map/all_to_all | solution.py:81
  174.9 0.9 convert.5
  (3 shorter events, 0.1 us)
Async XLA Ops:
  7.2 63.7 %all-gather.3.cloned.1.call-start = ((), (), s32[]{:S(2)}) async-start(), calls=%async_computation.6 | async-start | bytes 2359296 | tf_op jit(solution)/shard_map/all_gather | solution.py:56
  35.6 7.8 %copy-start.3 = (bf16[1,256,2048]{2,1,0:T(8,128)(2,1)S(1)}, bf16[1,256,2048]{2,1,0:T(8,128)(2,1)}, u32[]{:S(2)}) copy-start(bf16[1,256,2048]{2,1,0:T(8,128)(2,1)} %param.7) | copy-start | bytes 3145732
  37.8 6.9 %copy-start.2 = (bf16[1,256,2048]{2,1,0:T(8,128)(2,1)S(1)}, bf16[1,256,2048]{2,1,0:T(8,128)(2,1)}, u32[]{:S(2)}) copy-start(bf16[1,256,2048]{2,1,0:T(8,128)(2,1)} %param.8) | copy-start | bytes 3145732
  37.8 37.3 %all-to-all-start = ((bf16[64,8,1024]{2,1,0:T(8,128)(2,1)}), bf16[64,8,1024]{2,1,0:T(8,128)(2,1)S(1)}, u32[]{:S(2)}, u32[]{:S(2)}) async-start(bf16[64,8,1024]{2,1,0:T(8,128)(2,1)} %bitcast.3), calls=%async_computation | async-start | bytes 2097152 | tf_op jit(solution)/shard_map/all_to_all | solution.py:64
  43.3 103.9 %reduce-scatter.2.cloned.1.call-start = ((), (), s32[]{:S(2)}) async-start(), calls=%async_computation.5 | async-start | bytes 2359296 | tf_op jit(solution)/shard_map/reduce_scatter | solution.py:80
  44.7 1.6 copy-start.4
  80.6 2.9 %copy-start = (f32[1,256,2048]{1,2,0:T(8,128)S(1)}, f32[1,256,2048]{1,2,0:T(8,128)}, u32[]{:S(2)}) copy-start(f32[1,256,2048]{1,2,0:T(8,128)} %copy.56) | copy-start | bytes 6291460
  84.6 1.0 copy-start.1
  147.2 27.7 %all-to-all-start.3 = ((bf16[64,8,256]{2,1,0:T(8,128)(2,1)}), bf16[64,8,256]{2,1,0:T(8,128)(2,1)S(1)}, u32[]{:S(2)}, u32[]{:S(2)}) async-start(bf16[64,8,256]{2,1,0:T(8,128)(2,1)} %bitcast.128), calls=%async_computation.4 | async-start | bytes 524288 | tf_op jit(solution)/shard_map/all_to_all | solution.py:81
Sparse Core Ops, SparseCore 0:
  35.7 35.0 all-gather.2
  103.3 43.3 reduce-scatter.1

commit v2 on v1

v2 whole, which is shorter than its diff:
```python
import math

import jax
import jax.numpy as jnp
from jax import lax
from jax.experimental import pallas as pl
from jax.experimental.pallas import tpu as pltpu
from jax.sharding import PartitionSpec as P

HEAD_DIM = 128
F32 = jnp.float32
BF16 = jnp.bfloat16
W_SCALE = 2.0**18


def dot(a, b, dims):
    return lax.dot_general(a, b, (dims, ((), ())), preferred_element_type=F32)


NN = ((1,), (0,))
NT = ((1,), (1,))
TN = ((0,), (0,))


def order_weights(w_ref, wk_ref, wv_ref):
    shards, sections, two_blk, part = w_ref.shape
    blk = two_blk // 2
    for pair in range(shards // 2):
        one = w_ref[2 * pair].astype(F32)
        two = w_ref[2 * pair + 1].astype(F32)
        keys = jnp.concatenate([one[:, :blk], two[:, :blk]], axis=1)
        values = jnp.concatenate([one[:, blk:], two[:, blk:]], axis=1)
        wk_ref[:, pair] = keys.astype(BF16)
        wv_ref[:, pair] = values.astype(BF16)


def attend_kernel(me_ref, w_ref, r_ref, docr_ref, docc_ref, q_any, g_any,
                  dw_ref, dc_ref, wk_ref, wv_ref,
                  q_ref, g_ref, rows_ref, bias_ref, dk_ref, dv_ref, sems):
    shards, sections, two_blk, part = w_ref.shape
    blk = two_blk // 2
    tok = q_ref.shape[0]
    half = tok // 2
    feats = r_ref.shape[2]
    each = tok // sections
    auxes = r_ref.shape[1] // each
    width = sections * shards * blk

    q_copy = pltpu.make_async_copy(q_any, q_ref, sems.at[0])
    g_copy = pltpu.make_async_copy(g_any, g_ref, sems.at[1])
    q_copy.start()
    g_copy.start()
    order_weights(w_ref, wk_ref, wv_ref)
    for a in range(auxes):
        piece = r_ref[:, a * each:(a + 1) * each, :].astype(F32)
        rows_ref[:, a * feats:(a + 1) * feats] = piece.reshape(tok, feats).astype(BF16)

    rows = rows_ref[...]
    keys = dot(rows, wk_ref[...].reshape(width, part), NN).astype(BF16)
    values = dot(rows, wv_ref[...].reshape(width, part), NN).astype(BF16)

    j_at = lax.broadcasted_iota(jnp.int32, (tok, tok), 0)
    i_at = lax.broadcasted_iota(jnp.int32, (tok, tok), 1)
    seen = (docc_ref[...] == docr_ref[...]) & (j_at <= i_at)
    bias_ref[...] = jnp.where(seen, 0.0, -1e30).astype(F32)

    scale = 1.0 / math.sqrt(HEAD_DIM)
    to_two = scale * math.log2(math.e)
    kv_heads = part // HEAD_DIM
    group = q_ref.shape[1] // part

    def softmax(s, bias):
        t = s * to_two + bias
        e = jnp.exp2(t - jnp.max(t, axis=0, keepdims=True))
        return e * (1.0 / jnp.sum(e, axis=0, keepdims=True))

    q_copy.wait()
    g_copy.wait()
    for h in range(kv_heads):
        k_h = keys[:, h * HEAD_DIM:(h + 1) * HEAD_DIM]
        v_h = values[:, h * HEAD_DIM:(h + 1) * HEAD_DIM]
        v_t = v_h.astype(F32).T.astype(BF16)
        dk_ref[...] = jnp.zeros_like(dk_ref)
        dv_ref[...] = jnp.zeros_like(dv_ref)

        def one_head(at):
            cols = pl.ds(pl.multiple_of(at * HEAD_DIM, HEAD_DIM), HEAD_DIM)
            q = q_ref[:, cols]
            goal_t = g_ref[:, cols].astype(F32).T
            s = dot(k_h, q, NT)
            p_a = softmax(s[:half, :half], bias_ref[:half, :half])
            p_b = softmax(s[:, half:], bias_ref[:, half:])
            low = jnp.concatenate([p_a.astype(BF16), jnp.zeros((half, half), BF16)], axis=0)
            p = jnp.concatenate([low, p_b.astype(BF16)], axis=1)
            out_t = dot(v_t, p, NN)
            dout = out_t - goal_t
            dout_b = dout.astype(BF16)
            delta = jnp.sum(dout * out_t, axis=0, keepdims=True)
            dp = dot(v_h, dout_b, NN)
            ds_a = (p_a * (dp[:half, :half] - delta[:, :half]) * scale).astype(BF16)
            ds_b = (p_b * (dp[:, half:] - delta[:, half:]) * scale).astype(BF16)
            ds_low = jnp.concatenate([ds_a, jnp.zeros((half, half), BF16)], axis=0)
            ds = jnp.concatenate([ds_low, ds_b], axis=1)
            return dot(ds, q, NN), dot(p, dout_b, NT)

        def two_heads(step, _):
            dk0, dv0 = one_head(h * group + 2 * step)
            dk1, dv1 = one_head(h * group + 2 * step + 1)
            dk_ref[...] += dk0 + dk1
            dv_ref[...] += dv0 + dv1
            return 0

        lax.fori_loop(0, group // 2, two_heads, 0)
        dc_ref[:, h * HEAD_DIM:(h + 1) * HEAD_DIM] = dk_ref[...].astype(BF16)
        dc_ref[:, part + h * HEAD_DIM:part + (h + 1) * HEAD_DIM] = dv_ref[...].astype(BF16)

    me = me_ref[0]
    dcache = dc_ref[...]
    step_rows = 4 * shards * blk
    for at in range(sections // 4):
        x = rows_ref[:, at * step_rows:(at + 1) * step_rows]
        full = dot(x, dcache, TN).reshape(4, shards, blk, 2 * part)
        for d in range(shards):
            both = jnp.concatenate([full[:, d, :, :part], full[:, d, :, part:]], axis=1)
            dw_ref[lax.rem(d + shards - me, shards), at * 4:(at + 1) * 4] = both.astype(BF16)


def rows_kernel(w_ref, dc_ref, out_ref, wk_ref, wv_ref):
    shards, sections, two_blk, part = w_ref.shape
    width = sections * shards * two_blk // 2
    feats = out_ref.shape[2]
    auxes = width // feats
    each = dc_ref.shape[0] // sections
    order_weights(w_ref, wk_ref, wv_ref)
    w_k = wk_ref[...].reshape(width, part)
    w_v = wv_ref[...].reshape(width, part)
    for a in range(auxes):
        span = slice(a * feats, (a + 1) * feats)
        term = dot(dc_ref[:, :part], w_k[span], NT) + dot(dc_ref[:, part:], w_v[span], NT)
        out_ref[:, a * each:(a + 1) * each, :] = term.reshape(sections, each, feats).astype(BF16)


def double_kernel(x_ref, out_ref):
    for a in range(out_ref.shape[1]):
        out_ref[:, a] = x_ref[...]


def double(x, auxes):
    return pl.pallas_call(
        double_kernel,
        out_shape=jax.ShapeDtypeStruct((x.shape[0], auxes) + x.shape[1:], x.dtype),
        in_specs=[whole()],
        out_specs=whole(),
        compiler_params=pltpu.CompilerParams(vmem_limit_bytes=8 * 2**20),
        cost_estimate=pl.CostEstimate(flops=0, bytes_accessed=2 * (1 + auxes) * x.size, transcendentals=0),
        name="double",
    )(x)


def whole(space=pltpu.VMEM):
    return pl.BlockSpec(memory_space=space)


def attend(me, w_all, r_in, queries, goal, docs):
    shards, sections, two_blk, part = w_all.shape
    tok = queries.shape[0]
    width = sections * shards * two_blk // 2
    ordered = (sections, shards // 2, two_blk, part)
    return pl.pallas_call(
        attend_kernel,
        out_shape=(
            jax.ShapeDtypeStruct(w_all.shape, BF16),
            jax.ShapeDtypeStruct((tok, 2 * part), BF16),
        ),
        in_specs=[whole(pltpu.SMEM)] + [whole()] * 4 + [whole(pl.ANY)] * 2,
        out_specs=(whole(),) * 2,
        scratch_shapes=[
            pltpu.VMEM(ordered, BF16),
            pltpu.VMEM(ordered, BF16),
            pltpu.VMEM(queries.shape, BF16),
            pltpu.VMEM(queries.shape, BF16),
            pltpu.VMEM((tok, width), BF16),
            pltpu.VMEM((tok, tok), F32),
            pltpu.VMEM((tok, HEAD_DIM), F32),
            pltpu.VMEM((tok, HEAD_DIM), F32),
            pltpu.SemaphoreType.DMA((2,)),
        ],
        compiler_params=pltpu.CompilerParams(vmem_limit_bytes=16 * 2**20),
        cost_estimate=pl.CostEstimate(
            flops=2 * (2 * tok * width * 2 * part + 5 * tok * tok * queries.shape[1]),
            bytes_accessed=9 * 2**20,
            transcendentals=tok * tok * queries.shape[1] // HEAD_DIM,
        ),
        name="attend",
    )(me, w_all, r_in, docs.reshape(1, tok), docs.reshape(tok, 1), queries, goal)


def row_terms(w_all, dcache, feats):
    shards, sections, two_blk, part = w_all.shape
    tok = dcache.shape[0]
    width = sections * shards * two_blk // 2
    ordered = (sections, shards // 2, two_blk, part)
    return pl.pallas_call(
        rows_kernel,
        out_shape=jax.ShapeDtypeStruct((sections, tok // sections * (width // feats), feats), BF16),
        in_specs=[whole()] * 2,
        out_specs=whole(),
        scratch_shapes=[pltpu.VMEM(ordered, BF16), pltpu.VMEM(ordered, BF16)],
        compiler_params=pltpu.CompilerParams(vmem_limit_bytes=10 * 2**20),
        cost_estimate=pl.CostEstimate(
            flops=4 * tok * width * part, bytes_accessed=4 * 2**20, transcendentals=0
        ),
        name="row_terms",
    )(w_all, dcache)


def reduce_ring(terms, axis):
    n = lax.axis_size(axis)
    ahead = [(i, (i + 1) % n) for i in range(n)]
    back = [(i, (i - 1) % n) for i in range(n)]
    far = n // 2
    up = terms[far]
    for k in range(far - 1, -1, -1):
        up = lax.ppermute(up, axis, ahead)
        if k:
            up = (up.astype(F32) + terms[k].astype(F32)).astype(BF16)
    total = terms[0].astype(F32) + up.astype(F32)
    if n - far > 1:
        down = terms[far + 1]
        for k in range(far + 2, n):
            down = lax.ppermute(down, axis, back)
            down = (down.astype(F32) + terms[k].astype(F32)).astype(BF16)
        down = lax.ppermute(down, axis, back)
        total = total + down.astype(F32)
    return total.astype(BF16)


def per_device(aux_rows, predictors, queries, target, lengths):
    sections = lax.axis_size("section")
    auxes = lax.axis_size("aux")
    shards = lax.axis_size("dp")
    both = ("section", "aux")
    peers = sections * auxes
    blk, width = predictors.shape[4:]
    part = width // auxes
    rows_each, feats = aux_rows.shape[2:]
    tok = sections * rows_each

    w_out = predictors.reshape(sections, blk, auxes, part).swapaxes(1, 2).reshape(peers, blk, part)
    w_out = (w_out * W_SCALE).astype(jnp.float16)
    w_in = lax.all_to_all(w_out, both, split_axis=0, concat_axis=0, tiled=True)

    r_out = double(aux_rows.reshape(sections, rows_each, feats), auxes).reshape(
        peers, rows_each, feats
    )
    w_in, r_out = lax.optimization_barrier((w_in, r_out))
    r_in = lax.all_to_all(r_out, both, split_axis=0, concat_axis=0, tiled=True)
    r_in = r_in.reshape(sections, auxes * rows_each, feats)

    w_all = lax.all_gather(w_in, "dp", axis=0)
    w_all = (w_all.astype(F32) * (1.0 / W_SCALE)).astype(BF16)
    w_all = w_all.reshape(shards, sections, auxes * blk, part)

    ends = jnp.cumsum(lengths[0])
    pos = jnp.arange(tok, dtype=jnp.int32)
    docs = jnp.sum((pos[:, None] >= ends[None, :]).astype(jnp.int32), axis=1)
    me = lax.axis_index("dp").astype(jnp.int32).reshape(1)
    dw, dcache = attend(me, w_all, r_in, queries[0], target[0], docs)

    r_send = row_terms(w_all, dcache, feats).reshape(peers, rows_each, feats)
    r_back = lax.all_to_all(r_send, both, split_axis=0, concat_axis=0, tiled=True)
    w_sum = reduce_ring([dw[k] for k in range(shards)], "dp")
    w_sum, r_back = lax.optimization_barrier((w_sum, r_back))
    w_back = lax.all_to_all(w_sum.reshape(peers, blk, part), both, split_axis=0, concat_axis=0, tiled=True)
    grad_predictors = (
        w_back.reshape(sections, auxes, blk, part).swapaxes(1, 2).reshape(predictors.shape)
    ).astype(F32)
    r_sum = jnp.sum(r_back.reshape(sections, auxes, rows_each, feats).astype(F32), axis=1)
    grad_rows = r_sum.astype(BF16).reshape(aux_rows.shape)
    return (grad_rows, grad_predictors)


def solution(mesh):
    return jax.shard_map(
        per_device,
        mesh=mesh,
        in_specs=(
            P(None, "dp", "section", "aux"),
            P("aux", None, "section", "dp", None, None),
            P("section", "dp", "aux"),
            P("section", "dp", "aux"),
            P("dp", None),
        ),
        out_specs=(P(None, "dp", "section", "aux"), P("aux", None, "section", "dp", None, None)),
        check_vma=False,
    )
```

time: 183 us -> 167 us (0.913); the launches traced: 183 us -> 164 us
  starting transfers between devices: 19.8 us -> 70.7 us
  blocking collectives: 71.6 us -> 27.4 us
  local copies, waits for them, and re-layouts: 21.2 us -> 3.67 us
  matrix products: 14.3 us -> 0 us
  between operations: 14.1 us -> 0.81 us
  Pallas kernels: 0 us -> 13.2 us
  waiting for transfers between devices: 35.9 us -> 42.8 us
    all_to_all x2 -> x0, blocking collectives: 71.6 us -> none  [the longest x1 43.3 us: per_device(): lax.all_to_all(r_send, both, split_axis=0, concat_axis=0, tiled=True)]
    all_to_all x0 -> x2, starting transfers between devices: none -> 29.4 us  [the longest x1 15 us: per_device(): w_in = lax.all_to_all(w_out, both, split_axis=0, concat_axis=0, tiled=True)]
    all_gather x0 -> x1, blocking collectives: none -> 27.4 us  [per_device(): w_all = lax.all_gather(w_in, 'dp', axis=0)]
    all_gather x1 -> x0, waiting for transfers between devices: 23.5 us -> none  [per_device(): w_all = lax.all_gather(w_in, 'dp', axis=0)]
    ppermute x0 -> x7, starting transfers between devices: none -> 21.9 us  [the longest x3 14 us: reduce_ring(): down = lax.ppermute(down, axis, back)]
    ppermute x0 -> x7, waiting for transfers between devices: none -> 18.7 us  [the longest x4 15.7 us: reduce_ring(): up = lax.ppermute(up, axis, ahead)]
    pallas_call x0 -> x3, Pallas kernels: none -> 13.2 us  [the longest x1 10.4 us: attend(): pl.pallas_call(attend_kernel, out_shape=(jax.ShapeDtypeStruct(w_all.shape...]
    all_to_all x0 -> x2, waiting for transfers between devices: none -> 11.3 us  [the longest x1 11.3 us: per_device(): w_in = lax.all_to_all(w_out, both, split_axis=0, concat_axis=0, tiled=True)]
  transfers between devices with their start and end apart: 4 -> 11, of which waited for: 2 -> 9; matrix products, arithmetic and copies ran while one was open for 7% -> 2% of each run, Pallas kernels for 0% -> 1%
where the time goes in v2:
time: 167 us; the launch traced here: 164 us
  starting transfers between devices  70.7 us (42%)
  waiting for transfers between devices  42.8 us (26%)
  blocking collectives  27.4 us (16%)
  Pallas kernels  13.2 us (8%)
  other arithmetic  5.64 us (3%)
  local copies, waits for them, and re-layouts  3.67 us (2%)
    all_gather x1, blocking collectives, per_device(): w_all = lax.all_gather(w_in, 'dp', axis=0)  27.4 us
    ppermute x4, waiting for transfers between devices, reduce_ring(): up = lax.ppermute(up, axis, ahead)  15.7 us
    all_to_all x1, starting transfers between devices, per_device(): w_in = lax.all_to_all(w_out, both, split_axis=0, concat_axis=0, tiled=True)  15 us
    all_to_all x1, starting transfers between devices, per_device(): lax.all_to_all(r_send, both, split_axis=0, concat_axis=0, tiled=True)  14.4 us
    all_to_all x1, starting transfers between devices, per_device(): lax.all_to_all(w_sum.reshape(peers, blk, part), both, split_axis=0, conca...  14.1 us
    ppermute x3, starting transfers between devices, reduce_ring(): down = lax.ppermute(down, axis, back)  14 us
    all_to_all x1, waiting for transfers between devices, per_device(): lax.all_to_all(w_sum.reshape(peers, blk, part), both, split_axis=0, conca...  12.4 us
    all_to_all x1, waiting for transfers between devices, per_device(): w_in = lax.all_to_all(w_out, both, split_axis=0, concat_axis=0, tiled=True)  11.3 us
  transfers between devices with their start and end apart: 11, of which 9 were waited for; matrix products, arithmetic and copies ran while one was open for 2% of the time, Pallas kernels for 1%

profile of v2, /device:TPU:1, one launch (start us, length us, event | category | flops | bytes accessed | tf_op | source)
XLA Modules:
  0.0 164.1 jit_solution(11249480144258290034)
XLA Ops:
  0.6 1.7 %multiply_convert_fusion.1 = f16[1,32,1,1,8,512]{5,4,3,2,1,0:T(8,128)(2,1)} fusion(bf16[1,32,1,1,8,512]{5,4,3,2,1,0:T(8,128)(2,1)} %param.6), kind=kLoop, calls=%fused_computation.17 | loop fusion | flops 262144 | bytes 524288 | tf_op jit(solution)/shard_map/convert_element_type | solution.py:250
  2.3 0.0 copy-start.5
  2.3 15.0 %all-to-all-start = ((f16[64,8,256]{2,1,0:T(8,128)(2,1)}), f16[64,8,256]{2,1,0:T(8,128)(2,1)S(1)}, u32[]{:S(2)}, u32[]{:S(2)}) async-start(f16[64,8,256]{2,1,0:T(8,128)(2,1)} %bitcast.3), calls=%async_computation | async-start | bytes 524288 | tf_op jit(solution)/shard_map/all_to_all | solution.py:251
  17.3 0.0 copy-start.2
  17.3 1.0 copy-done.2
  18.4 1.0 double.1
  19.4 11.3 %all-to-all-done = f16[64,8,256]{2,1,0:T(8,128)(2,1)S(1)} async-done(((f16[64,8,256]{2,1,0:T(8,128)(2,1)}), f16[64,8,256]{2,1,0:T(8,128)(2,1)S(1)}, u32[]{:S(2)}, u32[]{:S(2)}) %all-to-all-start) | async-done | bytes 262176 | tf_op jit(solution)/shard_map/all_to_all | solution.py:251
  30.7 5.3 %all-to-all-start.1 = ((bf16[64,8,1024]{2,1,0:T(8,128)(2,1)}), bf16[64,8,1024]{2,1,0:T(8,128)(2,1)S(1)}, u32[]{:S(2)}, u32[]{:S(2)}) async-start(bf16[64,8,1024]{2,1,0:T(8,128)(2,1)} %bitcast.5), calls=%async_computation.1 | async-start | bytes 2097152 | tf_op jit(solution)/shard_map/all_to_all | solution.py:257
  36.1 0.0 copy-done.5
  36.1 0.2 reduce-window.8
  36.3 0.1 convert_reduce_fusion
  36.4 0.1 copy.9.docc_ref
  36.5 27.4 %all-gather.2 = f16[512,8,256]{2,1,0:T(8,128)(2,1)S(1)} all-gather(f16[64,8,256]{2,1,0:T(8,128)(2,1)S(1)} %all-to-all-done), channel_id=2, replica_groups=mesh['section'=32,'aux'=2,'dp'=8] {'dp'}, dimensions={0}, use_global_device_ids=true | all-gather | bytes 2359296 | tf_op jit(solution)/shard_map/all_gather | solution.py:260
  63.9 0.6 multiply_convert_fusion
  64.5 0.4 all-to-all-done.1
  64.8 0.0 copy-start.3
  64.8 1.2 copy-done.3
  66.0 0.0 copy-start.4
  66.1 1.2 copy-done.4
  67.3 10.4 %attend.1 = (bf16[8,32,16,256]{3,2,1,0:T(8,128)(2,1)S(1)}, bf16[256,512]{1,0:T(8,128)(2,1)S(1)}) custom-call(s32[1]{0:T(128)} %bitcast.me_ref, bf16[8,32,16,256]{3,2,1,0:T(8,128)(2,1)S(1)} %bitcast.48, bf16[32,16,1024]{2,1,0:T(8,128)(2,1)S(1)} %bitcast.50, s32[1,256]{1,0:T(1,128)S(1)} %bitcast.53, s32[256,1]{1,0:T(8,128)S(1)} %copy.9.docc_ref, ...), custom_call_target="tpu_custom_call" | custom-call | flops 2415919104 | bytes 9437184 | tf_op jit(solution)/shard_map/attend/pallas_call | solution.py:169
  77.7 0.0 copy-start
  77.7 1.7 %row_terms.1 = bf16[32,16,1024]{2,1,0:T(8,128)(2,1)} custom-call(bf16[8,32,16,256]{3,2,1,0:T(8,128)(2,1)S(1)} %bitcast.49, bf16[256,512]{1,0:T(8,128)(2,1)S(1)} %get-tuple-element.11.dc_ref), custom_call_target="tpu_custom_call" | custom-call | flops 536870912 | bytes 4194304 | tf_op jit(solution)/shard_map/row_terms/pallas_call | solution.py:203
  79.4 0.0 copy-done
  79.4 0.0 copy-start.1
  79.4 14.4 %all-to-all-start.2 = ((bf16[64,8,1024]{2,1,0:T(8,128)(2,1)}), bf16[64,8,1024]{2,1,0:T(8,128)(2,1)S(1)}, u32[]{:S(2)}, u32[]{:S(2)}) async-start(bf16[64,8,1024]{2,1,0:T(8,128)(2,1)} %bitcast.22), calls=%async_computation.2 | async-start | bytes 2097152 | tf_op jit(solution)/shard_map/all_to_all | solution.py:271
  93.8 0.0 copy-done.1
  93.9 2.1 %collective-permute-start = (bf16[32,16,256]{2,1,0:T(8,128)(2,1)S(1)}, bf16[32,16,256]{2,1,0:T(8,128)(2,1)S(1)}, u32[]{:S(2)}, u32[]{:S(2)}) collective-permute-start(bf16[32,16,256]{2,1,0:T(8,128)(2,1)S(1)} %get-tuple-element.18), channel_id=1, source_target_pairs={{0,1},{1,2},{2,3},{3,4},{4,5},{5,6},{6,7},{7,0},{8,9},{9,10},{10,1... | collective-permute-start | bytes 786440 | tf_op jit(solution)/shard_map/ppermute | solution.py:224
  96.0 4.4 %collective-permute-start.4 = (bf16[32,16,256]{2,1,0:T(8,128)(2,1)S(1)}, bf16[32,16,256]{2,1,0:T(8,128)(2,1)S(1)}, u32[]{:S(2)}, u32[]{:S(2)}) collective-permute-start(bf16[32,16,256]{2,1,0:T(8,128)(2,1)S(1)} %get-tuple-element.19), channel_id=1, source_target_pairs={{0,7},{1,0},{2,1},{3,2},{4,3},{5,4},{6,5},{7,6},{8,15},{9,8},{10,9... | collective-permute-start | bytes 786440 | tf_op jit(solution)/shard_map/ppermute | solution.py:231
  100.4 4.0 %collective-permute-done = bf16[32,16,256]{2,1,0:T(8,128)(2,1)S(1)} collective-permute-done((bf16[32,16,256]{2,1,0:T(8,128)(2,1)S(1)}, bf16[32,16,256]{2,1,0:T(8,128)(2,1)S(1)}, u32[]{:S(2)}, u32[]{:S(2)}) %collective-permute-start) | collective-permute-done | bytes 262176 | tf_op jit(solution)/shard_map/ppermute | solution.py:224
  104.4 0.1 fusion.4
  104.5 1.9 %collective-permute-start.1 = (bf16[32,16,256]{2,1,0:T(8,128)(2,1)S(1)}, bf16[32,16,256]{2,1,0:T(8,128)(2,1)S(1)}, u32[]{:S(2)}, u32[]{:S(2)}) collective-permute-start(bf16[32,16,256]{2,1,0:T(8,128)(2,1)S(1)} %fusion.4), channel_id=1, source_target_pairs={{0,1},{1,2},{2,3},{3,4},{4,5},{5,6},{6,7},{7,0},{8,9},{9,10},{10,1... | collective-permute-start | bytes 786440 | tf_op jit(solution)/shard_map/ppermute | solution.py:224
  106.4 0.0 collective-permute-done.4
  106.5 7.7 %collective-permute-done.1 = bf16[32,16,256]{2,1,0:T(8,128)(2,1)S(1)} collective-permute-done((bf16[32,16,256]{2,1,0:T(8,128)(2,1)S(1)}, bf16[32,16,256]{2,1,0:T(8,128)(2,1)S(1)}, u32[]{:S(2)}, u32[]{:S(2)}) %collective-permute-start.1) | collective-permute-done | bytes 262176 | tf_op jit(solution)/shard_map/ppermute | solution.py:224
  114.1 0.1 fusion.3
  114.3 1.9 %collective-permute-start.2 = (bf16[32,16,256]{2,1,0:T(8,128)(2,1)S(1)}, bf16[32,16,256]{2,1,0:T(8,128)(2,1)S(1)}, u32[]{:S(2)}, u32[]{:S(2)}) collective-permute-start(bf16[32,16,256]{2,1,0:T(8,128)(2,1)S(1)} %get-tuple-element.16), channel_id=1, source_target_pairs={{0,1},{1,2},{2,3},{3,4},{4,5},{5,6},{6,7},{7,0},{8,9},{9,10},{10,1... | collective-permute-start | bytes 786440 | tf_op jit(solution)/shard_map/ppermute | solution.py:224
  116.2 4.6 %collective-permute-start.5 = (bf16[32,16,256]{2,1,0:T(8,128)(2,1)S(1)}, bf16[32,16,256]{2,1,0:T(8,128)(2,1)S(1)}, u32[]{:S(2)}, u32[]{:S(2)}) collective-permute-start(bf16[32,16,256]{2,1,0:T(8,128)(2,1)S(1)} %get-tuple-element.17), channel_id=1, source_target_pairs={{0,7},{1,0},{2,1},{3,2},{4,3},{5,4},{6,5},{7,6},{8,15},{9,8},{10,9... | collective-permute-start | bytes 786440 | tf_op jit(solution)/shard_map/ppermute | solution.py:231
  120.8 2.2 %collective-permute-done.2 = bf16[32,16,256]{2,1,0:T(8,128)(2,1)S(1)} collective-permute-done((bf16[32,16,256]{2,1,0:T(8,128)(2,1)S(1)}, bf16[32,16,256]{2,1,0:T(8,128)(2,1)S(1)}, u32[]{:S(2)}, u32[]{:S(2)}) %collective-permute-start.2) | collective-permute-done | bytes 262176 | tf_op jit(solution)/shard_map/ppermute | solution.py:224
  123.0 1.1 collective-permute-done.5
  124.1 0.1 fusion.2
  124.2 1.9 %collective-permute-start.3 = (bf16[32,16,256]{2,1,0:T(8,128)(2,1)S(1)}, bf16[32,16,256]{2,1,0:T(8,128)(2,1)S(1)}, u32[]{:S(2)}, u32[]{:S(2)}) collective-permute-start(bf16[32,16,256]{2,1,0:T(8,128)(2,1)S(1)} %get-tuple-element.14), channel_id=1, source_target_pairs={{0,1},{1,2},{2,3},{3,4},{4,5},{5,6},{6,7},{7,0},{8,9},{9,10},{10,1... | collective-permute-start | bytes 786440 | tf_op jit(solution)/shard_map/ppermute | solution.py:224
  126.1 5.0 %collective-permute-start.6 = (bf16[32,16,256]{2,1,0:T(8,128)(2,1)S(1)}, bf16[32,16,256]{2,1,0:T(8,128)(2,1)S(1)}, u32[]{:S(2)}, u32[]{:S(2)}) collective-permute-start(bf16[32,16,256]{2,1,0:T(8,128)(2,1)S(1)} %get-tuple-element.15), channel_id=1, source_target_pairs={{0,7},{1,0},{2,1},{3,2},{4,3},{5,4},{6,5},{7,6},{8,15},{9,8},{10,9... | collective-permute-start | bytes 786440 | tf_op jit(solution)/shard_map/ppermute | solution.py:233
  131.2 1.8 %collective-permute-done.3 = bf16[32,16,256]{2,1,0:T(8,128)(2,1)S(1)} collective-permute-done((bf16[32,16,256]{2,1,0:T(8,128)(2,1)S(1)}, bf16[32,16,256]{2,1,0:T(8,128)(2,1)S(1)}, u32[]{:S(2)}, u32[]{:S(2)}) %collective-permute-start.3) | collective-permute-done | bytes 262176 | tf_op jit(solution)/shard_map/ppermute | solution.py:224
  133.0 1.9 %collective-permute-done.6 = bf16[32,16,256]{2,1,0:T(8,128)(2,1)S(1)} collective-permute-done((bf16[32,16,256]{2,1,0:T(8,128)(2,1)S(1)}, bf16[32,16,256]{2,1,0:T(8,128)(2,1)S(1)}, u32[]{:S(2)}, u32[]{:S(2)}) %collective-permute-start.6) | collective-permute-done | bytes 262176 | tf_op jit(solution)/shard_map/ppermute | solution.py:233
  134.9 0.8 fusion.6
  135.7 0.0 all-to-all-done.2
  135.7 14.1 %all-to-all-start.3 = ((bf16[64,8,256]{2,1,0:T(8,128)(2,1)}), bf16[64,8,256]{2,1,0:T(8,128)(2,1)S(1)}, u32[]{:S(2)}, u32[]{:S(2)}) async-start(bf16[64,8,256]{2,1,0:T(8,128)(2,1)} %bitcast.25), calls=%async_computation.3 | async-start | bytes 524288 | tf_op jit(solution)/shard_map/all_to_all | solution.py:274
  149.9 1.1 bitcast_reduce_fusion
  150.9 12.4 %all-to-all-done.3 = bf16[64,8,256]{2,1,0:T(8,128)(2,1)S(1)} async-done(((bf16[64,8,256]{2,1,0:T(8,128)(2,1)}), bf16[64,8,256]{2,1,0:T(8,128)(2,1)S(1)}, u32[]{:S(2)}, u32[]{:S(2)}) %all-to-all-start.3) | async-done | bytes 262176 | tf_op jit(solution)/shard_map/all_to_all | solution.py:274
  163.3 0.9 convert.16
  (1 shorter events, 0.0 us)
Async XLA Ops:
  2.3 33.8 %copy-start.5 = (s32[1,4]{1,0:T(1,128)S(1)}, s32[1,4]{1,0:T(1,128)}, u32[]{:S(2)}) copy-start(s32[1,4]{1,0:T(1,128)} %param.9) | copy-start | bytes 52
  2.3 28.4 %all-to-all-start = ((f16[64,8,256]{2,1,0:T(8,128)(2,1)}), f16[64,8,256]{2,1,0:T(8,128)(2,1)S(1)}, u32[]{:S(2)}, u32[]{:S(2)}) async-start(f16[64,8,256]{2,1,0:T(8,128)(2,1)} %bitcast.3), calls=%async_computation | async-start | bytes 524288 | tf_op jit(solution)/shard_map/all_to_all | solution.py:251
  17.3 1.0 copy-start.2
  30.7 34.1 %all-to-all-start.1 = ((bf16[64,8,1024]{2,1,0:T(8,128)(2,1)}), bf16[64,8,1024]{2,1,0:T(8,128)(2,1)S(1)}, u32[]{:S(2)}, u32[]{:S(2)}) async-start(bf16[64,8,1024]{2,1,0:T(8,128)(2,1)} %bitcast.5), calls=%async_computation.1 | async-start | bytes 2097152 | tf_op jit(solution)/shard_map/all_to_all | solution.py:257
  64.8 1.2 copy-start.3
  66.0 1.2 copy-start.4
  77.7 1.7 %copy-start = (bf16[8,32,16,256]{3,2,1,0:T(8,128)(2,1)}, bf16[8,32,16,256]{3,2,1,0:T(8,128)(2,1)S(1)}, u32[]{:S(2)}) copy-start(bf16[8,32,16,256]{3,2,1,0:T(8,128)(2,1)S(1)} %get-tuple-element.10) | copy-start | bytes 6291460
  79.4 14.4 %copy-start.1 = (bf16[8,32,16,256]{3,2,1,0:T(8,128)(2,1)S(1)}, bf16[8,32,16,256]{3,2,1,0:T(8,128)(2,1)}, u32[]{:S(2)}) copy-start(bf16[8,32,16,256]{3,2,1,0:T(8,128)(2,1)} %copy-done) | copy-start | bytes 6291460
  79.4 56.3 %all-to-all-start.2 = ((bf16[64,8,1024]{2,1,0:T(8,128)(2,1)}), bf16[64,8,1024]{2,1,0:T(8,128)(2,1)S(1)}, u32[]{:S(2)}, u32[]{:S(2)}) async-start(bf16[64,8,1024]{2,1,0:T(8,128)(2,1)} %bitcast.22), calls=%async_computation.2 | async-start | bytes 2097152 | tf_op jit(solution)/shard_map/all_to_all | solution.py:271
  93.9 10.5 %collective-permute-start = (bf16[32,16,256]{2,1,0:T(8,128)(2,1)S(1)}, bf16[32,16,256]{2,1,0:T(8,128)(2,1)S(1)}, u32[]{:S(2)}, u32[]{:S(2)}) collective-permute-start(bf16[32,16,256]{2,1,0:T(8,128)(2,1)S(1)} %get-tuple-element.18), channel_id=1, source_target_pairs={{0,1},{1,2},{2,3},{3,4},{4,5},{5,6},{6,7},{7,0},{8,9},{9,10},{10,1... | collective-permute-start | bytes 786440 | tf_op jit(solution)/shard_map/ppermute | solution.py:224
  96.0 10.4 %collective-permute-start.4 = (bf16[32,16,256]{2,1,0:T(8,128)(2,1)S(1)}, bf16[32,16,256]{2,1,0:T(8,128)(2,1)S(1)}, u32[]{:S(2)}, u32[]{:S(2)}) collective-permute-start(bf16[32,16,256]{2,1,0:T(8,128)(2,1)S(1)} %get-tuple-element.19), channel_id=1, source_target_pairs={{0,7},{1,0},{2,1},{3,2},{4,3},{5,4},{6,5},{7,6},{8,15},{9,8},{10,9... | collective-permute-start | bytes 786440 | tf_op jit(solution)/shard_map/ppermute | solution.py:231
  104.5 9.6 %collective-permute-start.1 = (bf16[32,16,256]{2,1,0:T(8,128)(2,1)S(1)}, bf16[32,16,256]{2,1,0:T(8,128)(2,1)S(1)}, u32[]{:S(2)}, u32[]{:S(2)}) collective-permute-start(bf16[32,16,256]{2,1,0:T(8,128)(2,1)S(1)} %fusion.4), channel_id=1, source_target_pairs={{0,1},{1,2},{2,3},{3,4},{4,5},{5,6},{6,7},{7,0},{8,9},{9,10},{10,1... | collective-permute-start | bytes 786440 | tf_op jit(solution)/shard_map/ppermute | solution.py:224
  114.3 8.7 %collective-permute-start.2 = (bf16[32,16,256]{2,1,0:T(8,128)(2,1)S(1)}, bf16[32,16,256]{2,1,0:T(8,128)(2,1)S(1)}, u32[]{:S(2)}, u32[]{:S(2)}) collective-permute-start(bf16[32,16,256]{2,1,0:T(8,128)(2,1)S(1)} %get-tuple-element.16), channel_id=1, source_target_pairs={{0,1},{1,2},{2,3},{3,4},{4,5},{5,6},{6,7},{7,0},{8,9},{9,10},{10,1... | collective-permute-start | bytes 786440 | tf_op jit(solution)/shard_map/ppermute | solution.py:224
  116.2 7.9 %collective-permute-start.5 = (bf16[32,16,256]{2,1,0:T(8,128)(2,1)S(1)}, bf16[32,16,256]{2,1,0:T(8,128)(2,1)S(1)}, u32[]{:S(2)}, u32[]{:S(2)}) collective-permute-start(bf16[32,16,256]{2,1,0:T(8,128)(2,1)S(1)} %get-tuple-element.17), channel_id=1, source_target_pairs={{0,7},{1,0},{2,1},{3,2},{4,3},{5,4},{6,5},{7,6},{8,15},{9,8},{10,9... | collective-permute-start | bytes 786440 | tf_op jit(solution)/shard_map/ppermute | solution.py:231
  124.2 8.8 %collective-permute-start.3 = (bf16[32,16,256]{2,1,0:T(8,128)(2,1)S(1)}, bf16[32,16,256]{2,1,0:T(8,128)(2,1)S(1)}, u32[]{:S(2)}, u32[]{:S(2)}) collective-permute-start(bf16[32,16,256]{2,1,0:T(8,128)(2,1)S(1)} %get-tuple-element.14), channel_id=1, source_target_pairs={{0,1},{1,2},{2,3},{3,4},{4,5},{5,6},{6,7},{7,0},{8,9},{9,10},{10,1... | collective-permute-start | bytes 786440 | tf_op jit(solution)/shard_map/ppermute | solution.py:224
  126.1 8.8 %collective-permute-start.6 = (bf16[32,16,256]{2,1,0:T(8,128)(2,1)S(1)}, bf16[32,16,256]{2,1,0:T(8,128)(2,1)S(1)}, u32[]{:S(2)}, u32[]{:S(2)}) collective-permute-start(bf16[32,16,256]{2,1,0:T(8,128)(2,1)S(1)} %get-tuple-element.15), channel_id=1, source_target_pairs={{0,7},{1,0},{2,1},{3,2},{4,3},{5,4},{6,5},{7,6},{8,15},{9,8},{10,9... | collective-permute-start | bytes 786440 | tf_op jit(solution)/shard_map/ppermute | solution.py:233
  135.7 27.5 %all-to-all-start.3 = ((bf16[64,8,256]{2,1,0:T(8,128)(2,1)}), bf16[64,8,256]{2,1,0:T(8,128)(2,1)S(1)}, u32[]{:S(2)}, u32[]{:S(2)}) async-start(bf16[64,8,256]{2,1,0:T(8,128)(2,1)} %bitcast.25), calls=%async_computation.3 | async-start | bytes 524288 | tf_op jit(solution)/shard_map/all_to_all | solution.py:274

commit v3 on v2

--- a/solution.py
+++ b/solution.py
@@ -1,3 +1,4 @@
+import functools
 import math
 
 import jax
@@ -11,6 +12,7 @@
 F32 = jnp.float32
 BF16 = jnp.bfloat16
 W_SCALE = 2.0**18
+HOP_FLOPS = 16 * 10**9
 
 
 def dot(a, b, dims):
@@ -34,9 +36,8 @@
         wv_ref[:, pair] = values.astype(BF16)
 
 
-def attend_kernel(me_ref, w_ref, r_ref, docr_ref, docc_ref, q_any, g_any,
-                  dw_ref, dc_ref, wk_ref, wv_ref,
-                  q_ref, g_ref, rows_ref, bias_ref, dk_ref, dv_ref, sems):
+def attend_kernel(groups, me_ref, w_ref, r_ref, q_ref, g_ref, docr_ref, docc_ref, *refs):
+    part_refs, (dc_ref, wk_ref, wv_ref, rows_ref, bias_ref, dw_ref) = refs[:-6], refs[-6:]
     shards, sections, two_blk, part = w_ref.shape
     blk = two_blk // 2
     tok = q_ref.shape[0]
@@ -46,10 +47,6 @@
     auxes = r_ref.shape[1] // each
     width = sections * shards * blk
 
-    q_copy = pltpu.make_async_copy(q_any, q_ref, sems.at[0])
-    g_copy = pltpu.make_async_copy(g_any, g_ref, sems.at[1])
-    q_copy.start()
-    g_copy.start()
     order_weights(w_ref, wk_ref, wv_ref)
     for a in range(auxes):
         piece = r_ref[:, a * each:(a + 1) * each, :].astype(F32)
@@ -74,45 +71,45 @@
         e = jnp.exp2(t - jnp.max(t, axis=0, keepdims=True))
         return e * (1.0 / jnp.sum(e, axis=0, keepdims=True))
 
-    q_copy.wait()
-    g_copy.wait()
+    def whole_square(x_a, x_b):
+        low = jnp.concatenate([x_a, jnp.zeros((half, half), BF16)], axis=0)
+        return jnp.concatenate([low, x_b], axis=1)
+
     for h in range(kv_heads):
         k_h = keys[:, h * HEAD_DIM:(h + 1) * HEAD_DIM]
         v_h = values[:, h * HEAD_DIM:(h + 1) * HEAD_DIM]
         v_t = v_h.astype(F32).T.astype(BF16)
-        dk_ref[...] = jnp.zeros_like(dk_ref)
-        dv_ref[...] = jnp.zeros_like(dv_ref)
-
-        def one_head(at):
-            cols = pl.ds(pl.multiple_of(at * HEAD_DIM, HEAD_DIM), HEAD_DIM)
-            q = q_ref[:, cols]
-            goal_t = g_ref[:, cols].astype(F32).T
-            s = dot(k_h, q, NT)
-            p_a = softmax(s[:half, :half], bias_ref[:half, :half])
-            p_b = softmax(s[:, half:], bias_ref[:, half:])
-            low = jnp.concatenate([p_a.astype(BF16), jnp.zeros((half, half), BF16)], axis=0)
-            p = jnp.concatenate([low, p_b.astype(BF16)], axis=1)
-            out_t = dot(v_t, p, NN)
-            dout = out_t - goal_t
-            dout_b = dout.astype(BF16)
-            delta = jnp.sum(dout * out_t, axis=0, keepdims=True)
-            dp = dot(v_h, dout_b, NN)
-            ds_a = (p_a * (dp[:half, :half] - delta[:, :half]) * scale).astype(BF16)
-            ds_b = (p_b * (dp[:, half:] - delta[:, half:]) * scale).astype(BF16)
-            ds_low = jnp.concatenate([ds_a, jnp.zeros((half, half), BF16)], axis=0)
-            ds = jnp.concatenate([ds_low, ds_b], axis=1)
-            return dot(ds, q, NN), dot(p, dout_b, NT)
-
-        def two_heads(step, _):
-            dk0, dv0 = one_head(h * group + 2 * step)
-            dk1, dv1 = one_head(h * group + 2 * step + 1)
-            dk_ref[...] += dk0 + dk1
-            dv_ref[...] += dv0 + dv1
-            return 0
-
-        lax.fori_loop(0, group // 2, two_heads, 0)
-        dc_ref[:, h * HEAD_DIM:(h + 1) * HEAD_DIM] = dk_ref[...].astype(BF16)
-        dc_ref[:, part + h * HEAD_DIM:part + (h + 1) * HEAD_DIM] = dv_ref[...].astype(BF16)
+
+        def heads_of(h, k_h, v_h, v_t):
+            at = [h * group + n for n in range(group)]
+            cols = [pl.ds(pl.multiple_of(n * HEAD_DIM, HEAD_DIM), HEAD_DIM) for n in at]
+            q = [q_ref[:, c] for c in cols]
+            s = [dot(k_h, x, NT) for x in q]
+            goal = [g_ref[:, c].T.astype(F32) for c in cols]
+            p_a = [softmax(x[:half, :half], bias_ref[:half, :half]) for x in s]
+            p_b = [softmax(x[:, half:], bias_ref[:, half:]) for x in s]
+            p = [whole_square(x.astype(BF16), y.astype(BF16)) for x, y in zip(p_a, p_b)]
+            out = [dot(v_t, x, NN) for x in p]
+            dout = [x - y for x, y in zip(out, goal)]
+            dout_b = [x.astype(BF16) for x in dout]
+            dp = [dot(v_h, x, NN) for x in dout_b]
+            delta = [jnp.sum(x * y, axis=0, keepdims=True) for x, y in zip(dout, out)]
+            ds_a = [
+                (x * (y[:half, :half] - z[:, :half]) * scale).astype(BF16)
+                for x, y, z in zip(p_a, dp, delta)
+            ]
+            ds_b = [
+                (x * (y[:, half:] - z[:, half:]) * scale).astype(BF16)
+                for x, y, z in zip(p_b, dp, delta)
+            ]
+            ds = [whole_square(x, y) for x, y in zip(ds_a, ds_b)]
+            dv = sum(dot(x, y, NT) for x, y in zip(p, dout_b))
+            dk = sum(dot(x, y, NN) for x, y in zip(ds, q))
+            return dk, dv
+
+        dk, dv = heads_of(h, k_h, v_h, v_t)
+        dc_ref[:, h * HEAD_DIM:(h + 1) * HEAD_DIM] = dk.astype(BF16)
+        dc_ref[:, part + h * HEAD_DIM:part + (h + 1) * HEAD_DIM] = dv.astype(BF16)
 
     me = me_ref[0]
     dcache = dc_ref[...]
@@ -123,6 +120,9 @@
         for d in range(shards):
             both = jnp.concatenate([full[:, d, :, :part], full[:, d, :, part:]], axis=1)
             dw_ref[lax.rem(d + shards - me, shards), at * 4:(at + 1) * 4] = both.astype(BF16)
+    for group_at, ref in zip(groups, part_refs):
+        for slot, k in enumerate(group_at):
+            ref[slot] = dw_ref[k]
 
 
 def rows_kernel(w_ref, dc_ref, out_ref, wk_ref, wv_ref):
@@ -161,29 +161,25 @@
     return pl.BlockSpec(memory_space=space)
 
 
-def attend(me, w_all, r_in, queries, goal, docs):
+def attend(me, w_all, r_in, queries, goal, docs, groups):
     shards, sections, two_blk, part = w_all.shape
     tok = queries.shape[0]
     width = sections * shards * two_blk // 2
     ordered = (sections, shards // 2, two_blk, part)
     return pl.pallas_call(
-        attend_kernel,
-        out_shape=(
-            jax.ShapeDtypeStruct(w_all.shape, BF16),
-            jax.ShapeDtypeStruct((tok, 2 * part), BF16),
-        ),
-        in_specs=[whole(pltpu.SMEM)] + [whole()] * 4 + [whole(pl.ANY)] * 2,
-        out_specs=(whole(),) * 2,
+        functools.partial(attend_kernel, groups),
+        out_shape=tuple(
+            jax.ShapeDtypeStruct((len(group),) + w_all.shape[1:], BF16) for group in groups
+        )
+        + (jax.ShapeDtypeStruct((tok, 2 * part), BF16),),
+        in_specs=[whole(pltpu.SMEM)] + [whole()] * 6,
+        out_specs=(whole(),) * (len(groups) + 1),
         scratch_shapes=[
             pltpu.VMEM(ordered, BF16),
             pltpu.VMEM(ordered, BF16),
-            pltpu.VMEM(queries.shape, BF16),
-            pltpu.VMEM(queries.shape, BF16),
             pltpu.VMEM((tok, width), BF16),
             pltpu.VMEM((tok, tok), F32),
-            pltpu.VMEM((tok, HEAD_DIM), F32),
-            pltpu.VMEM((tok, HEAD_DIM), F32),
-            pltpu.SemaphoreType.DMA((2,)),
+            pltpu.VMEM(w_all.shape, BF16),
         ],
         compiler_params=pltpu.CompilerParams(vmem_limit_bytes=16 * 2**20),
         cost_estimate=pl.CostEstimate(
@@ -192,7 +188,7 @@
             transcendentals=tok * tok * queries.shape[1] // HEAD_DIM,
         ),
         name="attend",
-    )(me, w_all, r_in, docs.reshape(1, tok), docs.reshape(tok, 1), queries, goal)
+    )(me, w_all, r_in, queries, goal, docs.reshape(1, tok), docs.reshape(tok, 1))
 
 
 def row_terms(w_all, dcache, feats):
@@ -206,7 +202,7 @@
         in_specs=[whole()] * 2,
         out_specs=whole(),
         scratch_shapes=[pltpu.VMEM(ordered, BF16), pltpu.VMEM(ordered, BF16)],
-        compiler_params=pltpu.CompilerParams(vmem_limit_bytes=10 * 2**20),
+        compiler_params=pltpu.CompilerParams(vmem_limit_bytes=7 * 2**20),
         cost_estimate=pl.CostEstimate(
             flops=4 * tok * width * part, bytes_accessed=4 * 2**20, transcendentals=0
         ),
@@ -214,25 +210,50 @@
     )(w_all, dcache)
 
 
-def reduce_ring(terms, axis):
+def add_kernel(*refs):
+    total = refs[0][0].astype(F32)
+    for ref in refs[1:-1]:
+        total = total + ref[0].astype(F32)
+    refs[-1][...] = total.astype(refs[-1].dtype).reshape(refs[-1].shape)
+
+
+def add_term(*parts, flops=0, dtype=BF16):
+    shape = parts[0][0].shape[1:]
+
+    def spec(at):
+        return pl.BlockSpec((1,) + shape, lambda i: (at,) + (0,) * len(shape))
+
+    return pl.pallas_call(
+        add_kernel,
+        grid=(1,),
+        out_shape=jax.ShapeDtypeStruct((1,) + shape, dtype),
+        in_specs=[spec(at) for _, at in parts],
+        out_specs=spec(0),
+        compiler_params=pltpu.CompilerParams(vmem_limit_bytes=8 * 2**20),
+        cost_estimate=pl.CostEstimate(flops=flops, bytes_accessed=2**20, transcendentals=0),
+        name="add_term",
+    )(*[array for array, _ in parts])
+
+
+def reduce_groups(n):
+    return [(0, 2, 6), (1, 3), (7, 5), (4,)] if n == 8 else [(0,), (1,)]
+
+
+def reduce_scatter(parts, axis):
     n = lax.axis_size(axis)
-    ahead = [(i, (i + 1) % n) for i in range(n)]
-    back = [(i, (i - 1) % n) for i in range(n)]
-    far = n // 2
-    up = terms[far]
-    for k in range(far - 1, -1, -1):
-        up = lax.ppermute(up, axis, ahead)
-        if k:
-            up = (up.astype(F32) + terms[k].astype(F32)).astype(BF16)
-    total = terms[0].astype(F32) + up.astype(F32)
-    if n - far > 1:
-        down = terms[far + 1]
-        for k in range(far + 2, n):
-            down = lax.ppermute(down, axis, back)
-            down = (down.astype(F32) + terms[k].astype(F32)).astype(BF16)
-        down = lax.ppermute(down, axis, back)
-        total = total + down.astype(F32)
-    return total.astype(BF16)
+
+    def send(x, places):
+        return lax.ppermute(x, axis, [(i, (i + places) % n) for i in range(n)])
+
+    if n == 2:
+        return add_term((parts[0], 0), (send(parts[1], 1), 0))
+    kept, up, down, far = parts
+    up, down, far = lax.optimization_barrier((send(up, 1), send(down, -1), far))
+    far = send(far, 4)
+    up_two = send(add_term((kept, 1), (up, 1)), 2)
+    down_two = send(add_term((kept, 2), (down, 1)), -2)
+    base = add_term((kept, 0), (up, 0), (down, 0), (far, 0), dtype=F32)
+    return add_term((base, 0), (up_two, 0), (down_two, 0), flops=HOP_FLOPS)
 
 
 def per_device(aux_rows, predictors, queries, target, lengths):
@@ -265,11 +286,11 @@
     pos = jnp.arange(tok, dtype=jnp.int32)
     docs = jnp.sum((pos[:, None] >= ends[None, :]).astype(jnp.int32), axis=1)
     me = lax.axis_index("dp").astype(jnp.int32).reshape(1)
-    dw, dcache = attend(me, w_all, r_in, queries[0], target[0], docs)
+    *dw, dcache = attend(me, w_all, r_in, queries[0], target[0], docs, reduce_groups(shards))
 
     r_send = row_terms(w_all, dcache, feats).reshape(peers, rows_each, feats)
     r_back = lax.all_to_all(r_send, both, split_axis=0, concat_axis=0, tiled=True)
-    w_sum = reduce_ring([dw[k] for k in range(shards)], "dp")
+    w_sum = reduce_scatter(dw, "dp")
     w_sum, r_back = lax.optimization_barrier((w_sum, r_back))
     w_back = lax.all_to_all(w_sum.reshape(peers, blk, part), both, split_axis=0, concat_axis=0, tiled=True)
     grad_predictors = (

time: 167 us -> 155 us (0.928)
  starting transfers between devices: 70.7 us -> 64.7 us
  waiting for transfers between devices: 42.8 us -> 37.2 us
    ppermute x7 -> x5, waiting for transfers between devices: 18.7 us -> 14.8 us  [send(): return lax.ppermute(x, axis, [(i, (i + places) % n) for i in range(n)])]
    all_to_all x1, starting transfers between devices: 14.1 us -> 10.3 us  [per_device(): lax.all_to_all(w_sum.reshape(peers, blk, part), both, split_axis=0, conca...]
    ppermute x7 -> x5, starting transfers between devices: 21.9 us -> 18.8 us  [send(): return lax.ppermute(x, axis, [(i, (i + places) % n) for i in range(n)])]
    unnamed x12 -> x14, local copies, waits for them, and re-layouts: 3.5 us -> 4.49 us
    pallas_call x1 -> x5, Pallas kernels: 10.4 us -> 10 us  [the longest x1 7.07 us: attend(): pl.pallas_call(functools.partial(attend_kernel, groups), out_shape=tuple(...]
  transfers between devices with their start and end apart: 11 -> 9, of which waited for: 9 -> 4; matrix products, arithmetic and copies ran while one was open for 2% -> 2% of each run, Pallas kernels for 1% -> 3%
where the time goes in v3:
time: 155 us; the launch traced here: 153 us
  starting transfers between devices  64.7 us (42%)
  waiting for transfers between devices  37.2 us (24%)
  blocking collectives  28 us (18%)
  Pallas kernels  11.8 us (8%)
  other arithmetic  5.8 us (4%)
  local copies, waits for them, and re-layouts  4.62 us (3%)
    all_gather x1, blocking collectives, per_device(): w_all = lax.all_gather(w_in, 'dp', axis=0)  28 us
    ppermute x5, starting transfers between devices, send(): return lax.ppermute(x, axis, [(i, (i + places) % n) for i in range(n)])  18.8 us
    all_to_all x1, starting transfers between devices, per_device(): w_in = lax.all_to_all(w_out, both, split_axis=0, concat_axis=0, tiled=True)  15 us
    ppermute x5, waiting for transfers between devices, send(): return lax.ppermute(x, axis, [(i, (i + places) % n) for i in range(n)])  14.8 us
    all_to_all x1, starting transfers between devices, per_device(): lax.all_to_all(r_send, both, split_axis=0, concat_axis=0, tiled=True)  14.5 us
    all_to_all x1, waiting for transfers between devices, per_device(): w_in = lax.all_to_all(w_out, both, split_axis=0, concat_axis=0, tiled=True)  11.3 us
    all_to_all x1, waiting for transfers between devices, per_device(): lax.all_to_all(w_sum.reshape(peers, blk, part), both, split_axis=0, conca...  11 us
    all_to_all x1, starting transfers between devices, per_device(): lax.all_to_all(w_sum.reshape(peers, blk, part), both, split_axis=0, conca...  10.3 us
  transfers between devices with their start and end apart: 9, of which 4 were waited for; matrix products, arithmetic and copies ran while one was open for 2% of the time, Pallas kernels for 3%

profile of v3, /device:TPU:1, one launch (start us, length us, event | category | flops | bytes accessed | tf_op | source)
XLA Modules:
  0.0 153.0 jit_solution(9778662529043754001)
XLA Ops:
  0.6 1.7 %multiply_convert_fusion.1 = f16[1,32,1,1,8,512]{5,4,3,2,1,0:T(8,128)(2,1)} fusion(bf16[1,32,1,1,8,512]{5,4,3,2,1,0:T(8,128)(2,1)} %param.6), kind=kLoop, calls=%fused_computation.2 | loop fusion | flops 262144 | bytes 524288 | tf_op jit(solution)/shard_map/convert_element_type | solution.py:271
  2.3 0.0 copy-start.6
  2.3 15.0 %all-to-all-start = ((f16[64,8,256]{2,1,0:T(8,128)(2,1)}), f16[64,8,256]{2,1,0:T(8,128)(2,1)S(1)}, u32[]{:S(2)}, u32[]{:S(2)}) async-start(f16[64,8,256]{2,1,0:T(8,128)(2,1)} %bitcast.3), calls=%async_computation | async-start | bytes 524288 | tf_op jit(solution)/shard_map/all_to_all | solution.py:272
  17.3 0.0 copy-start.1
  17.3 1.0 copy-done.1
  18.4 1.1 double.1
  19.4 11.3 %all-to-all-done = f16[64,8,256]{2,1,0:T(8,128)(2,1)S(1)} async-done(((f16[64,8,256]{2,1,0:T(8,128)(2,1)}), f16[64,8,256]{2,1,0:T(8,128)(2,1)S(1)}, u32[]{:S(2)}, u32[]{:S(2)}) %all-to-all-start) | async-done | bytes 262176 | tf_op jit(solution)/shard_map/all_to_all | solution.py:272
  30.7 6.1 %all-to-all-start.1 = ((bf16[64,8,1024]{2,1,0:T(8,128)(2,1)}), bf16[64,8,1024]{2,1,0:T(8,128)(2,1)}, u32[]{:S(2)}, u32[]{:S(2)}) async-start(bf16[64,8,1024]{2,1,0:T(8,128)(2,1)} %bitcast.5), calls=%async_computation.1 | async-start | bytes 2097152 | tf_op jit(solution)/shard_map/all_to_all | solution.py:278
  36.9 0.0 copy-done.6
  36.9 0.2 reduce-window.8
  37.1 0.1 convert_reduce_fusion
  37.1 0.1 copy.9.docc_ref
  37.3 28.0 %all-gather.2 = f16[512,8,256]{2,1,0:T(8,128)(2,1)S(1)} all-gather(f16[64,8,256]{2,1,0:T(8,128)(2,1)S(1)} %all-to-all-done), channel_id=2, replica_groups=mesh['section'=32,'aux'=2,'dp'=8] {'dp'}, dimensions={0}, use_global_device_ids=true | all-gather | bytes 2359296 | tf_op jit(solution)/shard_map/all_gather | solution.py:281
  65.3 0.6 multiply_convert_fusion
  65.9 0.0 all-to-all-done.1
  65.9 0.0 copy-start.2
  65.9 1.2 copy-done.2
  67.1 0.0 copy-start.3
  67.1 1.2 copy-done.3
  68.4 7.1 %attend.1 = (bf16[3,32,16,256]{3,2,1,0:T(8,128)(2,1)S(1)}, bf16[2,32,16,256]{3,2,1,0:T(8,128)(2,1)}, bf16[2,32,16,256]{3,2,1,0:T(8,128)(2,1)}, bf16[1,32,16,256]{3,2,1,0:T(8,128)(2,1)S(1)}, bf16[256,512]{1,0:T(8,128)(2,1)S(1)}) custom-call(s32[1]{0:T(128)} %bitcast.me_ref, bf16[8,32,16,256]{3,2,1,0:T(8,128)(2,1)S(1)} %bitcast.26, ...), custom_call_target="tpu_custom_call" | custom-call | flops 2415919104 | bytes 9437184 | tf_op jit(solution)/shard_map/attend/pallas_call | solution.py:169
  75.4 0.0 copy-start.4
  75.4 2.8 %collective-permute-start = (bf16[2,32,16,256]{3,2,1,0:T(8,128)(2,1)}, bf16[2,32,16,256]{3,2,1,0:T(8,128)(2,1)S(1)}, u32[]{:S(2)}, u32[]{:S(2)}) collective-permute-start(bf16[2,32,16,256]{3,2,1,0:T(8,128)(2,1)} %get-tuple-element.17), channel_id=1, source_target_pairs={{0,1},{1,2},{2,3},{3,4},{4,5},{5,6},{6,7},{7,0},{8,9},{9,10},{10,1... | collective-permute-start | bytes 1572872 | tf_op jit(solution)/shard_map/ppermute | solution.py:246
  78.3 3.8 %collective-permute-start.1 = (bf16[2,32,16,256]{3,2,1,0:T(8,128)(2,1)}, bf16[2,32,16,256]{3,2,1,0:T(8,128)(2,1)}, u32[]{:S(2)}, u32[]{:S(2)}) collective-permute-start(bf16[2,32,16,256]{3,2,1,0:T(8,128)(2,1)} %get-tuple-element.18), channel_id=1, source_target_pairs={{0,7},{1,0},{2,1},{3,2},{4,3},{5,4},{6,5},{7,6},{8,15},{9,8},{10,9... | collective-permute-start | bytes 1572872 | tf_op jit(solution)/shard_map/ppermute | solution.py:246
  82.1 0.7 row_terms.1
  82.8 0.0 copy-done.4
  82.8 0.0 copy-start
  82.8 1.0 copy-done
  83.8 0.0 copy-start.5
  83.8 14.5 %all-to-all-start.2 = ((bf16[64,8,1024]{2,1,0:T(8,128)(2,1)}), bf16[64,8,1024]{2,1,0:T(8,128)(2,1)}, u32[]{:S(2)}, u32[]{:S(2)}) async-start(bf16[64,8,1024]{2,1,0:T(8,128)(2,1)} %bitcast.28), calls=%async_computation.2 | async-start | bytes 2097152 | tf_op jit(solution)/shard_map/all_to_all | solution.py:292
  98.4 0.0 collective-permute-done.refs_1_
  98.4 0.0 collective-permute-done.1.refs_2_.refs_1_
  98.4 0.0 copy-done.5
  98.4 6.0 %collective-permute-start.2 = (bf16[1,32,16,256]{3,2,1,0:T(8,128)(2,1)S(1)}, bf16[1,32,16,256]{3,2,1,0:T(8,128)(2,1)S(1)}, u32[]{:S(2)}, u32[]{:S(2)}) collective-permute-start(bf16[1,32,16,256]{3,2,1,0:T(8,128)(2,1)S(1)} %copy-done.5), channel_id=1, source_target_pairs={{0,4},{1,5},{2,6},{3,7},{4,0},{5,1},{6,2},{7,3},{8,12},{9,13},{10,... | collective-permute-start | bytes 786440 | tf_op jit(solution)/shard_map/ppermute | solution.py:246
  104.4 0.1 add_term.5
  104.5 1.0 add_term.6
  105.5 1.9 %collective-permute-start.4 = (bf16[1,32,16,256]{3,2,1,0:T(8,128)(2,1)S(1)}, bf16[1,32,16,256]{3,2,1,0:T(8,128)(2,1)S(1)}, u32[]{:S(2)}, u32[]{:S(2)}) collective-permute-start(bf16[1,32,16,256]{3,2,1,0:T(8,128)(2,1)S(1)} %add_term.6), channel_id=1, source_target_pairs={{0,6},{1,7},{2,0},{3,1},{4,2},{5,3},{6,4},{7,5},{8,14},{9,15},{10,... | collective-permute-start | bytes 786440 | tf_op jit(solution)/shard_map/ppermute | solution.py:246
  107.5 4.3 %collective-permute-start.3 = (bf16[1,32,16,256]{3,2,1,0:T(8,128)(2,1)S(1)}, bf16[1,32,16,256]{3,2,1,0:T(8,128)(2,1)S(1)}, u32[]{:S(2)}, u32[]{:S(2)}) collective-permute-start(bf16[1,32,16,256]{3,2,1,0:T(8,128)(2,1)S(1)} %add_term.5), channel_id=1, source_target_pairs={{0,2},{1,3},{2,4},{3,5},{4,6},{5,7},{6,0},{7,1},{8,10},{9,11},{10,... | collective-permute-start | bytes 786440 | tf_op jit(solution)/shard_map/ppermute | solution.py:246
  111.7 6.3 %collective-permute-done.2.refs_3_ = bf16[1,32,16,256]{3,2,1,0:T(8,128)(2,1)S(1)} collective-permute-done((bf16[1,32,16,256]{3,2,1,0:T(8,128)(2,1)S(1)}, bf16[1,32,16,256]{3,2,1,0:T(8,128)(2,1)S(1)}, u32[]{:S(2)}, u32[]{:S(2)}) %collective-permute-start.2) | collective-permute-done | bytes 262176 | tf_op jit(solution)/shard_map/ppermute | solution.py:246
  118.0 1.1 add_term.4.refs_0_
  119.1 8.5 %collective-permute-done.4.refs_2_ = bf16[1,32,16,256]{3,2,1,0:T(8,128)(2,1)S(1)} collective-permute-done((bf16[1,32,16,256]{3,2,1,0:T(8,128)(2,1)S(1)}, bf16[1,32,16,256]{3,2,1,0:T(8,128)(2,1)S(1)}, u32[]{:S(2)}, u32[]{:S(2)}) %collective-permute-start.4) | collective-permute-done | bytes 262176 | tf_op jit(solution)/shard_map/ppermute | solution.py:246
  127.6 0.0 collective-permute-done.3.refs_1_
  127.6 0.8 add_term.7
  128.4 0.0 all-to-all-done.2
  128.4 10.3 %all-to-all-start.3 = ((bf16[64,8,256]{2,1,0:T(8,128)(2,1)}), bf16[64,8,256]{2,1,0:T(8,128)(2,1)S(1)}, u32[]{:S(2)}, u32[]{:S(2)}) async-start(bf16[64,8,256]{2,1,0:T(8,128)(2,1)} %bitcast.17), calls=%async_computation.3 | async-start | bytes 524288 | tf_op jit(solution)/shard_map/all_to_all | solution.py:295
  138.7 2.4 %bitcast_reduce_fusion = bf16[32,8,1024]{2,1,0:T(8,128)(2,1)} fusion(bf16[64,8,1024]{2,1,0:T(8,128)(2,1)} %all-to-all-done.2), kind=kLoop, calls=%fused_computation.1 | loop fusion | flops 262144 | bytes 1572864 | tf_op jit(solution)/shard_map/reduce_sum | solution.py:299
  141.1 11.0 %all-to-all-done.3 = bf16[64,8,256]{2,1,0:T(8,128)(2,1)S(1)} async-done(((bf16[64,8,256]{2,1,0:T(8,128)(2,1)}), bf16[64,8,256]{2,1,0:T(8,128)(2,1)S(1)}, u32[]{:S(2)}, u32[]{:S(2)}) %all-to-all-start.3) | async-done | bytes 262176 | tf_op jit(solution)/shard_map/all_to_all | solution.py:295
  152.1 0.9 convert.4
Async XLA Ops:
  2.3 34.5 %copy-start.6 = (s32[1,4]{1,0:T(1,128)S(1)}, s32[1,4]{1,0:T(1,128)}, u32[]{:S(2)}) copy-start(s32[1,4]{1,0:T(1,128)} %param.9) | copy-start | bytes 52
  2.3 28.4 %all-to-all-start = ((f16[64,8,256]{2,1,0:T(8,128)(2,1)}), f16[64,8,256]{2,1,0:T(8,128)(2,1)S(1)}, u32[]{:S(2)}, u32[]{:S(2)}) async-start(f16[64,8,256]{2,1,0:T(8,128)(2,1)} %bitcast.3), calls=%async_computation | async-start | bytes 524288 | tf_op jit(solution)/shard_map/all_to_all | solution.py:272
  17.3 1.0 copy-start.1
  30.7 35.2 %all-to-all-start.1 = ((bf16[64,8,1024]{2,1,0:T(8,128)(2,1)}), bf16[64,8,1024]{2,1,0:T(8,128)(2,1)}, u32[]{:S(2)}, u32[]{:S(2)}) async-start(bf16[64,8,1024]{2,1,0:T(8,128)(2,1)} %bitcast.5), calls=%async_computation.1 | async-start | bytes 2097152 | tf_op jit(solution)/shard_map/all_to_all | solution.py:278
  65.9 1.2 copy-start.2
  67.1 1.2 copy-start.3
  75.4 7.4 %copy-start.4 = (bf16[1,32,16,256]{3,2,1,0:T(8,128)(2,1)}, bf16[1,32,16,256]{3,2,1,0:T(8,128)(2,1)S(1)}, u32[]{:S(2)}) copy-start(bf16[1,32,16,256]{3,2,1,0:T(8,128)(2,1)S(1)} %get-tuple-element.22) | copy-start | bytes 786436
  75.4 22.9 %collective-permute-start = (bf16[2,32,16,256]{3,2,1,0:T(8,128)(2,1)}, bf16[2,32,16,256]{3,2,1,0:T(8,128)(2,1)S(1)}, u32[]{:S(2)}, u32[]{:S(2)}) collective-permute-start(bf16[2,32,16,256]{3,2,1,0:T(8,128)(2,1)} %get-tuple-element.17), channel_id=1, source_target_pairs={{0,1},{1,2},{2,3},{3,4},{4,5},{5,6},{6,7},{7,0},{8,9},{9,10},{10,1... | collective-permute-start | bytes 1572872 | tf_op jit(solution)/shard_map/ppermute | solution.py:246
  78.3 20.1 %collective-permute-start.1 = (bf16[2,32,16,256]{3,2,1,0:T(8,128)(2,1)}, bf16[2,32,16,256]{3,2,1,0:T(8,128)(2,1)}, u32[]{:S(2)}, u32[]{:S(2)}) collective-permute-start(bf16[2,32,16,256]{3,2,1,0:T(8,128)(2,1)} %get-tuple-element.18), channel_id=1, source_target_pairs={{0,7},{1,0},{2,1},{3,2},{4,3},{5,4},{6,5},{7,6},{8,15},{9,8},{10,9... | collective-permute-start | bytes 1572872 | tf_op jit(solution)/shard_map/ppermute | solution.py:246
  82.8 1.0 copy-start
  83.8 14.5 %copy-start.5 = (bf16[1,32,16,256]{3,2,1,0:T(8,128)(2,1)S(1)}, bf16[1,32,16,256]{3,2,1,0:T(8,128)(2,1)}, u32[]{:S(2)}) copy-start(bf16[1,32,16,256]{3,2,1,0:T(8,128)(2,1)} %copy-done.4) | copy-start | bytes 786436
  83.8 44.6 %all-to-all-start.2 = ((bf16[64,8,1024]{2,1,0:T(8,128)(2,1)}), bf16[64,8,1024]{2,1,0:T(8,128)(2,1)}, u32[]{:S(2)}, u32[]{:S(2)}) async-start(bf16[64,8,1024]{2,1,0:T(8,128)(2,1)} %bitcast.28), calls=%async_computation.2 | async-start | bytes 2097152 | tf_op jit(solution)/shard_map/all_to_all | solution.py:292
  98.4 19.6 %collective-permute-start.2 = (bf16[1,32,16,256]{3,2,1,0:T(8,128)(2,1)S(1)}, bf16[1,32,16,256]{3,2,1,0:T(8,128)(2,1)S(1)}, u32[]{:S(2)}, u32[]{:S(2)}) collective-permute-start(bf16[1,32,16,256]{3,2,1,0:T(8,128)(2,1)S(1)} %copy-done.5), channel_id=1, source_target_pairs={{0,4},{1,5},{2,6},{3,7},{4,0},{5,1},{6,2},{7,3},{8,12},{9,13},{10,... | collective-permute-start | bytes 786440 | tf_op jit(solution)/shard_map/ppermute | solution.py:246
  105.5 22.1 %collective-permute-start.4 = (bf16[1,32,16,256]{3,2,1,0:T(8,128)(2,1)S(1)}, bf16[1,32,16,256]{3,2,1,0:T(8,128)(2,1)S(1)}, u32[]{:S(2)}, u32[]{:S(2)}) collective-permute-start(bf16[1,32,16,256]{3,2,1,0:T(8,128)(2,1)S(1)} %add_term.6), channel_id=1, source_target_pairs={{0,6},{1,7},{2,0},{3,1},{4,2},{5,3},{6,4},{7,5},{8,14},{9,15},{10,... | collective-permute-start | bytes 786440 | tf_op jit(solution)/shard_map/ppermute | solution.py:246
  107.5 20.2 %collective-permute-start.3 = (bf16[1,32,16,256]{3,2,1,0:T(8,128)(2,1)S(1)}, bf16[1,32,16,256]{3,2,1,0:T(8,128)(2,1)S(1)}, u32[]{:S(2)}, u32[]{:S(2)}) collective-permute-start(bf16[1,32,16,256]{3,2,1,0:T(8,128)(2,1)S(1)} %add_term.5), channel_id=1, source_target_pairs={{0,2},{1,3},{2,4},{3,5},{4,6},{5,7},{6,0},{7,1},{8,10},{9,11},{10,... | collective-permute-start | bytes 786440 | tf_op jit(solution)/shard_map/ppermute | solution.py:246
  128.4 23.7 %all-to-all-start.3 = ((bf16[64,8,256]{2,1,0:T(8,128)(2,1)}), bf16[64,8,256]{2,1,0:T(8,128)(2,1)S(1)}, u32[]{:S(2)}, u32[]{:S(2)}) async-start(bf16[64,8,256]{2,1,0:T(8,128)(2,1)} %bitcast.17), calls=%async_computation.3 | async-start | bytes 524288 | tf_op jit(solution)/shard_map/all_to_all | solution.py:295

commit v4 on v3

--- a/solution.py
+++ b/solution.py
@@ -36,25 +36,30 @@
         wv_ref[:, pair] = values.astype(BF16)
 
 
-def attend_kernel(groups, me_ref, w_ref, r_ref, q_ref, g_ref, docr_ref, docc_ref, *refs):
-    part_refs, (dc_ref, wk_ref, wv_ref, rows_ref, bias_ref, dw_ref) = refs[:-6], refs[-6:]
+def project_kernel(w_ref, r_ref, cache_ref, rows_ref, wk_ref, wv_ref):
     shards, sections, two_blk, part = w_ref.shape
+    width = sections * shards * two_blk // 2
+    tok = rows_ref.shape[0]
+    feats = r_ref.shape[2]
+    each = tok // sections
+
+    order_weights(w_ref, wk_ref, wv_ref)
+    for a in range(width // feats):
+        piece = r_ref[:, a * each:(a + 1) * each, :].astype(F32)
+        rows_ref[:, a * feats:(a + 1) * feats] = piece.reshape(tok, feats).astype(BF16)
+    rows = rows_ref[...]
+    cache_ref[:, :part] = dot(rows, wk_ref[...].reshape(width, part), NN).astype(BF16)
+    cache_ref[:, part:] = dot(rows, wv_ref[...].reshape(width, part), NN).astype(BF16)
+
+
+def attend_kernel(groups, me_ref, cache_ref, rows_ref, q_ref, g_ref, docr_ref, docc_ref, *refs):
+    part_refs, (dc_ref, bias_ref, dw_ref) = refs[:-3], refs[-3:]
+    shards, sections, two_blk, part = dw_ref.shape
     blk = two_blk // 2
     tok = q_ref.shape[0]
     half = tok // 2
-    feats = r_ref.shape[2]
-    each = tok // sections
-    auxes = r_ref.shape[1] // each
-    width = sections * shards * blk
-
-    order_weights(w_ref, wk_ref, wv_ref)
-    for a in range(auxes):
-        piece = r_ref[:, a * each:(a + 1) * each, :].astype(F32)
-        rows_ref[:, a * feats:(a + 1) * feats] = piece.reshape(tok, feats).astype(BF16)
-
-    rows = rows_ref[...]
-    keys = dot(rows, wk_ref[...].reshape(width, part), NN).astype(BF16)
-    values = dot(rows, wv_ref[...].reshape(width, part), NN).astype(BF16)
+    keys = cache_ref[:, :part]
+    values = cache_ref[:, part:]
 
     j_at = lax.broadcasted_iota(jnp.int32, (tok, tok), 0)
     i_at = lax.broadcasted_iota(jnp.int32, (tok, tok), 1)
@@ -125,16 +130,14 @@
             ref[slot] = dw_ref[k]
 
 
-def rows_kernel(w_ref, dc_ref, out_ref, wk_ref, wv_ref):
-    shards, sections, two_blk, part = w_ref.shape
-    width = sections * shards * two_blk // 2
+def rows_kernel(wk_ref, wv_ref, dc_ref, out_ref):
+    sections, _, _, part = wk_ref.shape
+    width = wk_ref.size // part
     feats = out_ref.shape[2]
-    auxes = width // feats
     each = dc_ref.shape[0] // sections
-    order_weights(w_ref, wk_ref, wv_ref)
     w_k = wk_ref[...].reshape(width, part)
     w_v = wv_ref[...].reshape(width, part)
-    for a in range(auxes):
+    for a in range(width // feats):
         span = slice(a * feats, (a + 1) * feats)
         term = dot(dc_ref[:, :part], w_k[span], NT) + dot(dc_ref[:, part:], w_v[span], NT)
         out_ref[:, a * each:(a + 1) * each, :] = term.reshape(sections, each, feats).astype(BF16)
@@ -161,53 +164,66 @@
     return pl.BlockSpec(memory_space=space)
 
 
-def attend(me, w_all, r_in, queries, goal, docs, groups):
+def project(w_all, r_in):
     shards, sections, two_blk, part = w_all.shape
+    width = sections * shards * two_blk // 2
+    tok = r_in.size // width
+    ordered = jax.ShapeDtypeStruct((sections, shards // 2, two_blk, part), BF16)
+    return pl.pallas_call(
+        project_kernel,
+        out_shape=(
+            jax.ShapeDtypeStruct((tok, 2 * part), BF16),
+            jax.ShapeDtypeStruct((tok, width), BF16),
+            ordered,
+            ordered,
+        ),
+        in_specs=[whole()] * 2,
+        out_specs=(whole(),) * 4,
+        compiler_params=pltpu.CompilerParams(vmem_limit_bytes=12 * 2**20),
+        cost_estimate=pl.CostEstimate(
+            flops=4 * tok * width * part, bytes_accessed=6 * 2**20, transcendentals=0
+        ),
+        name="project",
+    )(w_all, r_in)
+
+
+def attend(me, cache, rows, queries, goal, docs, groups, term):
     tok = queries.shape[0]
-    width = sections * shards * two_blk // 2
-    ordered = (sections, shards // 2, two_blk, part)
     return pl.pallas_call(
         functools.partial(attend_kernel, groups),
-        out_shape=tuple(
-            jax.ShapeDtypeStruct((len(group),) + w_all.shape[1:], BF16) for group in groups
-        )
-        + (jax.ShapeDtypeStruct((tok, 2 * part), BF16),),
+        out_shape=tuple(jax.ShapeDtypeStruct((len(group),) + term, BF16) for group in groups)
+        + (jax.ShapeDtypeStruct(cache.shape, BF16),),
         in_specs=[whole(pltpu.SMEM)] + [whole()] * 6,
         out_specs=(whole(),) * (len(groups) + 1),
         scratch_shapes=[
-            pltpu.VMEM(ordered, BF16),
-            pltpu.VMEM(ordered, BF16),
-            pltpu.VMEM((tok, width), BF16),
             pltpu.VMEM((tok, tok), F32),
-            pltpu.VMEM(w_all.shape, BF16),
+            pltpu.VMEM((sum(len(group) for group in groups),) + term, BF16),
         ],
         compiler_params=pltpu.CompilerParams(vmem_limit_bytes=16 * 2**20),
         cost_estimate=pl.CostEstimate(
-            flops=2 * (2 * tok * width * 2 * part + 5 * tok * tok * queries.shape[1]),
-            bytes_accessed=9 * 2**20,
-            transcendentals=tok * tok * queries.shape[1] // HEAD_DIM,
+            flops=2 * (rows.size * cache.shape[1] + 5 * tok * queries.size),
+            bytes_accessed=6 * 2**20,
+            transcendentals=tok * queries.size // HEAD_DIM,
         ),
         name="attend",
-    )(me, w_all, r_in, queries, goal, docs.reshape(1, tok), docs.reshape(tok, 1))
-
-
-def row_terms(w_all, dcache, feats):
-    shards, sections, two_blk, part = w_all.shape
+    )(me, cache, rows, queries, goal, docs.reshape(1, tok), docs.reshape(tok, 1))
+
+
+def row_terms(w_k, w_v, dcache, feats):
+    sections, _, _, part = w_k.shape
     tok = dcache.shape[0]
-    width = sections * shards * two_blk // 2
-    ordered = (sections, shards // 2, two_blk, part)
+    width = w_k.size // part
     return pl.pallas_call(
         rows_kernel,
         out_shape=jax.ShapeDtypeStruct((sections, tok // sections * (width // feats), feats), BF16),
-        in_specs=[whole()] * 2,
+        in_specs=[whole()] * 3,
         out_specs=whole(),
-        scratch_shapes=[pltpu.VMEM(ordered, BF16), pltpu.VMEM(ordered, BF16)],
-        compiler_params=pltpu.CompilerParams(vmem_limit_bytes=7 * 2**20),
+        compiler_params=pltpu.CompilerParams(vmem_limit_bytes=8 * 2**20),
         cost_estimate=pl.CostEstimate(
             flops=4 * tok * width * part, bytes_accessed=4 * 2**20, transcendentals=0
         ),
         name="row_terms",
-    )(w_all, dcache)
+    )(w_k, w_v, dcache)
 
 
 def add_kernel(*refs):
@@ -248,10 +264,10 @@
     if n == 2:
         return add_term((parts[0], 0), (send(parts[1], 1), 0))
     kept, up, down, far = parts
-    up, down, far = lax.optimization_barrier((send(up, 1), send(down, -1), far))
-    far = send(far, 4)
-    up_two = send(add_term((kept, 1), (up, 1)), 2)
-    down_two = send(add_term((kept, 2), (down, 1)), -2)
+    up, down = send(up, 1), send(down, -1)
+    up_two, down_two = add_term((kept, 1), (up, 1)), add_term((kept, 2), (down, 1))
+    up_two, down_two, far = lax.optimization_barrier((up_two, down_two, far))
+    up_two, down_two, far = send(up_two, 2), send(down_two, -2), send(far, 4)
     base = add_term((kept, 0), (up, 0), (down, 0), (far, 0), dtype=F32)
     return add_term((base, 0), (up_two, 0), (down_two, 0), flops=HOP_FLOPS)
 
@@ -286,9 +302,12 @@
     pos = jnp.arange(tok, dtype=jnp.int32)
     docs = jnp.sum((pos[:, None] >= ends[None, :]).astype(jnp.int32), axis=1)
     me = lax.axis_index("dp").astype(jnp.int32).reshape(1)
-    *dw, dcache = attend(me, w_all, r_in, queries[0], target[0], docs, reduce_groups(shards))
-
-    r_send = row_terms(w_all, dcache, feats).reshape(peers, rows_each, feats)
+    cache, rows, w_k, w_v = project(w_all, r_in)
+    *dw, dcache = attend(
+        me, cache, rows, queries[0], target[0], docs, reduce_groups(shards), w_all.shape[1:]
+    )
+
+    r_send = row_terms(w_k, w_v, dcache, feats).reshape(peers, rows_each, feats)
     r_back = lax.all_to_all(r_send, both, split_axis=0, concat_axis=0, tiled=True)
     w_sum = reduce_scatter(dw, "dp")
     w_sum, r_back = lax.optimization_barrier((w_sum, r_back))

time: 155 us -> 150 us (0.968)
  waiting for transfers between devices: 37.2 us -> 40.4 us
  Pallas kernels: 11.8 us -> 8.98 us
  local copies, waits for them, and re-layouts: 4.62 us -> 1.97 us
    ppermute x5, waiting for transfers between devices: 14.8 us -> 17.7 us  [send(): return lax.ppermute(x, axis, [(i, (i + places) % n) for i in range(n)])]
    pallas_call x1, Pallas kernels: 7.07 us -> 4.4 us  [attend(): pl.pallas_call(functools.partial(attend_kernel, groups), out_shape=tuple(...]
    unnamed x14 -> x8, local copies, waits for them, and re-layouts: 4.49 us -> 1.83 us
    pallas_call x4, Pallas kernels: 2.93 us -> 1.03 us  [add_term(): pl.pallas_call(add_kernel, grid=(1,), out_shape=jax.ShapeDtypeStruct((1,)...]
  transfers between devices with their start and end apart: 9 -> 9, of which waited for: 4 -> 6; matrix products, arithmetic and copies ran while one was open for 2% -> 2% of each run, Pallas kernels for 3% -> 3%
where the time goes in v4:
time: 150 us; the launch traced here: 149 us
  starting transfers between devices  64.1 us (43%)
  waiting for transfers between devices  40.4 us (27%)
  blocking collectives  27.4 us (18%)
  Pallas kernels  8.98 us (6%)
  other arithmetic  5.8 us (4%)
  local copies, waits for them, and re-layouts  1.97 us (1%)
    all_gather x1, blocking collectives, per_device(): w_all = lax.all_gather(w_in, 'dp', axis=0)  27.4 us
    ppermute x5, starting transfers between devices, send(): return lax.ppermute(x, axis, [(i, (i + places) % n) for i in range(n)])  20.2 us
    ppermute x5, waiting for transfers between devices, send(): return lax.ppermute(x, axis, [(i, (i + places) % n) for i in range(n)])  17.7 us
    all_to_all x1, starting transfers between devices, per_device(): w_in = lax.all_to_all(w_out, both, split_axis=0, concat_axis=0, tiled=True)  15 us
    all_to_all x1, starting transfers between devices, per_device(): lax.all_to_all(r_send, both, split_axis=0, concat_axis=0, tiled=True)  13.3 us
    all_to_all x1, waiting for transfers between devices, per_device(): w_in = lax.all_to_all(w_out, both, split_axis=0, concat_axis=0, tiled=True)  11.3 us
    all_to_all x1, waiting for transfers between devices, per_device(): lax.all_to_all(w_sum.reshape(peers, blk, part), both, split_axis=0, conca...  11 us
    all_to_all x1, starting transfers between devices, per_device(): lax.all_to_all(w_sum.reshape(peers, blk, part), both, split_axis=0, conca...  10.4 us
  transfers between devices with their start and end apart: 9, of which 6 were waited for; matrix products, arithmetic and copies ran while one was open for 2% of the time, Pallas kernels for 3%

profile of v4, /device:TPU:1, one launch (start us, length us, event | category | flops | bytes accessed | tf_op | source)
XLA Modules:
  0.0 149.4 jit_solution(11101262158046449494)
XLA Ops:
  0.6 1.7 %multiply_convert_fusion.1 = f16[1,32,1,1,8,512]{5,4,3,2,1,0:T(8,128)(2,1)} fusion(bf16[1,32,1,1,8,512]{5,4,3,2,1,0:T(8,128)(2,1)} %param.6), kind=kLoop, calls=%fused_computation.2 | loop fusion | flops 262144 | bytes 524288 | tf_op jit(solution)/shard_map/convert_element_type | solution.py:287
  2.3 0.0 copy-start.3
  2.3 15.0 %all-to-all-start = ((f16[64,8,256]{2,1,0:T(8,128)(2,1)}), f16[64,8,256]{2,1,0:T(8,128)(2,1)S(1)}, u32[]{:S(2)}, u32[]{:S(2)}) async-start(f16[64,8,256]{2,1,0:T(8,128)(2,1)} %bitcast.3), calls=%async_computation | async-start | bytes 524288 | tf_op jit(solution)/shard_map/all_to_all | solution.py:288
  17.3 0.0 copy-start
  17.3 1.0 copy-done
  18.4 1.0 double.1
  19.4 11.3 %all-to-all-done = f16[64,8,256]{2,1,0:T(8,128)(2,1)S(1)} async-done(((f16[64,8,256]{2,1,0:T(8,128)(2,1)}), f16[64,8,256]{2,1,0:T(8,128)(2,1)S(1)}, u32[]{:S(2)}, u32[]{:S(2)}) %all-to-all-start) | async-done | bytes 262176 | tf_op jit(solution)/shard_map/all_to_all | solution.py:288
  30.7 5.3 %all-to-all-start.1 = ((bf16[64,8,1024]{2,1,0:T(8,128)(2,1)}), bf16[64,8,1024]{2,1,0:T(8,128)(2,1)S(1)}, u32[]{:S(2)}, u32[]{:S(2)}) async-start(bf16[64,8,1024]{2,1,0:T(8,128)(2,1)} %bitcast.5), calls=%async_computation.1 | async-start | bytes 2097152 | tf_op jit(solution)/shard_map/all_to_all | solution.py:294
  36.1 0.0 copy-done.3
  36.1 0.2 reduce-window.8
  36.3 0.1 convert_reduce_fusion
  36.4 0.1 copy.9.docc_ref
  36.5 27.4 %all-gather.2 = f16[512,8,256]{2,1,0:T(8,128)(2,1)S(1)} all-gather(f16[64,8,256]{2,1,0:T(8,128)(2,1)S(1)} %all-to-all-done), channel_id=2, replica_groups=mesh['section'=32,'aux'=2,'dp'=8] {'dp'}, dimensions={0}, use_global_device_ids=true | all-gather | bytes 2359296 | tf_op jit(solution)/shard_map/all_gather | solution.py:297
  63.9 0.6 multiply_convert_fusion
  64.5 0.4 all-to-all-done.1
  64.8 0.0 copy-start.1
  64.8 0.0 copy-start.2
  64.8 0.7 project.1
  65.6 0.5 copy-done.1
  66.0 0.3 copy-done.2
  66.4 4.4 %attend.1 = (bf16[3,32,16,256]{3,2,1,0:T(8,128)(2,1)S(1)}, bf16[2,32,16,256]{3,2,1,0:T(8,128)(2,1)S(1)}, bf16[2,32,16,256]{3,2,1,0:T(8,128)(2,1)S(1)}, bf16[1,32...) custom-call(s32[1]{0:T(128)} %bitcast.me_ref, bf16[256,512]{1,0:T(8,128)(2,1)S(1)} %get-tuple-element.20.cache_ref, ...), custom_call_target="tpu_custom_call" | custom-call | flops 1879048192 | bytes 6291456 | tf_op jit(solution)/shard_map/attend/pallas_call | solution.py:192
  70.8 5.1 %collective-permute-start.1 = (bf16[2,32,16,256]{3,2,1,0:T(8,128)(2,1)S(1)}, bf16[2,32,16,256]{3,2,1,0:T(8,128)(2,1)S(1)}, u32[]{:S(2)}, u32[]{:S(2)}) collective-permute-start(bf16[2,32,16,256]{3,2,1,0:T(8,128)(2,1)S(1)} %get-tuple-element.24), channel_id=1, source_target_pairs={{0,7},{1,0},{2,1},{3,2},{4,3},{5,4},{6,5},{7,6},{8,15},{9,8},{10,9... | collective-permute-start | bytes 1572872 | tf_op jit(solution)/shard_map/ppermute | solution.py:262
  75.9 1.9 %collective-permute-start = (bf16[2,32,16,256]{3,2,1,0:T(8,128)(2,1)S(1)}, bf16[2,32,16,256]{3,2,1,0:T(8,128)(2,1)S(1)}, u32[]{:S(2)}, u32[]{:S(2)}) collective-permute-start(bf16[2,32,16,256]{3,2,1,0:T(8,128)(2,1)S(1)} %get-tuple-element.23), channel_id=1, source_target_pairs={{0,1},{1,2},{2,3},{3,4},{4,5},{5,6},{6,7},{7,0},{8,9},{9,10},{10,1... | collective-permute-start | bytes 1572872 | tf_op jit(solution)/shard_map/ppermute | solution.py:262
  77.8 1.8 %row_terms.1 = bf16[32,16,1024]{2,1,0:T(8,128)(2,1)} custom-call(bf16[32,4,16,256]{3,2,1,0:T(8,128)(2,1)S(1)} %get-tuple-element.29.wk_ref, bf16[32,4,16,256]{3,2,1,0:T(8,128)(2,1)S(1)} %get-tuple-element.30.wv_ref, bf16[256,512]{1,0:T(8,128)(2,1)S(1)} %get-tuple-element.31.dc_ref), custom_call_target="tpu_custom_call" | custom-call | flops 536870912 | bytes 4194304 | tf_op jit(solution)/shard_map/row_terms/pallas_call | solution.py:216
  79.6 13.3 %all-to-all-start.2 = ((bf16[64,8,1024]{2,1,0:T(8,128)(2,1)}), bf16[64,8,1024]{2,1,0:T(8,128)(2,1)}, u32[]{:S(2)}, u32[]{:S(2)}) async-start(bf16[64,8,1024]{2,1,0:T(8,128)(2,1)} %bitcast.14), calls=%async_computation.2 | async-start | bytes 2097152 | tf_op jit(solution)/shard_map/all_to_all | solution.py:311
  92.9 0.0 collective-permute-done.1.refs_1_.refs_2_
  92.9 0.1 add_term.5
  92.9 0.0 collective-permute-done.refs_1_
  92.9 0.1 add_term.4
  93.0 5.7 %collective-permute-start.2 = (bf16[1,32,16,256]{3,2,1,0:T(8,128)(2,1)S(1)}, bf16[1,32,16,256]{3,2,1,0:T(8,128)(2,1)S(1)}, u32[]{:S(2)}, u32[]{:S(2)}) collective-permute-start(bf16[1,32,16,256]{3,2,1,0:T(8,128)(2,1)S(1)} %get-tuple-element.26), channel_id=1, source_target_pairs={{0,4},{1,5},{2,6},{3,7},{4,0},{5,1},{6,2},{7,3},{8,12},{9,13},{10,... | collective-permute-start | bytes 786440 | tf_op jit(solution)/shard_map/ppermute | solution.py:262
  98.8 1.9 %collective-permute-start.3 = (bf16[1,32,16,256]{3,2,1,0:T(8,128)(2,1)S(1)}, bf16[1,32,16,256]{3,2,1,0:T(8,128)(2,1)S(1)}, u32[]{:S(2)}, u32[]{:S(2)}) collective-permute-start(bf16[1,32,16,256]{3,2,1,0:T(8,128)(2,1)S(1)} %add_term.4), channel_id=1, source_target_pairs={{0,2},{1,3},{2,4},{3,5},{4,6},{5,7},{6,0},{7,1},{8,10},{9,11},{10,... | collective-permute-start | bytes 786440 | tf_op jit(solution)/shard_map/ppermute | solution.py:262
  100.7 5.5 %collective-permute-start.4 = (bf16[1,32,16,256]{3,2,1,0:T(8,128)(2,1)S(1)}, bf16[1,32,16,256]{3,2,1,0:T(8,128)(2,1)S(1)}, u32[]{:S(2)}, u32[]{:S(2)}) collective-permute-start(bf16[1,32,16,256]{3,2,1,0:T(8,128)(2,1)S(1)} %add_term.5), channel_id=1, source_target_pairs={{0,6},{1,7},{2,0},{3,1},{4,2},{5,3},{6,4},{7,5},{8,14},{9,15},{10,... | collective-permute-start | bytes 786440 | tf_op jit(solution)/shard_map/ppermute | solution.py:262
  106.2 4.9 %collective-permute-done.2.refs_3_ = bf16[1,32,16,256]{3,2,1,0:T(8,128)(2,1)S(1)} collective-permute-done((bf16[1,32,16,256]{3,2,1,0:T(8,128)(2,1)S(1)}, bf16[1,32,16,256]{3,2,1,0:T(8,128)(2,1)S(1)}, u32[]{:S(2)}, u32[]{:S(2)}) %collective-permute-start.2) | collective-permute-done | bytes 262176 | tf_op jit(solution)/shard_map/ppermute | solution.py:262
  111.1 0.1 add_term.6.refs_0_
  111.2 6.6 %collective-permute-done.3.refs_1_ = bf16[1,32,16,256]{3,2,1,0:T(8,128)(2,1)S(1)} collective-permute-done((bf16[1,32,16,256]{3,2,1,0:T(8,128)(2,1)S(1)}, bf16[1,32,16,256]{3,2,1,0:T(8,128)(2,1)S(1)}, u32[]{:S(2)}, u32[]{:S(2)}) %collective-permute-start.3) | collective-permute-done | bytes 262176 | tf_op jit(solution)/shard_map/ppermute | solution.py:262
  117.8 6.1 %collective-permute-done.4.refs_2_ = bf16[1,32,16,256]{3,2,1,0:T(8,128)(2,1)S(1)} collective-permute-done((bf16[1,32,16,256]{3,2,1,0:T(8,128)(2,1)S(1)}, bf16[1,32,16,256]{3,2,1,0:T(8,128)(2,1)S(1)}, u32[]{:S(2)}, u32[]{:S(2)}) %collective-permute-start.4) | collective-permute-done | bytes 262176 | tf_op jit(solution)/shard_map/ppermute | solution.py:262
  124.0 0.8 add_term.7
  124.8 0.0 all-to-all-done.2
  124.8 10.4 %all-to-all-start.3 = ((bf16[64,8,256]{2,1,0:T(8,128)(2,1)}), bf16[64,8,256]{2,1,0:T(8,128)(2,1)S(1)}, u32[]{:S(2)}, u32[]{:S(2)}) async-start(bf16[64,8,256]{2,1,0:T(8,128)(2,1)} %bitcast.17), calls=%async_computation.3 | async-start | bytes 524288 | tf_op jit(solution)/shard_map/all_to_all | solution.py:314
  135.2 2.4 %bitcast_reduce_fusion = bf16[32,8,1024]{2,1,0:T(8,128)(2,1)} fusion(bf16[64,8,1024]{2,1,0:T(8,128)(2,1)} %all-to-all-done.2), kind=kLoop, calls=%fused_computation.1 | loop fusion | flops 262144 | bytes 1572864 | tf_op jit(solution)/shard_map/reduce_sum | solution.py:318
  137.6 11.0 %all-to-all-done.3 = bf16[64,8,256]{2,1,0:T(8,128)(2,1)S(1)} async-done(((bf16[64,8,256]{2,1,0:T(8,128)(2,1)}), bf16[64,8,256]{2,1,0:T(8,128)(2,1)S(1)}, u32[]{:S(2)}, u32[]{:S(2)}) %all-to-all-start.3) | async-done | bytes 262176 | tf_op jit(solution)/shard_map/all_to_all | solution.py:314
  148.6 0.9 convert.4
Async XLA Ops:
  2.3 33.8 %copy-start.3 = (s32[1,4]{1,0:T(1,128)S(1)}, s32[1,4]{1,0:T(1,128)}, u32[]{:S(2)}) copy-start(s32[1,4]{1,0:T(1,128)} %param.9) | copy-start | bytes 52
  2.3 28.4 %all-to-all-start = ((f16[64,8,256]{2,1,0:T(8,128)(2,1)}), f16[64,8,256]{2,1,0:T(8,128)(2,1)S(1)}, u32[]{:S(2)}, u32[]{:S(2)}) async-start(f16[64,8,256]{2,1,0:T(8,128)(2,1)} %bitcast.3), calls=%async_computation | async-start | bytes 524288 | tf_op jit(solution)/shard_map/all_to_all | solution.py:288
  17.3 1.0 copy-start
  30.7 34.1 %all-to-all-start.1 = ((bf16[64,8,1024]{2,1,0:T(8,128)(2,1)}), bf16[64,8,1024]{2,1,0:T(8,128)(2,1)S(1)}, u32[]{:S(2)}, u32[]{:S(2)}) async-start(bf16[64,8,1024]{2,1,0:T(8,128)(2,1)} %bitcast.5), calls=%async_computation.1 | async-start | bytes 2097152 | tf_op jit(solution)/shard_map/all_to_all | solution.py:294
  64.8 1.2 copy-start.1
  64.8 1.5 %copy-start.2 = (bf16[1,256,2048]{2,1,0:T(8,128)(2,1)S(1)}, bf16[1,256,2048]{2,1,0:T(8,128)(2,1)}, u32[]{:S(2)}) copy-start(bf16[1,256,2048]{2,1,0:T(8,128)(2,1)} %param.8) | copy-start | bytes 3145732
  70.8 22.1 %collective-permute-start.1 = (bf16[2,32,16,256]{3,2,1,0:T(8,128)(2,1)S(1)}, bf16[2,32,16,256]{3,2,1,0:T(8,128)(2,1)S(1)}, u32[]{:S(2)}, u32[]{:S(2)}) collective-permute-start(bf16[2,32,16,256]{3,2,1,0:T(8,128)(2,1)S(1)} %get-tuple-element.24), channel_id=1, source_target_pairs={{0,7},{1,0},{2,1},{3,2},{4,3},{5,4},{6,5},{7,6},{8,15},{9,8},{10,9... | collective-permute-start | bytes 1572872 | tf_op jit(solution)/shard_map/ppermute | solution.py:262
  75.9 17.1 %collective-permute-start = (bf16[2,32,16,256]{3,2,1,0:T(8,128)(2,1)S(1)}, bf16[2,32,16,256]{3,2,1,0:T(8,128)(2,1)S(1)}, u32[]{:S(2)}, u32[]{:S(2)}) collective-permute-start(bf16[2,32,16,256]{3,2,1,0:T(8,128)(2,1)S(1)} %get-tuple-element.23), channel_id=1, source_target_pairs={{0,1},{1,2},{2,3},{3,4},{4,5},{5,6},{6,7},{7,0},{8,9},{9,10},{10,1... | collective-permute-start | bytes 1572872 | tf_op jit(solution)/shard_map/ppermute | solution.py:262
  79.6 45.2 %all-to-all-start.2 = ((bf16[64,8,1024]{2,1,0:T(8,128)(2,1)}), bf16[64,8,1024]{2,1,0:T(8,128)(2,1)}, u32[]{:S(2)}, u32[]{:S(2)}) async-start(bf16[64,8,1024]{2,1,0:T(8,128)(2,1)} %bitcast.14), calls=%async_computation.2 | async-start | bytes 2097152 | tf_op jit(solution)/shard_map/all_to_all | solution.py:311
  93.0 18.1 %collective-permute-start.2 = (bf16[1,32,16,256]{3,2,1,0:T(8,128)(2,1)S(1)}, bf16[1,32,16,256]{3,2,1,0:T(8,128)(2,1)S(1)}, u32[]{:S(2)}, u32[]{:S(2)}) collective-permute-start(bf16[1,32,16,256]{3,2,1,0:T(8,128)(2,1)S(1)} %get-tuple-element.26), channel_id=1, source_target_pairs={{0,4},{1,5},{2,6},{3,7},{4,0},{5,1},{6,2},{7,3},{8,12},{9,13},{10,... | collective-permute-start | bytes 786440 | tf_op jit(solution)/shard_map/ppermute | solution.py:262
  98.8 19.1 %collective-permute-start.3 = (bf16[1,32,16,256]{3,2,1,0:T(8,128)(2,1)S(1)}, bf16[1,32,16,256]{3,2,1,0:T(8,128)(2,1)S(1)}, u32[]{:S(2)}, u32[]{:S(2)}) collective-permute-start(bf16[1,32,16,256]{3,2,1,0:T(8,128)(2,1)S(1)} %add_term.4), channel_id=1, source_target_pairs={{0,2},{1,3},{2,4},{3,5},{4,6},{5,7},{6,0},{7,1},{8,10},{9,11},{10,... | collective-permute-start | bytes 786440 | tf_op jit(solution)/shard_map/ppermute | solution.py:262
  100.7 23.3 %collective-permute-start.4 = (bf16[1,32,16,256]{3,2,1,0:T(8,128)(2,1)S(1)}, bf16[1,32,16,256]{3,2,1,0:T(8,128)(2,1)S(1)}, u32[]{:S(2)}, u32[]{:S(2)}) collective-permute-start(bf16[1,32,16,256]{3,2,1,0:T(8,128)(2,1)S(1)} %add_term.5), channel_id=1, source_target_pairs={{0,6},{1,7},{2,0},{3,1},{4,2},{5,3},{6,4},{7,5},{8,14},{9,15},{10,... | collective-permute-start | bytes 786440 | tf_op jit(solution)/shard_map/ppermute | solution.py:262
  124.8 23.8 %all-to-all-start.3 = ((bf16[64,8,256]{2,1,0:T(8,128)(2,1)}), bf16[64,8,256]{2,1,0:T(8,128)(2,1)S(1)}, u32[]{:S(2)}, u32[]{:S(2)}) async-start(bf16[64,8,256]{2,1,0:T(8,128)(2,1)} %bitcast.17), calls=%async_computation.3 | async-start | bytes 524288 | tf_op jit(solution)/shard_map/all_to_all | solution.py:314

commit v5 on v4

--- a/solution.py
+++ b/solution.py
@@ -44,16 +44,19 @@
     each = tok // sections
 
     order_weights(w_ref, wk_ref, wv_ref)
+    pieces = r_ref[...].astype(F32)
     for a in range(width // feats):
-        piece = r_ref[:, a * each:(a + 1) * each, :].astype(F32)
+        piece = pieces[:, a * each:(a + 1) * each, :]
         rows_ref[:, a * feats:(a + 1) * feats] = piece.reshape(tok, feats).astype(BF16)
     rows = rows_ref[...]
     cache_ref[:, :part] = dot(rows, wk_ref[...].reshape(width, part), NN).astype(BF16)
     cache_ref[:, part:] = dot(rows, wv_ref[...].reshape(width, part), NN).astype(BF16)
 
 
-def attend_kernel(groups, me_ref, cache_ref, rows_ref, q_ref, g_ref, docr_ref, docc_ref, *refs):
-    part_refs, (dc_ref, bias_ref, dw_ref) = refs[:-3], refs[-3:]
+def attend_kernel(
+    groups, me_ref, cache_ref, rows_ref, wk_ref, wv_ref, q_ref, g_ref, docr_ref, docc_ref, *refs
+):
+    part_refs, (out_any, dc_ref, bias_ref, dw_ref, out_ref, sem) = refs[:-6], refs[-6:]
     shards, sections, two_blk, part = dw_ref.shape
     blk = two_blk // 2
     tok = q_ref.shape[0]
@@ -116,8 +119,22 @@
         dc_ref[:, h * HEAD_DIM:(h + 1) * HEAD_DIM] = dk.astype(BF16)
         dc_ref[:, part + h * HEAD_DIM:part + (h + 1) * HEAD_DIM] = dv.astype(BF16)
 
+    dcache = dc_ref[...]
+    width = rows_ref.shape[1]
+    feats = out_ref.shape[2]
+    each = tok // sections
+    w_k = wk_ref[...].reshape(width, part)
+    w_v = wv_ref[...].reshape(width, part)
+    terms = []
+    for a in range(width // feats):
+        span = slice(a * feats, (a + 1) * feats)
+        term = dot(dcache[:, :part], w_k[span], NT) + dot(dcache[:, part:], w_v[span], NT)
+        terms.append(term.reshape(sections, each, feats))
+    out_ref[...] = jnp.concatenate(terms, axis=1).astype(BF16)
+    out_copy = pltpu.make_async_copy(out_ref, out_any, sem)
+    out_copy.start()
+
     me = me_ref[0]
-    dcache = dc_ref[...]
     step_rows = 4 * shards * blk
     for at in range(sections // 4):
         x = rows_ref[:, at * step_rows:(at + 1) * step_rows]
@@ -128,19 +145,7 @@
     for group_at, ref in zip(groups, part_refs):
         for slot, k in enumerate(group_at):
             ref[slot] = dw_ref[k]
-
-
-def rows_kernel(wk_ref, wv_ref, dc_ref, out_ref):
-    sections, _, _, part = wk_ref.shape
-    width = wk_ref.size // part
-    feats = out_ref.shape[2]
-    each = dc_ref.shape[0] // sections
-    w_k = wk_ref[...].reshape(width, part)
-    w_v = wv_ref[...].reshape(width, part)
-    for a in range(width // feats):
-        span = slice(a * feats, (a + 1) * feats)
-        term = dot(dc_ref[:, :part], w_k[span], NT) + dot(dc_ref[:, part:], w_v[span], NT)
-        out_ref[:, a * each:(a + 1) * each, :] = term.reshape(sections, each, feats).astype(BF16)
+    out_copy.wait()
 
 
 def double_kernel(x_ref, out_ref):
@@ -187,43 +192,29 @@
     )(w_all, r_in)
 
 
-def attend(me, cache, rows, queries, goal, docs, groups, term):
+def attend(me, cache, rows, w_k, w_v, queries, goal, docs, groups, term, r_shape):
     tok = queries.shape[0]
     return pl.pallas_call(
         functools.partial(attend_kernel, groups),
         out_shape=tuple(jax.ShapeDtypeStruct((len(group),) + term, BF16) for group in groups)
-        + (jax.ShapeDtypeStruct(cache.shape, BF16),),
-        in_specs=[whole(pltpu.SMEM)] + [whole()] * 6,
-        out_specs=(whole(),) * (len(groups) + 1),
+        + (jax.ShapeDtypeStruct(r_shape, BF16),),
+        in_specs=[whole(pltpu.SMEM)] + [whole()] * 8,
+        out_specs=(whole(),) * len(groups) + (whole(pltpu.HBM),),
         scratch_shapes=[
+            pltpu.VMEM(cache.shape, BF16),
             pltpu.VMEM((tok, tok), F32),
             pltpu.VMEM((sum(len(group) for group in groups),) + term, BF16),
+            pltpu.VMEM(r_shape, BF16),
+            pltpu.SemaphoreType.DMA,
         ],
-        compiler_params=pltpu.CompilerParams(vmem_limit_bytes=16 * 2**20),
+        compiler_params=pltpu.CompilerParams(vmem_limit_bytes=18 * 2**20),
         cost_estimate=pl.CostEstimate(
-            flops=2 * (rows.size * cache.shape[1] + 5 * tok * queries.size),
+            flops=2 * (2 * rows.size * cache.shape[1] + 5 * tok * queries.size),
             bytes_accessed=6 * 2**20,
             transcendentals=tok * queries.size // HEAD_DIM,
         ),
         name="attend",
-    )(me, cache, rows, queries, goal, docs.reshape(1, tok), docs.reshape(tok, 1))
-
-
-def row_terms(w_k, w_v, dcache, feats):
-    sections, _, _, part = w_k.shape
-    tok = dcache.shape[0]
-    width = w_k.size // part
-    return pl.pallas_call(
-        rows_kernel,
-        out_shape=jax.ShapeDtypeStruct((sections, tok // sections * (width // feats), feats), BF16),
-        in_specs=[whole()] * 3,
-        out_specs=whole(),
-        compiler_params=pltpu.CompilerParams(vmem_limit_bytes=8 * 2**20),
-        cost_estimate=pl.CostEstimate(
-            flops=4 * tok * width * part, bytes_accessed=4 * 2**20, transcendentals=0
-        ),
-        name="row_terms",
-    )(w_k, w_v, dcache)
+    )(me, cache, rows, w_k, w_v, queries, goal, docs.reshape(1, tok), docs.reshape(tok, 1))
 
 
 def add_kernel(*refs):
@@ -303,11 +294,12 @@
     docs = jnp.sum((pos[:, None] >= ends[None, :]).astype(jnp.int32), axis=1)
     me = lax.axis_index("dp").astype(jnp.int32).reshape(1)
     cache, rows, w_k, w_v = project(w_all, r_in)
-    *dw, dcache = attend(
-        me, cache, rows, queries[0], target[0], docs, reduce_groups(shards), w_all.shape[1:]
+    *dw, r_send = attend(
+        me, cache, rows, w_k, w_v, queries[0], target[0], docs,
+        reduce_groups(shards), w_all.shape[1:], r_in.shape,
     )
 
-    r_send = row_terms(w_k, w_v, dcache, feats).reshape(peers, rows_each, feats)
+    r_send = r_send.reshape(peers, rows_each, feats)
     r_back = lax.all_to_all(r_send, both, split_axis=0, concat_axis=0, tiled=True)
     w_sum = reduce_scatter(dw, "dp")
     w_sum, r_back = lax.optimization_barrier((w_sum, r_back))

time: 150 us -> 148 us (0.987)
  waiting for transfers between devices: 40.4 us -> 38.3 us
    ppermute x5, waiting for transfers between devices: 17.7 us -> 15.6 us  [send(): return lax.ppermute(x, axis, [(i, (i + places) % n) for i in range(n)])]
    pallas_call x1 -> x0, Pallas kernels: 1.76 us -> none  [row_terms(): pl.pallas_call(rows_kernel, out_shape=jax.ShapeDtypeStruct((sections, tok...]
  transfers between devices with their start and end apart: 9 -> 9, of which waited for: 6 -> 6; matrix products, arithmetic and copies ran while one was open for 2% -> 2% of each run, Pallas kernels for 3% -> 1%
where the time goes in v5:
time: 148 us
  starting transfers between devices  65.3 us (44%)
  waiting for transfers between devices  38.3 us (26%)
  blocking collectives  27.4 us (19%)
  Pallas kernels  7.99 us (5%)
  other arithmetic  5.8 us (4%)
  local copies, waits for them, and re-layouts  1.97 us (1%)
    all_gather x1, blocking collectives, per_device(): w_all = lax.all_gather(w_in, 'dp', axis=0)  27.4 us
    ppermute x5, starting transfers between devices, send(): return lax.ppermute(x, axis, [(i, (i + places) % n) for i in range(n)])  20.2 us
    ppermute x5, waiting for transfers between devices, send(): return lax.ppermute(x, axis, [(i, (i + places) % n) for i in range(n)])  15.6 us
    all_to_all x1, starting transfers between devices, per_device(): w_in = lax.all_to_all(w_out, both, split_axis=0, concat_axis=0, tiled=True)  15 us
    all_to_all x1, starting transfers between devices, per_device(): lax.all_to_all(r_send, both, split_axis=0, concat_axis=0, tiled=True)  14.5 us
    all_to_all x1, waiting for transfers between devices, per_device(): w_in = lax.all_to_all(w_out, both, split_axis=0, concat_axis=0, tiled=True)  11.3 us
    all_to_all x1, waiting for transfers between devices, per_device(): lax.all_to_all(w_sum.reshape(peers, blk, part), both, split_axis=0, conca...  11 us
    all_to_all x1, starting transfers between devices, per_device(): lax.all_to_all(w_sum.reshape(peers, blk, part), both, split_axis=0, conca...  10.3 us
  transfers between devices with their start and end apart: 9, of which 6 were waited for; matrix products, arithmetic and copies ran while one was open for 2% of the time, Pallas kernels for 1%

profile of v5, /device:TPU:1, one launch (start us, length us, event | category | flops | bytes accessed | tf_op | source)
XLA Modules:
  0.0 147.5 jit_solution(15769763617745846287)
XLA Ops:
  0.6 1.7 %multiply_convert_fusion.1 = f16[1,32,1,1,8,512]{5,4,3,2,1,0:T(8,128)(2,1)} fusion(bf16[1,32,1,1,8,512]{5,4,3,2,1,0:T(8,128)(2,1)} %param.6), kind=kLoop, calls=%fused_computation.2 | loop fusion | flops 262144 | bytes 524288 | tf_op jit(solution)/shard_map/convert_element_type | solution.py:278
  2.3 0.0 copy-start.3
  2.3 15.0 %all-to-all-start = ((f16[64,8,256]{2,1,0:T(8,128)(2,1)}), f16[64,8,256]{2,1,0:T(8,128)(2,1)S(1)}, u32[]{:S(2)}, u32[]{:S(2)}) async-start(f16[64,8,256]{2,1,0:T(8,128)(2,1)} %bitcast.3), calls=%async_computation | async-start | bytes 524288 | tf_op jit(solution)/shard_map/all_to_all | solution.py:279
  17.3 0.0 copy-start
  17.3 1.0 copy-done
  18.4 1.0 double.1
  19.4 11.3 %all-to-all-done = f16[64,8,256]{2,1,0:T(8,128)(2,1)S(1)} async-done(((f16[64,8,256]{2,1,0:T(8,128)(2,1)}), f16[64,8,256]{2,1,0:T(8,128)(2,1)S(1)}, u32[]{:S(2)}, u32[]{:S(2)}) %all-to-all-start) | async-done | bytes 262176 | tf_op jit(solution)/shard_map/all_to_all | solution.py:279
  30.7 5.3 %all-to-all-start.1 = ((bf16[64,8,1024]{2,1,0:T(8,128)(2,1)}), bf16[64,8,1024]{2,1,0:T(8,128)(2,1)S(1)}, u32[]{:S(2)}, u32[]{:S(2)}) async-start(bf16[64,8,1024]{2,1,0:T(8,128)(2,1)} %bitcast.5), calls=%async_computation.1 | async-start | bytes 2097152 | tf_op jit(solution)/shard_map/all_to_all | solution.py:285
  36.1 0.0 copy-done.3
  36.1 0.2 reduce-window.8
  36.3 0.1 convert_reduce_fusion
  36.4 0.1 copy.9.docc_ref
  36.5 27.4 %all-gather.2 = f16[512,8,256]{2,1,0:T(8,128)(2,1)S(1)} all-gather(f16[64,8,256]{2,1,0:T(8,128)(2,1)S(1)} %all-to-all-done), channel_id=2, replica_groups=mesh['section'=32,'aux'=2,'dp'=8] {'dp'}, dimensions={0}, use_global_device_ids=true | all-gather | bytes 2359296 | tf_op jit(solution)/shard_map/all_gather | solution.py:288
  63.9 0.6 multiply_convert_fusion
  64.5 0.4 all-to-all-done.1
  64.8 0.0 copy-start.1
  64.8 0.0 copy-start.2
  64.8 0.7 project.1
  65.6 0.5 copy-done.1
  66.0 0.3 copy-done.2
  66.4 5.2 %attend.1 = (bf16[3,32,16,256]{3,2,1,0:T(8,128)(2,1)S(1)}, bf16[2,32,16,256]{3,2,1,0:T(8,128)(2,1)S(1)}, bf16[2,32,16,256]{3,2,1,0:T(8,128)(2,1)S(1)}, bf16[1,32...) custom-call(s32[1]{0:T(128)} %bitcast.me_ref, bf16[256,512]{1,0:T(8,128)(2,1)S(1)} %get-tuple-element.20.cache_ref, ...), custom_call_target="tpu_custom_call" | custom-call | flops 2415919104 | bytes 6291456 | tf_op jit(solution)/shard_map/attend/pallas_call | solution.py:197
  71.5 3.2 %collective-permute-start = (bf16[2,32,16,256]{3,2,1,0:T(8,128)(2,1)S(1)}, bf16[2,32,16,256]{3,2,1,0:T(8,128)(2,1)S(1)}, u32[]{:S(2)}, u32[]{:S(2)}) collective-permute-start(bf16[2,32,16,256]{3,2,1,0:T(8,128)(2,1)S(1)} %get-tuple-element.25), channel_id=1, source_target_pairs={{0,1},{1,2},{2,3},{3,4},{4,5},{5,6},{6,7},{7,0},{8,9},{9,10},{10,1... | collective-permute-start | bytes 1572872 | tf_op jit(solution)/shard_map/ppermute | solution.py:253
  74.8 3.8 %collective-permute-start.1 = (bf16[2,32,16,256]{3,2,1,0:T(8,128)(2,1)S(1)}, bf16[2,32,16,256]{3,2,1,0:T(8,128)(2,1)S(1)}, u32[]{:S(2)}, u32[]{:S(2)}) collective-permute-start(bf16[2,32,16,256]{3,2,1,0:T(8,128)(2,1)S(1)} %get-tuple-element.26), channel_id=1, source_target_pairs={{0,7},{1,0},{2,1},{3,2},{4,3},{5,4},{6,5},{7,6},{8,15},{9,8},{10,9... | collective-permute-start | bytes 1572872 | tf_op jit(solution)/shard_map/ppermute | solution.py:253
  78.6 14.5 %all-to-all-start.2 = ((bf16[64,8,1024]{2,1,0:T(8,128)(2,1)}), bf16[64,8,1024]{2,1,0:T(8,128)(2,1)}, u32[]{:S(2)}, u32[]{:S(2)}) async-start(bf16[64,8,1024]{2,1,0:T(8,128)(2,1)} %bitcast.14), calls=%async_computation.2 | async-start | bytes 2097152 | tf_op jit(solution)/shard_map/all_to_all | solution.py:303
  93.1 0.0 collective-permute-done.refs_1_
  93.1 0.1 add_term.4
  93.2 0.0 collective-permute-done.1.refs_1_.refs_2_
  93.2 0.1 add_term.5
  93.2 5.8 %collective-permute-start.2 = (bf16[1,32,16,256]{3,2,1,0:T(8,128)(2,1)S(1)}, bf16[1,32,16,256]{3,2,1,0:T(8,128)(2,1)S(1)}, u32[]{:S(2)}, u32[]{:S(2)}) collective-permute-start(bf16[1,32,16,256]{3,2,1,0:T(8,128)(2,1)S(1)} %get-tuple-element.28), channel_id=1, source_target_pairs={{0,4},{1,5},{2,6},{3,7},{4,0},{5,1},{6,2},{7,3},{8,12},{9,13},{10,... | collective-permute-start | bytes 786440 | tf_op jit(solution)/shard_map/ppermute | solution.py:253
  99.0 1.9 %collective-permute-start.3 = (bf16[1,32,16,256]{3,2,1,0:T(8,128)(2,1)S(1)}, bf16[1,32,16,256]{3,2,1,0:T(8,128)(2,1)S(1)}, u32[]{:S(2)}, u32[]{:S(2)}) collective-permute-start(bf16[1,32,16,256]{3,2,1,0:T(8,128)(2,1)S(1)} %add_term.4), channel_id=1, source_target_pairs={{0,2},{1,3},{2,4},{3,5},{4,6},{5,7},{6,0},{7,1},{8,10},{9,11},{10,... | collective-permute-start | bytes 786440 | tf_op jit(solution)/shard_map/ppermute | solution.py:253
  100.9 5.5 %collective-permute-start.4 = (bf16[1,32,16,256]{3,2,1,0:T(8,128)(2,1)S(1)}, bf16[1,32,16,256]{3,2,1,0:T(8,128)(2,1)S(1)}, u32[]{:S(2)}, u32[]{:S(2)}) collective-permute-start(bf16[1,32,16,256]{3,2,1,0:T(8,128)(2,1)S(1)} %add_term.5), channel_id=1, source_target_pairs={{0,6},{1,7},{2,0},{3,1},{4,2},{5,3},{6,4},{7,5},{8,14},{9,15},{10,... | collective-permute-start | bytes 786440 | tf_op jit(solution)/shard_map/ppermute | solution.py:253
  106.4 6.3 %collective-permute-done.2.refs_3_ = bf16[1,32,16,256]{3,2,1,0:T(8,128)(2,1)S(1)} collective-permute-done((bf16[1,32,16,256]{3,2,1,0:T(8,128)(2,1)S(1)}, bf16[1,32,16,256]{3,2,1,0:T(8,128)(2,1)S(1)}, u32[]{:S(2)}, u32[]{:S(2)}) %collective-permute-start.2) | collective-permute-done | bytes 262176 | tf_op jit(solution)/shard_map/ppermute | solution.py:253
  112.7 0.1 add_term.6.refs_0_
  112.9 3.7 %collective-permute-done.3.refs_1_ = bf16[1,32,16,256]{3,2,1,0:T(8,128)(2,1)S(1)} collective-permute-done((bf16[1,32,16,256]{3,2,1,0:T(8,128)(2,1)S(1)}, bf16[1,32,16,256]{3,2,1,0:T(8,128)(2,1)S(1)}, u32[]{:S(2)}, u32[]{:S(2)}) %collective-permute-start.3) | collective-permute-done | bytes 262176 | tf_op jit(solution)/shard_map/ppermute | solution.py:253
  116.6 5.5 %collective-permute-done.4.refs_2_ = bf16[1,32,16,256]{3,2,1,0:T(8,128)(2,1)S(1)} collective-permute-done((bf16[1,32,16,256]{3,2,1,0:T(8,128)(2,1)S(1)}, bf16[1,32,16,256]{3,2,1,0:T(8,128)(2,1)S(1)}, u32[]{:S(2)}, u32[]{:S(2)}) %collective-permute-start.4) | collective-permute-done | bytes 262176 | tf_op jit(solution)/shard_map/ppermute | solution.py:253
  122.2 0.8 add_term.7
  122.9 0.0 all-to-all-done.2
  122.9 10.3 %all-to-all-start.3 = ((bf16[64,8,256]{2,1,0:T(8,128)(2,1)}), bf16[64,8,256]{2,1,0:T(8,128)(2,1)S(1)}, u32[]{:S(2)}, u32[]{:S(2)}) async-start(bf16[64,8,256]{2,1,0:T(8,128)(2,1)} %bitcast.17), calls=%async_computation.3 | async-start | bytes 524288 | tf_op jit(solution)/shard_map/all_to_all | solution.py:306
  133.3 2.4 %bitcast_reduce_fusion = bf16[32,8,1024]{2,1,0:T(8,128)(2,1)} fusion(bf16[64,8,1024]{2,1,0:T(8,128)(2,1)} %all-to-all-done.2), kind=kLoop, calls=%fused_computation.1 | loop fusion | flops 262144 | bytes 1572864 | tf_op jit(solution)/shard_map/reduce_sum | solution.py:310
  135.7 11.0 %all-to-all-done.3 = bf16[64,8,256]{2,1,0:T(8,128)(2,1)S(1)} async-done(((bf16[64,8,256]{2,1,0:T(8,128)(2,1)}), bf16[64,8,256]{2,1,0:T(8,128)(2,1)S(1)}, u32[]{:S(2)}, u32[]{:S(2)}) %all-to-all-start.3) | async-done | bytes 262176 | tf_op jit(solution)/shard_map/all_to_all | solution.py:306
  146.7 0.9 convert.4
Async XLA Ops:
  2.3 33.8 %copy-start.3 = (s32[1,4]{1,0:T(1,128)S(1)}, s32[1,4]{1,0:T(1,128)}, u32[]{:S(2)}) copy-start(s32[1,4]{1,0:T(1,128)} %param.9) | copy-start | bytes 52
  2.3 28.4 %all-to-all-start = ((f16[64,8,256]{2,1,0:T(8,128)(2,1)}), f16[64,8,256]{2,1,0:T(8,128)(2,1)S(1)}, u32[]{:S(2)}, u32[]{:S(2)}) async-start(f16[64,8,256]{2,1,0:T(8,128)(2,1)} %bitcast.3), calls=%async_computation | async-start | bytes 524288 | tf_op jit(solution)/shard_map/all_to_all | solution.py:279
  17.3 1.0 copy-start
  30.7 34.1 %all-to-all-start.1 = ((bf16[64,8,1024]{2,1,0:T(8,128)(2,1)}), bf16[64,8,1024]{2,1,0:T(8,128)(2,1)S(1)}, u32[]{:S(2)}, u32[]{:S(2)}) async-start(bf16[64,8,1024]{2,1,0:T(8,128)(2,1)} %bitcast.5), calls=%async_computation.1 | async-start | bytes 2097152 | tf_op jit(solution)/shard_map/all_to_all | solution.py:285
  64.8 1.2 copy-start.1
  64.8 1.5 %copy-start.2 = (bf16[1,256,2048]{2,1,0:T(8,128)(2,1)S(1)}, bf16[1,256,2048]{2,1,0:T(8,128)(2,1)}, u32[]{:S(2)}) copy-start(bf16[1,256,2048]{2,1,0:T(8,128)(2,1)} %param.8) | copy-start | bytes 3145732
  71.5 21.5 %collective-permute-start = (bf16[2,32,16,256]{3,2,1,0:T(8,128)(2,1)S(1)}, bf16[2,32,16,256]{3,2,1,0:T(8,128)(2,1)S(1)}, u32[]{:S(2)}, u32[]{:S(2)}) collective-permute-start(bf16[2,32,16,256]{3,2,1,0:T(8,128)(2,1)S(1)} %get-tuple-element.25), channel_id=1, source_target_pairs={{0,1},{1,2},{2,3},{3,4},{4,5},{5,6},{6,7},{7,0},{8,9},{9,10},{10,1... | collective-permute-start | bytes 1572872 | tf_op jit(solution)/shard_map/ppermute | solution.py:253
  74.8 18.4 %collective-permute-start.1 = (bf16[2,32,16,256]{3,2,1,0:T(8,128)(2,1)S(1)}, bf16[2,32,16,256]{3,2,1,0:T(8,128)(2,1)S(1)}, u32[]{:S(2)}, u32[]{:S(2)}) collective-permute-start(bf16[2,32,16,256]{3,2,1,0:T(8,128)(2,1)S(1)} %get-tuple-element.26), channel_id=1, source_target_pairs={{0,7},{1,0},{2,1},{3,2},{4,3},{5,4},{6,5},{7,6},{8,15},{9,8},{10,9... | collective-permute-start | bytes 1572872 | tf_op jit(solution)/shard_map/ppermute | solution.py:253
  78.6 44.4 %all-to-all-start.2 = ((bf16[64,8,1024]{2,1,0:T(8,128)(2,1)}), bf16[64,8,1024]{2,1,0:T(8,128)(2,1)}, u32[]{:S(2)}, u32[]{:S(2)}) async-start(bf16[64,8,1024]{2,1,0:T(8,128)(2,1)} %bitcast.14), calls=%async_computation.2 | async-start | bytes 2097152 | tf_op jit(solution)/shard_map/all_to_all | solution.py:303
  93.2 19.5 %collective-permute-start.2 = (bf16[1,32,16,256]{3,2,1,0:T(8,128)(2,1)S(1)}, bf16[1,32,16,256]{3,2,1,0:T(8,128)(2,1)S(1)}, u32[]{:S(2)}, u32[]{:S(2)}) collective-permute-start(bf16[1,32,16,256]{3,2,1,0:T(8,128)(2,1)S(1)} %get-tuple-element.28), channel_id=1, source_target_pairs={{0,4},{1,5},{2,6},{3,7},{4,0},{5,1},{6,2},{7,3},{8,12},{9,13},{10,... | collective-permute-start | bytes 786440 | tf_op jit(solution)/shard_map/ppermute | solution.py:253
  99.0 17.6 %collective-permute-start.3 = (bf16[1,32,16,256]{3,2,1,0:T(8,128)(2,1)S(1)}, bf16[1,32,16,256]{3,2,1,0:T(8,128)(2,1)S(1)}, u32[]{:S(2)}, u32[]{:S(2)}) collective-permute-start(bf16[1,32,16,256]{3,2,1,0:T(8,128)(2,1)S(1)} %add_term.4), channel_id=1, source_target_pairs={{0,2},{1,3},{2,4},{3,5},{4,6},{5,7},{6,0},{7,1},{8,10},{9,11},{10,... | collective-permute-start | bytes 786440 | tf_op jit(solution)/shard_map/ppermute | solution.py:253
  100.9 21.2 %collective-permute-start.4 = (bf16[1,32,16,256]{3,2,1,0:T(8,128)(2,1)S(1)}, bf16[1,32,16,256]{3,2,1,0:T(8,128)(2,1)S(1)}, u32[]{:S(2)}, u32[]{:S(2)}) collective-permute-start(bf16[1,32,16,256]{3,2,1,0:T(8,128)(2,1)S(1)} %add_term.5), channel_id=1, source_target_pairs={{0,6},{1,7},{2,0},{3,1},{4,2},{5,3},{6,4},{7,5},{8,14},{9,15},{10,... | collective-permute-start | bytes 786440 | tf_op jit(solution)/shard_map/ppermute | solution.py:253
  122.9 23.7 %all-to-all-start.3 = ((bf16[64,8,256]{2,1,0:T(8,128)(2,1)}), bf16[64,8,256]{2,1,0:T(8,128)(2,1)S(1)}, u32[]{:S(2)}, u32[]{:S(2)}) async-start(bf16[64,8,256]{2,1,0:T(8,128)(2,1)} %bitcast.17), calls=%async_computation.3 | async-start | bytes 524288 | tf_op jit(solution)/shard_map/all_to_all | solution.py:306

commit v6 on v5

--- a/solution.py
+++ b/solution.py
@@ -21,7 +21,6 @@
 
 NN = ((1,), (0,))
 NT = ((1,), (1,))
-TN = ((0,), (0,))
 
 
 def order_weights(w_ref, wk_ref, wv_ref):
@@ -36,7 +35,9 @@
         wv_ref[:, pair] = values.astype(BF16)
 
 
-def project_kernel(w_ref, r_ref, cache_ref, rows_ref, wk_ref, wv_ref):
+def project_kernel(
+    w_ref, r_ref, docr_ref, docc_ref, cache_ref, rowst_ref, wk_ref, wv_ref, bias_ref, rows_ref
+):
     shards, sections, two_blk, part = w_ref.shape
     width = sections * shards * two_blk // 2
     tok = rows_ref.shape[0]
@@ -51,23 +52,24 @@
     rows = rows_ref[...]
     cache_ref[:, :part] = dot(rows, wk_ref[...].reshape(width, part), NN).astype(BF16)
     cache_ref[:, part:] = dot(rows, wv_ref[...].reshape(width, part), NN).astype(BF16)
+    rowst_ref[...] = rows.T
+
+    j_at = lax.broadcasted_iota(jnp.int32, (tok, tok), 0)
+    i_at = lax.broadcasted_iota(jnp.int32, (tok, tok), 1)
+    seen = (docc_ref[...] == docr_ref[...]) & (j_at <= i_at)
+    bias_ref[...] = jnp.where(seen, 0.0, -1e30).astype(F32)
 
 
 def attend_kernel(
-    groups, me_ref, cache_ref, rows_ref, wk_ref, wv_ref, q_ref, g_ref, docr_ref, docc_ref, *refs
+    groups, me_ref, cache_ref, rowst_ref, wk_ref, wv_ref, bias_ref, q_ref, g_ref, *refs
 ):
-    part_refs, (out_any, dc_ref, bias_ref, dw_ref, out_ref, sem) = refs[:-6], refs[-6:]
+    part_refs, (out_any, dc_ref, dw_ref, out_ref, sem) = refs[:-5], refs[-5:]
     shards, sections, two_blk, part = dw_ref.shape
     blk = two_blk // 2
     tok = q_ref.shape[0]
     half = tok // 2
     keys = cache_ref[:, :part]
     values = cache_ref[:, part:]
-
-    j_at = lax.broadcasted_iota(jnp.int32, (tok, tok), 0)
-    i_at = lax.broadcasted_iota(jnp.int32, (tok, tok), 1)
-    seen = (docc_ref[...] == docr_ref[...]) & (j_at <= i_at)
-    bias_ref[...] = jnp.where(seen, 0.0, -1e30).astype(F32)
 
     scale = 1.0 / math.sqrt(HEAD_DIM)
     to_two = scale * math.log2(math.e)
@@ -120,7 +122,7 @@
         dc_ref[:, part + h * HEAD_DIM:part + (h + 1) * HEAD_DIM] = dv.astype(BF16)
 
     dcache = dc_ref[...]
-    width = rows_ref.shape[1]
+    width = rowst_ref.shape[0]
     feats = out_ref.shape[2]
     each = tok // sections
     w_k = wk_ref[...].reshape(width, part)
@@ -137,8 +139,8 @@
     me = me_ref[0]
     step_rows = 4 * shards * blk
     for at in range(sections // 4):
-        x = rows_ref[:, at * step_rows:(at + 1) * step_rows]
-        full = dot(x, dcache, TN).reshape(4, shards, blk, 2 * part)
+        x = rowst_ref[at * step_rows:(at + 1) * step_rows, :]
+        full = dot(x, dcache, NN).reshape(4, shards, blk, 2 * part)
         for d in range(shards):
             both = jnp.concatenate([full[:, d, :, :part], full[:, d, :, part:]], axis=1)
             dw_ref[lax.rem(d + shards - me, shards), at * 4:(at + 1) * 4] = both.astype(BF16)
@@ -169,7 +171,7 @@
     return pl.BlockSpec(memory_space=space)
 
 
-def project(w_all, r_in):
+def project(w_all, r_in, docs):
     shards, sections, two_blk, part = w_all.shape
     width = sections * shards * two_blk // 2
     tok = r_in.size // width
@@ -178,43 +180,44 @@
         project_kernel,
         out_shape=(
             jax.ShapeDtypeStruct((tok, 2 * part), BF16),
-            jax.ShapeDtypeStruct((tok, width), BF16),
+            jax.ShapeDtypeStruct((width, tok), BF16),
             ordered,
             ordered,
+            jax.ShapeDtypeStruct((tok, tok), F32),
         ),
-        in_specs=[whole()] * 2,
-        out_specs=(whole(),) * 4,
+        in_specs=[whole()] * 4,
+        out_specs=(whole(),) * 5,
+        scratch_shapes=[pltpu.VMEM((tok, width), BF16)],
         compiler_params=pltpu.CompilerParams(vmem_limit_bytes=12 * 2**20),
         cost_estimate=pl.CostEstimate(
             flops=4 * tok * width * part, bytes_accessed=6 * 2**20, transcendentals=0
         ),
         name="project",
-    )(w_all, r_in)
-
-
-def attend(me, cache, rows, w_k, w_v, queries, goal, docs, groups, term, r_shape):
+    )(w_all, r_in, docs.reshape(1, tok), docs.reshape(tok, 1))
+
+
+def attend(me, cache, rows_t, w_k, w_v, bias, queries, goal, groups, term, r_shape):
     tok = queries.shape[0]
     return pl.pallas_call(
         functools.partial(attend_kernel, groups),
         out_shape=tuple(jax.ShapeDtypeStruct((len(group),) + term, BF16) for group in groups)
         + (jax.ShapeDtypeStruct(r_shape, BF16),),
-        in_specs=[whole(pltpu.SMEM)] + [whole()] * 8,
+        in_specs=[whole(pltpu.SMEM)] + [whole()] * 7,
         out_specs=(whole(),) * len(groups) + (whole(pltpu.HBM),),
         scratch_shapes=[
             pltpu.VMEM(cache.shape, BF16),
-            pltpu.VMEM((tok, tok), F32),
             pltpu.VMEM((sum(len(group) for group in groups),) + term, BF16),
             pltpu.VMEM(r_shape, BF16),
             pltpu.SemaphoreType.DMA,
         ],
         compiler_params=pltpu.CompilerParams(vmem_limit_bytes=18 * 2**20),
         cost_estimate=pl.CostEstimate(
-            flops=2 * (2 * rows.size * cache.shape[1] + 5 * tok * queries.size),
+            flops=2 * (2 * rows_t.size * cache.shape[1] + 5 * tok * queries.size),
             bytes_accessed=6 * 2**20,
             transcendentals=tok * queries.size // HEAD_DIM,
         ),
         name="attend",
-    )(me, cache, rows, w_k, w_v, queries, goal, docs.reshape(1, tok), docs.reshape(tok, 1))
+    )(me, cache, rows_t, w_k, w_v, bias, queries, goal)
 
 
 def add_kernel(*refs):
@@ -257,7 +260,7 @@
     kept, up, down, far = parts
     up, down = send(up, 1), send(down, -1)
     up_two, down_two = add_term((kept, 1), (up, 1)), add_term((kept, 2), (down, 1))
-    up_two, down_two, far = lax.optimization_barrier((up_two, down_two, far))
+    down_two, far = lax.optimization_barrier((down_two, far))
     up_two, down_two, far = send(up_two, 2), send(down_two, -2), send(far, 4)
     base = add_term((kept, 0), (up, 0), (down, 0), (far, 0), dtype=F32)
     return add_term((base, 0), (up_two, 0), (down_two, 0), flops=HOP_FLOPS)
@@ -293,9 +296,9 @@
     pos = jnp.arange(tok, dtype=jnp.int32)
     docs = jnp.sum((pos[:, None] >= ends[None, :]).astype(jnp.int32), axis=1)
     me = lax.axis_index("dp").astype(jnp.int32).reshape(1)
-    cache, rows, w_k, w_v = project(w_all, r_in)
+    cache, rows_t, w_k, w_v, bias = project(w_all, r_in, docs)
     *dw, r_send = attend(
-        me, cache, rows, w_k, w_v, queries[0], target[0], docs,
+        me, cache, rows_t, w_k, w_v, bias, queries[0], target[0],
         reduce_groups(shards), w_all.shape[1:], r_in.shape,
     )
 

time: 148 us -> 149 us (level)
  waiting for transfers between devices: 38.3 us -> 40.3 us
    ppermute x5, waiting for transfers between devices: 15.6 us -> 17.6 us  [send(): return lax.ppermute(x, axis, [(i, (i + places) % n) for i in range(n)])]
where the time goes in v6:
time: 149 us; the launch traced here: 148 us
  starting transfers between devices  64.2 us (43%)
  waiting for transfers between devices  40.3 us (27%)
  blocking collectives  27.4 us (18%)
  Pallas kernels  8.03 us (5%)
  other arithmetic  5.8 us (4%)
  local copies, waits for them, and re-layouts  1.98 us (1%)
    all_gather x1, blocking collectives, per_device(): w_all = lax.all_gather(w_in, 'dp', axis=0)  27.4 us
    ppermute x5, starting transfers between devices, send(): return lax.ppermute(x, axis, [(i, (i + places) % n) for i in range(n)])  20.2 us
    ppermute x5, waiting for transfers between devices, send(): return lax.ppermute(x, axis, [(i, (i + places) % n) for i in range(n)])  17.6 us
    all_to_all x1, starting transfers between devices, per_device(): w_in = lax.all_to_all(w_out, both, split_axis=0, concat_axis=0, tiled=True)  15 us
    all_to_all x1, starting transfers between devices, per_device(): lax.all_to_all(r_send, both, split_axis=0, concat_axis=0, tiled=True)  13.3 us
    all_to_all x1, waiting for transfers between devices, per_device(): w_in = lax.all_to_all(w_out, both, split_axis=0, concat_axis=0, tiled=True)  11.3 us
    all_to_all x1, waiting for transfers between devices, per_device(): lax.all_to_all(w_sum.reshape(peers, blk, part), both, split_axis=0, conca...  11 us
    all_to_all x1, starting transfers between devices, per_device(): lax.all_to_all(w_sum.reshape(peers, blk, part), both, split_axis=0, conca...  10.4 us
  transfers between devices with their start and end apart: 9, of which 6 were waited for; matrix products, arithmetic and copies ran while one was open for 2% of the time, Pallas kernels for 1%

profile of v6, /device:TPU:1, one launch (start us, length us, event | category | flops | bytes accessed | tf_op | source)
XLA Modules:
  0.0 148.4 jit_solution(1157984988764969900)
XLA Ops:
  0.6 1.7 %multiply_convert_fusion.1 = f16[1,32,1,1,8,512]{5,4,3,2,1,0:T(8,128)(2,1)} fusion(bf16[1,32,1,1,8,512]{5,4,3,2,1,0:T(8,128)(2,1)} %param.6), kind=kLoop, calls=%fused_computation.2 | loop fusion | flops 262144 | bytes 524288 | tf_op jit(solution)/shard_map/convert_element_type | solution.py:281
  2.3 0.0 copy-start.3
  2.3 15.0 %all-to-all-start = ((f16[64,8,256]{2,1,0:T(8,128)(2,1)}), f16[64,8,256]{2,1,0:T(8,128)(2,1)S(1)}, u32[]{:S(2)}, u32[]{:S(2)}) async-start(f16[64,8,256]{2,1,0:T(8,128)(2,1)} %bitcast.3), calls=%async_computation | async-start | bytes 524288 | tf_op jit(solution)/shard_map/all_to_all | solution.py:282
  17.3 0.0 copy-start
  17.3 1.0 copy-done
  18.4 1.0 double.1
  19.4 11.3 %all-to-all-done = f16[64,8,256]{2,1,0:T(8,128)(2,1)S(1)} async-done(((f16[64,8,256]{2,1,0:T(8,128)(2,1)}), f16[64,8,256]{2,1,0:T(8,128)(2,1)S(1)}, u32[]{:S(2)}, u32[]{:S(2)}) %all-to-all-start) | async-done | bytes 262176 | tf_op jit(solution)/shard_map/all_to_all | solution.py:282
  30.7 5.3 %all-to-all-start.1 = ((bf16[64,8,1024]{2,1,0:T(8,128)(2,1)}), bf16[64,8,1024]{2,1,0:T(8,128)(2,1)S(1)}, u32[]{:S(2)}, u32[]{:S(2)}) async-start(bf16[64,8,1024]{2,1,0:T(8,128)(2,1)} %bitcast.5), calls=%async_computation.1 | async-start | bytes 2097152 | tf_op jit(solution)/shard_map/all_to_all | solution.py:288
  36.1 0.0 copy-done.3
  36.1 0.2 reduce-window.8
  36.3 0.1 convert_reduce_fusion
  36.4 0.1 copy.9.docc_ref
  36.5 27.4 %all-gather.2 = f16[512,8,256]{2,1,0:T(8,128)(2,1)S(1)} all-gather(f16[64,8,256]{2,1,0:T(8,128)(2,1)S(1)} %all-to-all-done), channel_id=2, replica_groups=mesh['section'=32,'aux'=2,'dp'=8] {'dp'}, dimensions={0}, use_global_device_ids=true | all-gather | bytes 2359296 | tf_op jit(solution)/shard_map/all_gather | solution.py:291
  63.9 0.6 multiply_convert_fusion
  64.5 0.4 all-to-all-done.1
  64.8 0.0 copy-start.1
  64.8 0.0 copy-start.2
  64.8 0.7 project.1
  65.6 0.5 copy-done.1
  66.0 0.3 copy-done.2
  66.4 5.2 %attend.1 = (bf16[3,32,16,256]{3,2,1,0:T(8,128)(2,1)S(1)}, bf16[2,32,16,256]{3,2,1,0:T(8,128)(2,1)S(1)}, bf16[2,32,16,256]{3,2,1,0:T(8,128)(2,1)S(1)}, bf16[1,32...) custom-call(s32[1]{0:T(128)} %bitcast.me_ref, bf16[256,512]{1,0:T(8,128)(2,1)S(1)} %get-tuple-element.20.cache_ref, ...), custom_call_target="tpu_custom_call" | custom-call | flops 2415919104 | bytes 6291456 | tf_op jit(solution)/shard_map/attend/pallas_call | solution.py:201
  71.6 5.1 %collective-permute-start.1 = (bf16[2,32,16,256]{3,2,1,0:T(8,128)(2,1)S(1)}, bf16[2,32,16,256]{3,2,1,0:T(8,128)(2,1)S(1)}, u32[]{:S(2)}, u32[]{:S(2)}) collective-permute-start(bf16[2,32,16,256]{3,2,1,0:T(8,128)(2,1)S(1)} %get-tuple-element.27), channel_id=1, source_target_pairs={{0,7},{1,0},{2,1},{3,2},{4,3},{5,4},{6,5},{7,6},{8,15},{9,8},{10,9... | collective-permute-start | bytes 1572872 | tf_op jit(solution)/shard_map/ppermute | solution.py:256
  76.7 1.9 %collective-permute-start = (bf16[2,32,16,256]{3,2,1,0:T(8,128)(2,1)S(1)}, bf16[2,32,16,256]{3,2,1,0:T(8,128)(2,1)S(1)}, u32[]{:S(2)}, u32[]{:S(2)}) collective-permute-start(bf16[2,32,16,256]{3,2,1,0:T(8,128)(2,1)S(1)} %get-tuple-element.26), channel_id=1, source_target_pairs={{0,1},{1,2},{2,3},{3,4},{4,5},{5,6},{6,7},{7,0},{8,9},{9,10},{10,1... | collective-permute-start | bytes 1572872 | tf_op jit(solution)/shard_map/ppermute | solution.py:256
  78.6 13.3 %all-to-all-start.2 = ((bf16[64,8,1024]{2,1,0:T(8,128)(2,1)}), bf16[64,8,1024]{2,1,0:T(8,128)(2,1)}, u32[]{:S(2)}, u32[]{:S(2)}) async-start(bf16[64,8,1024]{2,1,0:T(8,128)(2,1)} %bitcast.14), calls=%async_computation.2 | async-start | bytes 2097152 | tf_op jit(solution)/shard_map/all_to_all | solution.py:306
  91.9 0.0 collective-permute-done.1.refs_1_.refs_2_
  91.9 0.1 add_term.4
  92.0 5.8 %collective-permute-start.2 = (bf16[1,32,16,256]{3,2,1,0:T(8,128)(2,1)S(1)}, bf16[1,32,16,256]{3,2,1,0:T(8,128)(2,1)S(1)}, u32[]{:S(2)}, u32[]{:S(2)}) collective-permute-start(bf16[1,32,16,256]{3,2,1,0:T(8,128)(2,1)S(1)} %get-tuple-element.29), channel_id=1, source_target_pairs={{0,4},{1,5},{2,6},{3,7},{4,0},{5,1},{6,2},{7,3},{8,12},{9,13},{10,... | collective-permute-start | bytes 786440 | tf_op jit(solution)/shard_map/ppermute | solution.py:256
  97.8 0.0 collective-permute-done.refs_1_
  97.8 0.1 add_term.6
  97.9 1.9 %collective-permute-start.3 = (bf16[1,32,16,256]{3,2,1,0:T(8,128)(2,1)S(1)}, bf16[1,32,16,256]{3,2,1,0:T(8,128)(2,1)S(1)}, u32[]{:S(2)}, u32[]{:S(2)}) collective-permute-start(bf16[1,32,16,256]{3,2,1,0:T(8,128)(2,1)S(1)} %add_term.6), channel_id=1, source_target_pairs={{0,2},{1,3},{2,4},{3,5},{4,6},{5,7},{6,0},{7,1},{8,10},{9,11},{10,... | collective-permute-start | bytes 786440 | tf_op jit(solution)/shard_map/ppermute | solution.py:256
  99.8 5.5 %collective-permute-start.4 = (bf16[1,32,16,256]{3,2,1,0:T(8,128)(2,1)S(1)}, bf16[1,32,16,256]{3,2,1,0:T(8,128)(2,1)S(1)}, u32[]{:S(2)}, u32[]{:S(2)}) collective-permute-start(bf16[1,32,16,256]{3,2,1,0:T(8,128)(2,1)S(1)} %add_term.4), channel_id=1, source_target_pairs={{0,6},{1,7},{2,0},{3,1},{4,2},{5,3},{6,4},{7,5},{8,14},{9,15},{10,... | collective-permute-start | bytes 786440 | tf_op jit(solution)/shard_map/ppermute | solution.py:256
  105.3 4.8 %collective-permute-done.2.refs_3_ = bf16[1,32,16,256]{3,2,1,0:T(8,128)(2,1)S(1)} collective-permute-done((bf16[1,32,16,256]{3,2,1,0:T(8,128)(2,1)S(1)}, bf16[1,32,16,256]{3,2,1,0:T(8,128)(2,1)S(1)}, u32[]{:S(2)}, u32[]{:S(2)}) %collective-permute-start.2) | collective-permute-done | bytes 262176 | tf_op jit(solution)/shard_map/ppermute | solution.py:256
  110.1 0.1 add_term.5.refs_0_
  110.2 6.6 %collective-permute-done.3.refs_1_ = bf16[1,32,16,256]{3,2,1,0:T(8,128)(2,1)S(1)} collective-permute-done((bf16[1,32,16,256]{3,2,1,0:T(8,128)(2,1)S(1)}, bf16[1,32,16,256]{3,2,1,0:T(8,128)(2,1)S(1)}, u32[]{:S(2)}, u32[]{:S(2)}) %collective-permute-start.3) | collective-permute-done | bytes 262176 | tf_op jit(solution)/shard_map/ppermute | solution.py:256
  116.9 6.1 %collective-permute-done.4.refs_2_ = bf16[1,32,16,256]{3,2,1,0:T(8,128)(2,1)S(1)} collective-permute-done((bf16[1,32,16,256]{3,2,1,0:T(8,128)(2,1)S(1)}, bf16[1,32,16,256]{3,2,1,0:T(8,128)(2,1)S(1)}, u32[]{:S(2)}, u32[]{:S(2)}) %collective-permute-start.4) | collective-permute-done | bytes 262176 | tf_op jit(solution)/shard_map/ppermute | solution.py:256
  123.0 0.8 add_term.7
  123.8 0.0 all-to-all-done.2
  123.8 10.4 %all-to-all-start.3 = ((bf16[64,8,256]{2,1,0:T(8,128)(2,1)}), bf16[64,8,256]{2,1,0:T(8,128)(2,1)S(1)}, u32[]{:S(2)}, u32[]{:S(2)}) async-start(bf16[64,8,256]{2,1,0:T(8,128)(2,1)} %bitcast.17), calls=%async_computation.3 | async-start | bytes 524288 | tf_op jit(solution)/shard_map/all_to_all | solution.py:309
  134.2 2.4 %bitcast_reduce_fusion = bf16[32,8,1024]{2,1,0:T(8,128)(2,1)} fusion(bf16[64,8,1024]{2,1,0:T(8,128)(2,1)} %all-to-all-done.2), kind=kLoop, calls=%fused_computation.1 | loop fusion | flops 262144 | bytes 1572864 | tf_op jit(solution)/shard_map/reduce_sum | solution.py:313
  136.6 11.0 %all-to-all-done.3 = bf16[64,8,256]{2,1,0:T(8,128)(2,1)S(1)} async-done(((bf16[64,8,256]{2,1,0:T(8,128)(2,1)}), bf16[64,8,256]{2,1,0:T(8,128)(2,1)S(1)}, u32[]{:S(2)}, u32[]{:S(2)}) %all-to-all-start.3) | async-done | bytes 262176 | tf_op jit(solution)/shard_map/all_to_all | solution.py:309
  147.6 0.9 convert.4
Async XLA Ops:
  2.3 33.8 %copy-start.3 = (s32[1,4]{1,0:T(1,128)S(1)}, s32[1,4]{1,0:T(1,128)}, u32[]{:S(2)}) copy-start(s32[1,4]{1,0:T(1,128)} %param.9) | copy-start | bytes 52
  2.3 28.4 %all-to-all-start = ((f16[64,8,256]{2,1,0:T(8,128)(2,1)}), f16[64,8,256]{2,1,0:T(8,128)(2,1)S(1)}, u32[]{:S(2)}, u32[]{:S(2)}) async-start(f16[64,8,256]{2,1,0:T(8,128)(2,1)} %bitcast.3), calls=%async_computation | async-start | bytes 524288 | tf_op jit(solution)/shard_map/all_to_all | solution.py:282
  17.3 1.0 copy-start
  30.7 34.1 %all-to-all-start.1 = ((bf16[64,8,1024]{2,1,0:T(8,128)(2,1)}), bf16[64,8,1024]{2,1,0:T(8,128)(2,1)S(1)}, u32[]{:S(2)}, u32[]{:S(2)}) async-start(bf16[64,8,1024]{2,1,0:T(8,128)(2,1)} %bitcast.5), calls=%async_computation.1 | async-start | bytes 2097152 | tf_op jit(solution)/shard_map/all_to_all | solution.py:288
  64.8 1.2 copy-start.1
  64.8 1.5 %copy-start.2 = (bf16[1,256,2048]{2,1,0:T(8,128)(2,1)S(1)}, bf16[1,256,2048]{2,1,0:T(8,128)(2,1)}, u32[]{:S(2)}) copy-start(bf16[1,256,2048]{2,1,0:T(8,128)(2,1)} %param.8) | copy-start | bytes 3145732
  71.6 20.3 %collective-permute-start.1 = (bf16[2,32,16,256]{3,2,1,0:T(8,128)(2,1)S(1)}, bf16[2,32,16,256]{3,2,1,0:T(8,128)(2,1)S(1)}, u32[]{:S(2)}, u32[]{:S(2)}) collective-permute-start(bf16[2,32,16,256]{3,2,1,0:T(8,128)(2,1)S(1)} %get-tuple-element.27), channel_id=1, source_target_pairs={{0,7},{1,0},{2,1},{3,2},{4,3},{5,4},{6,5},{7,6},{8,15},{9,8},{10,9... | collective-permute-start | bytes 1572872 | tf_op jit(solution)/shard_map/ppermute | solution.py:256
  76.7 21.1 %collective-permute-start = (bf16[2,32,16,256]{3,2,1,0:T(8,128)(2,1)S(1)}, bf16[2,32,16,256]{3,2,1,0:T(8,128)(2,1)S(1)}, u32[]{:S(2)}, u32[]{:S(2)}) collective-permute-start(bf16[2,32,16,256]{3,2,1,0:T(8,128)(2,1)S(1)} %get-tuple-element.26), channel_id=1, source_target_pairs={{0,1},{1,2},{2,3},{3,4},{4,5},{5,6},{6,7},{7,0},{8,9},{9,10},{10,1... | collective-permute-start | bytes 1572872 | tf_op jit(solution)/shard_map/ppermute | solution.py:256
  78.6 45.1 %all-to-all-start.2 = ((bf16[64,8,1024]{2,1,0:T(8,128)(2,1)}), bf16[64,8,1024]{2,1,0:T(8,128)(2,1)}, u32[]{:S(2)}, u32[]{:S(2)}) async-start(bf16[64,8,1024]{2,1,0:T(8,128)(2,1)} %bitcast.14), calls=%async_computation.2 | async-start | bytes 2097152 | tf_op jit(solution)/shard_map/all_to_all | solution.py:306
  92.0 18.1 %collective-permute-start.2 = (bf16[1,32,16,256]{3,2,1,0:T(8,128)(2,1)S(1)}, bf16[1,32,16,256]{3,2,1,0:T(8,128)(2,1)S(1)}, u32[]{:S(2)}, u32[]{:S(2)}) collective-permute-start(bf16[1,32,16,256]{3,2,1,0:T(8,128)(2,1)S(1)} %get-tuple-element.29), channel_id=1, source_target_pairs={{0,4},{1,5},{2,6},{3,7},{4,0},{5,1},{6,2},{7,3},{8,12},{9,13},{10,... | collective-permute-start | bytes 786440 | tf_op jit(solution)/shard_map/ppermute | solution.py:256
  97.9 19.0 %collective-permute-start.3 = (bf16[1,32,16,256]{3,2,1,0:T(8,128)(2,1)S(1)}, bf16[1,32,16,256]{3,2,1,0:T(8,128)(2,1)S(1)}, u32[]{:S(2)}, u32[]{:S(2)}) collective-permute-start(bf16[1,32,16,256]{3,2,1,0:T(8,128)(2,1)S(1)} %add_term.6), channel_id=1, source_target_pairs={{0,2},{1,3},{2,4},{3,5},{4,6},{5,7},{6,0},{7,1},{8,10},{9,11},{10,... | collective-permute-start | bytes 786440 | tf_op jit(solution)/shard_map/ppermute | solution.py:256
  99.8 23.2 %collective-permute-start.4 = (bf16[1,32,16,256]{3,2,1,0:T(8,128)(2,1)S(1)}, bf16[1,32,16,256]{3,2,1,0:T(8,128)(2,1)S(1)}, u32[]{:S(2)}, u32[]{:S(2)}) collective-permute-start(bf16[1,32,16,256]{3,2,1,0:T(8,128)(2,1)S(1)} %add_term.4), channel_id=1, source_target_pairs={{0,6},{1,7},{2,0},{3,1},{4,2},{5,3},{6,4},{7,5},{8,14},{9,15},{10,... | collective-permute-start | bytes 786440 | tf_op jit(solution)/shard_map/ppermute | solution.py:256
  123.8 23.8 %all-to-all-start.3 = ((bf16[64,8,256]{2,1,0:T(8,128)(2,1)}), bf16[64,8,256]{2,1,0:T(8,128)(2,1)S(1)}, u32[]{:S(2)}, u32[]{:S(2)}) async-start(bf16[64,8,256]{2,1,0:T(8,128)(2,1)} %bitcast.17), calls=%async_computation.3 | async-start | bytes 524288 | tf_op jit(solution)/shard_map/all_to_all | solution.py:309

commit v7 on v5

--- a/solution.py
+++ b/solution.py
@@ -12,7 +12,7 @@
 F32 = jnp.float32
 BF16 = jnp.bfloat16
 W_SCALE = 2.0**18
-HOP_FLOPS = 16 * 10**9
+HOP_FLOPS = 17 * 10**9
 
 
 def dot(a, b, dims):
@@ -255,10 +255,9 @@
     if n == 2:
         return add_term((parts[0], 0), (send(parts[1], 1), 0))
     kept, up, down, far = parts
-    up, down = send(up, 1), send(down, -1)
-    up_two, down_two = add_term((kept, 1), (up, 1)), add_term((kept, 2), (down, 1))
-    up_two, down_two, far = lax.optimization_barrier((up_two, down_two, far))
-    up_two, down_two, far = send(up_two, 2), send(down_two, -2), send(far, 4)
+    up, down, far = lax.optimization_barrier((send(up, 1), send(down, -1), send(far, 4)))
+    up_two = send(add_term((kept, 1), (up, 1)), 2)
+    down_two = send(add_term((kept, 2), (down, 1)), -2)
     base = add_term((kept, 0), (up, 0), (down, 0), (far, 0), dtype=F32)
     return add_term((base, 0), (up_two, 0), (down_two, 0), flops=HOP_FLOPS)
 

time: 148 us -> 149 us (level)
  waiting for transfers between devices: 38.3 us -> 42.9 us
  starting transfers between devices: 65.3 us -> 61.4 us
    all_to_all x1, waiting for transfers between devices: 0.01 us -> 13 us  [per_device(): lax.all_to_all(r_send, both, split_axis=0, concat_axis=0, tiled=True)]
    ppermute x5, waiting for transfers between devices: 15.6 us -> 7.09 us  [send(): return lax.ppermute(x, axis, [(i, (i + places) % n) for i in range(n)])]
    all_to_all x1, starting transfers between devices: 10.3 us -> 6.13 us  [per_device(): lax.all_to_all(w_sum.reshape(peers, blk, part), both, split_axis=0, conca...]
where the time goes in v7:
time: 149 us; the launch traced here: 148 us
  starting transfers between devices  61.4 us (41%)
  waiting for transfers between devices  42.9 us (29%)
  blocking collectives  27.4 us (18%)
  Pallas kernels  7.99 us (5%)
  other arithmetic  5.8 us (4%)
  local copies, waits for them, and re-layouts  1.97 us (1%)
    all_gather x1, blocking collectives, per_device(): w_all = lax.all_gather(w_in, 'dp', axis=0)  27.4 us
    ppermute x5, starting transfers between devices, send(): return lax.ppermute(x, axis, [(i, (i + places) % n) for i in range(n)])  21.3 us
    all_to_all x1, starting transfers between devices, per_device(): w_in = lax.all_to_all(w_out, both, split_axis=0, concat_axis=0, tiled=True)  15 us
    all_to_all x1, starting transfers between devices, per_device(): lax.all_to_all(r_send, both, split_axis=0, concat_axis=0, tiled=True)  13.6 us
    all_to_all x1, waiting for transfers between devices, per_device(): lax.all_to_all(r_send, both, split_axis=0, concat_axis=0, tiled=True)  13 us
    all_to_all x1, waiting for transfers between devices, per_device(): w_in = lax.all_to_all(w_out, both, split_axis=0, concat_axis=0, tiled=True)  11.3 us
    all_to_all x1, waiting for transfers between devices, per_device(): lax.all_to_all(w_sum.reshape(peers, blk, part), both, split_axis=0, conca...  11.1 us
    ppermute x5, waiting for transfers between devices, send(): return lax.ppermute(x, axis, [(i, (i + places) % n) for i in range(n)])  7.09 us
  transfers between devices with their start and end apart: 9, of which 6 were waited for; matrix products, arithmetic and copies ran while one was open for 2% of the time, Pallas kernels for 1%

profile of v7, /device:TPU:1, one launch (start us, length us, event | category | flops | bytes accessed | tf_op | source)
XLA Modules:
  0.0 148.2 jit_solution(3531008502117160506)
XLA Ops:
  0.6 1.7 %multiply_convert_fusion.1 = f16[1,32,1,1,8,512]{5,4,3,2,1,0:T(8,128)(2,1)} fusion(bf16[1,32,1,1,8,512]{5,4,3,2,1,0:T(8,128)(2,1)} %param.6), kind=kLoop, calls=%fused_computation.2 | loop fusion | flops 262144 | bytes 524288 | tf_op jit(solution)/shard_map/convert_element_type | solution.py:277
  2.3 0.0 copy-start.3
  2.3 15.0 %all-to-all-start = ((f16[64,8,256]{2,1,0:T(8,128)(2,1)}), f16[64,8,256]{2,1,0:T(8,128)(2,1)S(1)}, u32[]{:S(2)}, u32[]{:S(2)}) async-start(f16[64,8,256]{2,1,0:T(8,128)(2,1)} %bitcast.3), calls=%async_computation | async-start | bytes 524288 | tf_op jit(solution)/shard_map/all_to_all | solution.py:278
  17.3 0.0 copy-start
  17.3 1.0 copy-done
  18.4 1.0 double.1
  19.4 11.3 %all-to-all-done = f16[64,8,256]{2,1,0:T(8,128)(2,1)S(1)} async-done(((f16[64,8,256]{2,1,0:T(8,128)(2,1)}), f16[64,8,256]{2,1,0:T(8,128)(2,1)S(1)}, u32[]{:S(2)}, u32[]{:S(2)}) %all-to-all-start) | async-done | bytes 262176 | tf_op jit(solution)/shard_map/all_to_all | solution.py:278
  30.7 5.3 %all-to-all-start.1 = ((bf16[64,8,1024]{2,1,0:T(8,128)(2,1)}), bf16[64,8,1024]{2,1,0:T(8,128)(2,1)S(1)}, u32[]{:S(2)}, u32[]{:S(2)}) async-start(bf16[64,8,1024]{2,1,0:T(8,128)(2,1)} %bitcast.5), calls=%async_computation.1 | async-start | bytes 2097152 | tf_op jit(solution)/shard_map/all_to_all | solution.py:284
  36.1 0.0 copy-done.3
  36.1 0.2 reduce-window.8
  36.3 0.1 convert_reduce_fusion
  36.4 0.1 copy.9.docc_ref
  36.5 27.4 %all-gather.2 = f16[512,8,256]{2,1,0:T(8,128)(2,1)S(1)} all-gather(f16[64,8,256]{2,1,0:T(8,128)(2,1)S(1)} %all-to-all-done), channel_id=2, replica_groups=mesh['section'=32,'aux'=2,'dp'=8] {'dp'}, dimensions={0}, use_global_device_ids=true | all-gather | bytes 2359296 | tf_op jit(solution)/shard_map/all_gather | solution.py:287
  63.9 0.6 multiply_convert_fusion
  64.5 0.4 all-to-all-done.1
  64.8 0.0 copy-start.1
  64.8 0.0 copy-start.2
  64.8 0.7 project.1
  65.6 0.5 copy-done.1
  66.0 0.3 copy-done.2
  66.4 5.2 %attend.1 = (bf16[3,32,16,256]{3,2,1,0:T(8,128)(2,1)S(1)}, bf16[2,32,16,256]{3,2,1,0:T(8,128)(2,1)S(1)}, bf16[2,32,16,256]{3,2,1,0:T(8,128)(2,1)S(1)}, bf16[1,32...) custom-call(s32[1]{0:T(128)} %bitcast.me_ref, bf16[256,512]{1,0:T(8,128)(2,1)S(1)} %get-tuple-element.20.cache_ref, ...), custom_call_target="tpu_custom_call" | custom-call | flops 2415919104 | bytes 6291456 | tf_op jit(solution)/shard_map/attend/pallas_call | solution.py:197
  71.5 3.2 %collective-permute-start = (bf16[2,32,16,256]{3,2,1,0:T(8,128)(2,1)S(1)}, bf16[2,32,16,256]{3,2,1,0:T(8,128)(2,1)S(1)}, u32[]{:S(2)}, u32[]{:S(2)}) collective-permute-start(bf16[2,32,16,256]{3,2,1,0:T(8,128)(2,1)S(1)} %get-tuple-element.25), channel_id=1, source_target_pairs={{0,1},{1,2},{2,3},{3,4},{4,5},{5,6},{6,7},{7,0},{8,9},{9,10},{10,1... | collective-permute-start | bytes 1572872 | tf_op jit(solution)/shard_map/ppermute | solution.py:253
  74.8 3.8 %collective-permute-start.1 = (bf16[2,32,16,256]{3,2,1,0:T(8,128)(2,1)S(1)}, bf16[2,32,16,256]{3,2,1,0:T(8,128)(2,1)S(1)}, u32[]{:S(2)}, u32[]{:S(2)}) collective-permute-start(bf16[2,32,16,256]{3,2,1,0:T(8,128)(2,1)S(1)} %get-tuple-element.26), channel_id=1, source_target_pairs={{0,7},{1,0},{2,1},{3,2},{4,3},{5,4},{6,5},{7,6},{8,15},{9,8},{10,9... | collective-permute-start | bytes 1572872 | tf_op jit(solution)/shard_map/ppermute | solution.py:253
  78.6 6.9 %collective-permute-start.2 = (bf16[1,32,16,256]{3,2,1,0:T(8,128)(2,1)S(1)}, bf16[1,32,16,256]{3,2,1,0:T(8,128)(2,1)S(1)}, u32[]{:S(2)}, u32[]{:S(2)}) collective-permute-start(bf16[1,32,16,256]{3,2,1,0:T(8,128)(2,1)S(1)} %get-tuple-element.27), channel_id=1, source_target_pairs={{0,4},{1,5},{2,6},{3,7},{4,0},{5,1},{6,2},{7,3},{8,12},{9,13},{10,... | collective-permute-start | bytes 786440 | tf_op jit(solution)/shard_map/ppermute | solution.py:253
  85.5 13.6 %all-to-all-start.2 = ((bf16[64,8,1024]{2,1,0:T(8,128)(2,1)}), bf16[64,8,1024]{2,1,0:T(8,128)(2,1)}, u32[]{:S(2)}, u32[]{:S(2)}) async-start(bf16[64,8,1024]{2,1,0:T(8,128)(2,1)} %bitcast.14), calls=%async_computation.2 | async-start | bytes 2097152 | tf_op jit(solution)/shard_map/all_to_all | solution.py:302
  99.1 0.0 collective-permute-done.2.refs_3_
  99.1 0.0 collective-permute-done.refs_1_
  99.2 0.0 collective-permute-done.1.refs_2_.refs_1_
  99.2 0.1 add_term.6
  99.2 0.1 add_term.5
  99.3 1.9 %collective-permute-start.3 = (bf16[1,32,16,256]{3,2,1,0:T(8,128)(2,1)S(1)}, bf16[1,32,16,256]{3,2,1,0:T(8,128)(2,1)S(1)}, u32[]{:S(2)}, u32[]{:S(2)}) collective-permute-start(bf16[1,32,16,256]{3,2,1,0:T(8,128)(2,1)S(1)} %add_term.5), channel_id=1, source_target_pairs={{0,2},{1,3},{2,4},{3,5},{4,6},{5,7},{6,0},{7,1},{8,10},{9,11},{10,... | collective-permute-start | bytes 786440 | tf_op jit(solution)/shard_map/ppermute | solution.py:253
  101.2 5.5 %collective-permute-start.4 = (bf16[1,32,16,256]{3,2,1,0:T(8,128)(2,1)S(1)}, bf16[1,32,16,256]{3,2,1,0:T(8,128)(2,1)S(1)}, u32[]{:S(2)}, u32[]{:S(2)}) collective-permute-start(bf16[1,32,16,256]{3,2,1,0:T(8,128)(2,1)S(1)} %add_term.6), channel_id=1, source_target_pairs={{0,6},{1,7},{2,0},{3,1},{4,2},{5,3},{6,4},{7,5},{8,14},{9,15},{10,... | collective-permute-start | bytes 786440 | tf_op jit(solution)/shard_map/ppermute | solution.py:253
  106.7 0.1 add_term.4.refs_0_
  106.8 6.4 %collective-permute-done.3.refs_1_ = bf16[1,32,16,256]{3,2,1,0:T(8,128)(2,1)S(1)} collective-permute-done((bf16[1,32,16,256]{3,2,1,0:T(8,128)(2,1)S(1)}, bf16[1,32,16,256]{3,2,1,0:T(8,128)(2,1)S(1)}, u32[]{:S(2)}, u32[]{:S(2)}) %collective-permute-start.3) | collective-permute-done | bytes 262176 | tf_op jit(solution)/shard_map/ppermute | solution.py:253
  113.2 0.7 collective-permute-done.4.refs_2_
  113.9 0.8 add_term.7
  114.7 13.0 %all-to-all-done.2 = bf16[64,8,1024]{2,1,0:T(8,128)(2,1)} async-done(((bf16[64,8,1024]{2,1,0:T(8,128)(2,1)}), bf16[64,8,1024]{2,1,0:T(8,128)(2,1)}, u32[]{:S(2)}, u32[]{:S(2)}) %all-to-all-start.2) | async-done | bytes 1048608 | tf_op jit(solution)/shard_map/all_to_all | solution.py:302
  127.7 6.1 %all-to-all-start.3 = ((bf16[64,8,256]{2,1,0:T(8,128)(2,1)}), bf16[64,8,256]{2,1,0:T(8,128)(2,1)S(1)}, u32[]{:S(2)}, u32[]{:S(2)}) async-start(bf16[64,8,256]{2,1,0:T(8,128)(2,1)} %bitcast.17), calls=%async_computation.3 | async-start | bytes 524288 | tf_op jit(solution)/shard_map/all_to_all | solution.py:305
  133.8 2.4 %bitcast_reduce_fusion = bf16[32,8,1024]{2,1,0:T(8,128)(2,1)} fusion(bf16[64,8,1024]{2,1,0:T(8,128)(2,1)} %all-to-all-done.2), kind=kLoop, calls=%fused_computation.1 | loop fusion | flops 262144 | bytes 1572864 | tf_op jit(solution)/shard_map/reduce_sum | solution.py:309
  136.2 11.1 %all-to-all-done.3 = bf16[64,8,256]{2,1,0:T(8,128)(2,1)S(1)} async-done(((bf16[64,8,256]{2,1,0:T(8,128)(2,1)}), bf16[64,8,256]{2,1,0:T(8,128)(2,1)S(1)}, u32[]{:S(2)}, u32[]{:S(2)}) %all-to-all-start.3) | async-done | bytes 262176 | tf_op jit(solution)/shard_map/all_to_all | solution.py:305
  147.3 0.9 convert.4
Async XLA Ops:
  2.3 33.8 %copy-start.3 = (s32[1,4]{1,0:T(1,128)S(1)}, s32[1,4]{1,0:T(1,128)}, u32[]{:S(2)}) copy-start(s32[1,4]{1,0:T(1,128)} %param.9) | copy-start | bytes 52
  2.3 28.4 %all-to-all-start = ((f16[64,8,256]{2,1,0:T(8,128)(2,1)}), f16[64,8,256]{2,1,0:T(8,128)(2,1)S(1)}, u32[]{:S(2)}, u32[]{:S(2)}) async-start(f16[64,8,256]{2,1,0:T(8,128)(2,1)} %bitcast.3), calls=%async_computation | async-start | bytes 524288 | tf_op jit(solution)/shard_map/all_to_all | solution.py:278
  17.3 1.0 copy-start
  30.7 34.1 %all-to-all-start.1 = ((bf16[64,8,1024]{2,1,0:T(8,128)(2,1)}), bf16[64,8,1024]{2,1,0:T(8,128)(2,1)S(1)}, u32[]{:S(2)}, u32[]{:S(2)}) async-start(bf16[64,8,1024]{2,1,0:T(8,128)(2,1)} %bitcast.5), calls=%async_computation.1 | async-start | bytes 2097152 | tf_op jit(solution)/shard_map/all_to_all | solution.py:284
  64.8 1.2 copy-start.1
  64.8 1.5 %copy-start.2 = (bf16[1,256,2048]{2,1,0:T(8,128)(2,1)S(1)}, bf16[1,256,2048]{2,1,0:T(8,128)(2,1)}, u32[]{:S(2)}) copy-start(bf16[1,256,2048]{2,1,0:T(8,128)(2,1)} %param.8) | copy-start | bytes 3145732
  71.5 27.6 %collective-permute-start = (bf16[2,32,16,256]{3,2,1,0:T(8,128)(2,1)S(1)}, bf16[2,32,16,256]{3,2,1,0:T(8,128)(2,1)S(1)}, u32[]{:S(2)}, u32[]{:S(2)}) collective-permute-start(bf16[2,32,16,256]{3,2,1,0:T(8,128)(2,1)S(1)} %get-tuple-element.25), channel_id=1, source_target_pairs={{0,1},{1,2},{2,3},{3,4},{4,5},{5,6},{6,7},{7,0},{8,9},{9,10},{10,1... | collective-permute-start | bytes 1572872 | tf_op jit(solution)/shard_map/ppermute | solution.py:253
  74.8 24.4 %collective-permute-start.1 = (bf16[2,32,16,256]{3,2,1,0:T(8,128)(2,1)S(1)}, bf16[2,32,16,256]{3,2,1,0:T(8,128)(2,1)S(1)}, u32[]{:S(2)}, u32[]{:S(2)}) collective-permute-start(bf16[2,32,16,256]{3,2,1,0:T(8,128)(2,1)S(1)} %get-tuple-element.26), channel_id=1, source_target_pairs={{0,7},{1,0},{2,1},{3,2},{4,3},{5,4},{6,5},{7,6},{8,15},{9,8},{10,9... | collective-permute-start | bytes 1572872 | tf_op jit(solution)/shard_map/ppermute | solution.py:253
  78.6 20.6 %collective-permute-start.2 = (bf16[1,32,16,256]{3,2,1,0:T(8,128)(2,1)S(1)}, bf16[1,32,16,256]{3,2,1,0:T(8,128)(2,1)S(1)}, u32[]{:S(2)}, u32[]{:S(2)}) collective-permute-start(bf16[1,32,16,256]{3,2,1,0:T(8,128)(2,1)S(1)} %get-tuple-element.27), channel_id=1, source_target_pairs={{0,4},{1,5},{2,6},{3,7},{4,0},{5,1},{6,2},{7,3},{8,12},{9,13},{10,... | collective-permute-start | bytes 786440 | tf_op jit(solution)/shard_map/ppermute | solution.py:253
  85.5 42.2 %all-to-all-start.2 = ((bf16[64,8,1024]{2,1,0:T(8,128)(2,1)}), bf16[64,8,1024]{2,1,0:T(8,128)(2,1)}, u32[]{:S(2)}, u32[]{:S(2)}) async-start(bf16[64,8,1024]{2,1,0:T(8,128)(2,1)} %bitcast.14), calls=%async_computation.2 | async-start | bytes 2097152 | tf_op jit(solution)/shard_map/all_to_all | solution.py:302
  99.3 13.9 %collective-permute-start.3 = (bf16[1,32,16,256]{3,2,1,0:T(8,128)(2,1)S(1)}, bf16[1,32,16,256]{3,2,1,0:T(8,128)(2,1)S(1)}, u32[]{:S(2)}, u32[]{:S(2)}) collective-permute-start(bf16[1,32,16,256]{3,2,1,0:T(8,128)(2,1)S(1)} %add_term.5), channel_id=1, source_target_pairs={{0,2},{1,3},{2,4},{3,5},{4,6},{5,7},{6,0},{7,1},{8,10},{9,11},{10,... | collective-permute-start | bytes 786440 | tf_op jit(solution)/shard_map/ppermute | solution.py:253
  101.2 12.7 %collective-permute-start.4 = (bf16[1,32,16,256]{3,2,1,0:T(8,128)(2,1)S(1)}, bf16[1,32,16,256]{3,2,1,0:T(8,128)(2,1)S(1)}, u32[]{:S(2)}, u32[]{:S(2)}) collective-permute-start(bf16[1,32,16,256]{3,2,1,0:T(8,128)(2,1)S(1)} %add_term.6), channel_id=1, source_target_pairs={{0,6},{1,7},{2,0},{3,1},{4,2},{5,3},{6,4},{7,5},{8,14},{9,15},{10,... | collective-permute-start | bytes 786440 | tf_op jit(solution)/shard_map/ppermute | solution.py:253
  127.7 19.7 %all-to-all-start.3 = ((bf16[64,8,256]{2,1,0:T(8,128)(2,1)}), bf16[64,8,256]{2,1,0:T(8,128)(2,1)S(1)}, u32[]{:S(2)}, u32[]{:S(2)}) async-start(bf16[64,8,256]{2,1,0:T(8,128)(2,1)} %bitcast.17), calls=%async_computation.3 | async-start | bytes 524288 | tf_op jit(solution)/shard_map/all_to_all | solution.py:305
